TPU v7x, 32 devices: a whole 2x2x4 slice. The times are simulated.
32 devices in a mesh: wide: 8 (over z, core), narrow: 4 (over y, x).
Axes of the slice: x: 2, y: 2, z: 4, core: 2. Of those that a mesh axis runs over, the one named last changes fastest.
Arguments:
- activations: bfloat16 [6144, 4096], P('wide'), may hold values from -12 to 12
- gain: bfloat16 [4096], replicated, may hold values from 0.099609375 to 1.8984375
- w_query: bfloat16 [4096, 4096], P('wide', 'narrow'), may hold values from -0.5 to 0.5
- w_key: bfloat16 [4096, 1024], P('wide', 'narrow'), may hold values from -14 to 14
- w_value: bfloat16 [4096, 1024], P('wide', 'narrow'), may hold values from -0.09375 to 0.09375
- w_out: bfloat16 [4096, 4096], P('wide', 'narrow'), may hold values from -0.09375 to 0.09375
- cotangent: bfloat16 [6144, 4096], P('wide'), may hold values from -6 to 6
Outputs:
- outputs: bfloat16 [6144, 4096], P('wide', 'narrow')
- grad_query: float32 [4096, 4096], P('wide', 'narrow')
- grad_key: float32 [4096, 1024], P('wide', 'narrow')
- grad_value: float32 [4096, 1024], P('wide', 'narrow')
- grad_out: float32 [4096, 4096], P('wide', 'narrow')
All inputs are finite; a program needn't handle non-finite values.
Results may differ from a plain program's by a relative error of at most 0.017.
The roundings to bfloat16 on the way count: a program that leaves them out, or rounds other values in their place, can miss the bound.
Values may be sent and summed in bfloat16 or wider, within the bound.
No kernel may reach another device: no remote copies, remote signals or barrier semaphores. Data moves between devices by JAX's collectives and lax.ppermute only.
A program may use at most 192 MiB of HBM per device.

v0:
```python
import functools
import jax
import jax.numpy as jnp
from jax import lax
from jax.experimental import pallas as pl
from jax.experimental.pallas import tpu as pltpu
from jax.sharding import PartitionSpec as P

HEAD_DIM = 128
BLOCK = 256
EPSILON = 1e-05
MASKED = -1e30
F32 = jnp.float32
BF16 = jnp.bfloat16
SHORT = pl.CostEstimate(flops=1, bytes_accessed=1, transcendentals=0)


def normalize(rows, gain):
    values32 = rows.astype(F32)
    mean_square = jnp.mean(values32 * values32, axis=-1, keepdims=True)
    return (values32 * lax.rsqrt(mean_square + EPSILON) * gain.astype(F32)).astype(BF16)


def nt(a, b):
    return lax.dot_general(a, b, (((1,), (1,)), ((), ())), preferred_element_type=F32)


def nn(a, b):
    return lax.dot_general(a, b, (((1,), (0,)), ((), ())), preferred_element_type=F32)


def masked_scores(keys, queries, start, size):
    scores = nt(keys, queries) * HEAD_DIM ** (-0.5)
    key_at = lax.broadcasted_iota(jnp.int32, (size, size), 0)
    query_at = lax.broadcasted_iota(jnp.int32, (size, size), 1)
    last = jnp.where(key_at <= query_at, scores[start:], MASKED)
    if start == 0:
        return last
    return jnp.concatenate([scores[:start], last], axis=0)


def forward_kernel(members, block, qkv_ref, mixed_ref, lse_ref):
    length = qkv_ref.shape[0]
    width = HEAD_DIM
    key_col, value_col = members * width, (members + 1) * width
    values_t = qkv_ref[:, value_col : value_col + width].T
    for h in range(members):
        for start in range(0, length, block):
            stop = start + block
            queries = qkv_ref[start:stop, h * width : (h + 1) * width]
            keys = qkv_ref[:stop, key_col : key_col + width]
            scores = masked_scores(keys, queries, start, block)
            highest = jnp.max(scores, axis=0, keepdims=True)
            exponent = jnp.exp(scores - highest)
            total = jnp.sum(exponent, axis=0, keepdims=True)
            rounded = (exponent * (1.0 / total)).astype(BF16)
            mixed_t = nn(values_t[:, :stop], rounded)
            mixed_ref[start:stop, h * width : (h + 1) * width] = mixed_t.T.astype(BF16)
            lse_ref[h : h + 1, start:stop] = highest + jnp.log(total)


def attend_forward(qkv, members, block):
    length = qkv.shape[0]
    width = HEAD_DIM
    vmem = pl.BlockSpec(memory_space=pltpu.VMEM)
    return pl.pallas_call(
        functools.partial(forward_kernel, members, block),
        out_shape=(
            jax.ShapeDtypeStruct((length, members * width), BF16),
            jax.ShapeDtypeStruct((members, length), F32),
        ),
        in_specs=[vmem],
        out_specs=(vmem, vmem),
        compiler_params=pltpu.CompilerParams(vmem_limit_bytes=40 * 2**20),
        cost_estimate=SHORT,
        name="attend_forward",
    )(qkv)


def backward_kernel(members, block, qkv_ref, grad_ref, lse_ref, out_ref, gk_ref, gv_ref):
    length = qkv_ref.shape[0]
    width = HEAD_DIM
    key_col, value_col = members * width, (members + 1) * width
    keys_t = qkv_ref[:, key_col : key_col + width].T
    gk_ref[...] = jnp.zeros_like(gk_ref)
    gv_ref[...] = jnp.zeros_like(gv_ref)
    for h in range(members):
        cols = slice(h * width, (h + 1) * width)
        for start in range(0, length, block):
            stop = start + block
            queries = qkv_ref[start:stop, cols]
            grads = grad_ref[start:stop, cols]
            keys = qkv_ref[:stop, key_col : key_col + width]
            values = qkv_ref[:stop, value_col : value_col + width]
            scores = masked_scores(keys, queries, start, block)
            probs = jnp.exp(scores - lse_ref[h : h + 1, start:stop])
            grad_probs = nt(values, grads)
            gv_ref[:stop, :] += nn(probs.astype(BF16), grads)
            inner = jnp.sum(grad_probs * probs, axis=0, keepdims=True)
            grad_scores = (probs * (grad_probs - inner) * width ** (-0.5)).astype(BF16)
            gk_ref[:stop, :] += nn(grad_scores, queries)
            out_ref[start:stop, cols] = nn(keys_t[:, :stop], grad_scores).T.astype(BF16)
    out_ref[:, key_col : key_col + width] = gk_ref[...].astype(BF16)
    out_ref[:, value_col : value_col + width] = gv_ref[...].astype(BF16)


def attend_backward(qkv, grad_mixed, lse, members, block):
    length = qkv.shape[0]
    width = HEAD_DIM
    vmem = pl.BlockSpec(memory_space=pltpu.VMEM)
    return pl.pallas_call(
        functools.partial(backward_kernel, members, block),
        out_shape=jax.ShapeDtypeStruct(qkv.shape, BF16),
        in_specs=[vmem, vmem, vmem],
        out_specs=vmem,
        scratch_shapes=[pltpu.VMEM((length, width), F32), pltpu.VMEM((length, width), F32)],
        compiler_params=pltpu.CompilerParams(vmem_limit_bytes=40 * 2**20),
        cost_estimate=SHORT,
        name="attend_backward",
    )(qkv, grad_mixed, lse)


def take(blocks, at):
    return lax.dynamic_index_in_dim(blocks, at, 0, keepdims=False)


def split_kernel(chips, core_ref, x_ref, gain_ref, grad_ref, out, xt_own, gt_own, xt_other, gt_other):
    features = x_ref.shape[1]
    rows = features // (2 * chips)
    core = core_ref[0]
    total = None
    for w in range(2 * chips):
        values = x_ref[:, w * rows : (w + 1) * rows].astype(F32)
        part = jnp.sum(values * values, axis=-1, keepdims=True)
        total = part if total is None else total + part
    scale = lax.rsqrt(total / features + EPSILON)
    for side, xt_out, gt_out in ((core, xt_own, gt_own), (1 - core, xt_other, gt_other)):
        for chip in range(chips):
            cols = pl.ds(pl.multiple_of((2 * chip + side) * rows, 128), rows)
            to = slice(chip * rows, (chip + 1) * rows)
            normed = (x_ref[:, cols].astype(F32) * scale * gain_ref[:, cols]).astype(BF16)
            out[:, cols] = normed
            xt_out[to, :] = normed.T
            gt_out[to, :] = grad_ref[:, cols].T


def norm_and_split(core, activations, gain, cotangent, chips):
    length, features = activations.shape
    step = 128 if length % 128 == 0 else length
    whole = pl.BlockSpec((step, features), lambda i: (i, 0))
    turned = pl.BlockSpec((features // 2, step), lambda i: (0, i))
    shape_t = jax.ShapeDtypeStruct((features // 2, length), BF16)
    return pl.pallas_call(
        functools.partial(split_kernel, chips),
        grid=(length // step,),
        out_shape=(jax.ShapeDtypeStruct((length, features), BF16),) + (shape_t,) * 4,
        in_specs=[
            pl.BlockSpec(memory_space=pltpu.SMEM),
            whole,
            pl.BlockSpec((1, features), lambda i: (0, 0)),
            whole,
        ],
        out_specs=(whole,) + (turned,) * 4,
        compiler_params=pltpu.CompilerParams(vmem_limit_bytes=32 * 2**20),
        cost_estimate=SHORT,
        name="norm_and_split",
    )(core.reshape(1), activations, gain.astype(F32).reshape(1, -1), cotangent)


def product_kernel(a, b, out, total):
    part = nn(a[...], b[...])
    at = pl.program_id(0)

    @pl.when(at == 0)
    def _():
        total[...] = part

    @pl.when(at > 0)
    def _():
        total[...] += part

    @pl.when(at == pl.num_programs(0) - 1)
    def _():
        out[...] = total[...].astype(BF16)


def product(rows, weights):
    length, depth = rows.shape
    cols = weights.shape[1]
    step = 1024 if depth % 1024 == 0 else depth
    return pl.pallas_call(
        product_kernel,
        grid=(depth // step,),
        out_shape=jax.ShapeDtypeStruct((length, cols), BF16),
        in_specs=[
            pl.BlockSpec((length, step), lambda i: (0, i)),
            pl.BlockSpec((step, cols), lambda i: (i, 0)),
        ],
        out_specs=pl.BlockSpec((length, cols), lambda i: (0, 0)),
        scratch_shapes=[pltpu.VMEM((length, cols), F32)],
        compiler_params=pltpu.CompilerParams(vmem_limit_bytes=32 * 2**20),
        cost_estimate=SHORT,
        name="product",
    )(rows, weights)


def term_kernel(a, b, out):
    out[...] = nn(a[...], b[...]).astype(BF16)


def term(a, b):
    features, length = a.shape
    cols = b.shape[1]
    step = 512 if features % 512 == 0 else features
    return pl.pallas_call(
        term_kernel,
        grid=(features // step,),
        out_shape=jax.ShapeDtypeStruct((features, cols), BF16),
        in_specs=[
            pl.BlockSpec((step, length), lambda i: (i, 0)),
            pl.BlockSpec((length, cols), lambda i: (0, 0)),
        ],
        out_specs=pl.BlockSpec((step, cols), lambda i: (i, 0)),
        compiler_params=pltpu.CompilerParams(vmem_limit_bytes=32 * 2**20),
        cost_estimate=SHORT,
        name="term",
    )(a, b)


def project_kernel(count, *refs):
    out = refs[-1]
    total = None
    for mixed, side in zip(refs[:count], refs[count : 2 * count]):
        part = nt(mixed[...], side[...])
        total = part if total is None else total + part
    out[...] = total.astype(BF16)


def project(mixed, sides):
    length, span = mixed[0].shape
    features = sides[0].shape[0]
    step = 512 if features % 512 == 0 else features
    count = len(mixed)
    return pl.pallas_call(
        functools.partial(project_kernel, count),
        grid=(features // step,),
        out_shape=jax.ShapeDtypeStruct((length, features), BF16),
        in_specs=[pl.BlockSpec((length, span), lambda i: (0, 0))] * count
        + [pl.BlockSpec((step, span), lambda i: (i, 0))] * count,
        out_specs=pl.BlockSpec((length, step), lambda i: (0, i)),
        compiler_params=pltpu.CompilerParams(vmem_limit_bytes=32 * 2**20),
        cost_estimate=SHORT,
        name="project",
    )(*mixed, *sides)


class Order:
    def __init__(self):
        self.last = None

    def __call__(self, compute, *operands):
        result = compute(*self.after(*operands))
        leaves, form = jax.tree.flatten(result)
        if len(leaves) > 1:
            leaves = lax.optimization_barrier(tuple(leaves))
        self.last = leaves[0]
        return jax.tree.unflatten(form, leaves)

    def after(self, *operands):
        if self.last is None:
            return operands
        least = min(range(len(operands)), key=lambda i: operands[i].size)
        tied = lax.optimization_barrier((self.last, operands[least]))[1]
        return operands[:least] + (tied,) + operands[least + 1 :]


def swap_cores(array, chips):
    return lax.ppermute(array, "wide", [(w, w ^ 1) for w in range(2 * chips)])


class LineSum:
    def __init__(self, order, chips):
        self.order, self.chips = order, chips
        self.chip = lax.axis_index("wide") // 2
        self.arrived = ()
        self.hops = 0

    def blocks(self, array):
        return array.reshape(self.chips, -1, array.shape[-1])

    def swap(self, send):
        self.received = self.blocks(swap_cores(send, self.chips))

    def hold(self, keep):
        self.keep = self.blocks(keep)

    def advance(self):
        self.hops += 1
        t, chips, chip = self.hops, self.chips, self.chip
        far = chips - t

        def messages(keep, received, *arrived):
            sums = []
            for i, at in enumerate((jnp.minimum(chip + far, chips - 1), jnp.maximum(chip - far, 0))):
                total = take(keep, at).astype(F32) + take(received, at).astype(F32)
                if arrived:
                    total = total + arrived[i].astype(F32)
                sums.append(total.astype(BF16))
            return tuple(sums)

        up, down = self.order(messages, self.keep, self.received, *self.arrived)
        self.arrived = (
            lax.ppermute(up, "wide", [(w, w + 2) for w in range(2 * t)]),
            lax.ppermute(down, "wide", [(w, w - 2) for w in range(2 * far, 2 * chips)]),
        )

    def total(self):
        def add(keep, received, *arrived):
            result = take(keep, self.chip).astype(F32) + take(received, self.chip).astype(F32)
            for part in arrived:
                result = result + part.astype(F32)
            return result

        return self.order(add, self.keep, self.received, *self.arrived)


def plan(groups, chips):
    steps = [("N", 0)]
    under_way = []

    def hops(count):
        for _ in range(count):
            if under_way:
                k = under_way[0]
                steps.append(("M", k))
                left[k] -= 1
                if not left[k]:
                    steps.append(("T", k))
                    under_way.pop(0)

    left = {k: chips - 1 for k in range(2 * groups)}
    for k in range(2 * groups):
        g = k // 2
        steps.append(("P", k))
        if k == 2 * groups - 1:
            steps.append(("J", 0))
        hops(1)
        steps.append(("F", g) if k % 2 == 0 else ("B", g))
        hops(1)
        steps += [("S", k), ("W", k)]
        under_way.append(k)
        hops(1)
        if k < 2 * groups - 1:
            hops(1)
    hops(chips * 2)
    steps.insert(-1, ("O", 0))
    return steps


def shards(wide, activations, gain, w_query, w_key, w_value, w_out, cotangent):
    width = HEAD_DIM
    length, features = activations.shape
    chips = wide // 2
    groups = w_key.shape[1] // width
    members = w_query.shape[1] // w_key.shape[1]
    block = BLOCK if length % BLOCK == 0 else length
    span = members * width
    rows = features // wide
    core = lax.axis_index("wide") % 2
    order = Order()

    def columns(g):
        cols = slice(g * span, (g + 1) * span)
        heads = slice(g * width, (g + 1) * width)
        return jnp.concatenate([w_query[:, cols], w_key[:, heads], w_value[:, heads]], axis=1)

    pieces = []
    for g in range(groups):
        pieces += [columns(g), w_out[:, g * span : (g + 1) * span]]
    weights = []
    for piece in pieces:
        if weights:
            piece = lax.optimization_barrier((pieces[len(weights) - 1], piece))[1]
        pieces[len(weights)] = piece
        weights.append(lax.all_gather(piece, "wide", axis=0, tiled=True))
    sums = [LineSum(order, chips) for _ in weights]
    made = {}

    def finish_outputs(activations, summed):
        share = summed.shape[1]
        own_columns = lax.dynamic_slice_in_dim(
            activations, lax.axis_index("narrow") * share, share, 1
        )
        return (own_columns.astype(F32) + summed.astype(F32)).astype(BF16)

    def step(name, i):
        g = i // 2
        if name == "N":
            parts = order(
                lambda a, b, c: norm_and_split(core, a, b, c, chips), activations, gain, cotangent
            )
            made["x"], made["xt"], made["gradt"] = parts[0], parts[1::2], parts[2::2]
        elif name == "P":
            left = cotangent if i % 2 else made["x"]
            made["p", i] = order(product, left, weights[i])
        elif name == "F":
            made["mixed", i], made["lse", i] = order(
                lambda a: attend_forward(a, members, block), made["p", 2 * i]
            )
        elif name == "B":
            made["back", i] = order(
                lambda a, b, c: attend_backward(a, b, c, members, block),
                made["p", 2 * i],
                made["p", 2 * i + 1],
                made["lse", i],
            )
        elif name in "SW":
            left = made["xt" if i % 2 else "gradt"][name == "S"]
            result = order(term, left, made["back" if i % 2 else "mixed", g])
            if name == "S":
                sums[i].swap(result)
            else:
                sums[i].hold(result)
        elif name == "M":
            sums[i].advance()
        elif name == "T":
            made["sum", i] = sums[i].total()
        elif name == "J":
            mixed = [made["mixed", g] for g in range(groups)]
            part = order(
                lambda *a: project(a[:groups], a[groups:]), *mixed, *weights[1::2]
            )
            made["summed"] = lax.psum_scatter(
                part, "narrow", scatter_dimension=1, tiled=True
            )
        elif name == "O":
            made["out"] = order(finish_outputs, activations, made["summed"])

    for name, i in plan(groups, chips):
        step(name, i)
    outputs = made["out"]
    out_sum = [made["sum", 2 * g] for g in range(groups)]
    qkv_sum = [made["sum", 2 * g + 1] for g in range(groups)]

    def joined(pieces):
        return pieces[0] if len(pieces) == 1 else jnp.concatenate(pieces, axis=1)

    grad_query = joined([s[:, :span] for s in qkv_sum])
    grad_key = joined([s[:, span : span + width] for s in qkv_sum])
    grad_value = joined([s[:, span + width :] for s in qkv_sum])
    grad_out = joined(out_sum)
    return (outputs, grad_query, grad_key, grad_value, grad_out)


def solution(mesh):
    return jax.shard_map(
        functools.partial(shards, mesh.shape["wide"]),
        mesh=mesh,
        in_specs=(
            P("wide", None),
            P(),
            P("wide", "narrow"),
            P("wide", "narrow"),
            P("wide", "narrow"),
            P("wide", "narrow"),
            P("wide", None),
        ),
        out_specs=(
            P("wide", "narrow"),
            P("wide", "narrow"),
            P("wide", "narrow"),
            P("wide", "narrow"),
            P("wide", "narrow"),
        ),
        check_vma=False,
    )
```

profile of v0, /device:TPU:0, one launch (start us, length us, event | category | flops | bytes accessed | tf_op | source)
XLA Modules:
  0.0 523.4 jit_solution(7794320537941993176)
XLA Ops:
  12.3 10.1 %norm_and_split.1 = (bf16[768,4096]{1,0:T(8,128)(2,1)S(1)}, bf16[2048,768]{1,0:T(8,128)(2,1)S(1)}, bf16[2048,768]{1,0:T(8,128)(2,1)S(1)}, bf16[2048,768]{1,0:T(8,128)(2,1)S(1)}, bf16[2048,768]{1,0:T(8,128)(2,1)S(1)}) custom-call(s32[1]{0:T(128)} %bitcast.core_ref, bf16[768,4096]{1,0:T(8,128)(2,1)} %x_ref.1, f32[1,4096]{1,0:T(1,128)S(1)} %bitcast.122, ...), custom_call_target="tpu_custom_call" | custom-call | flops 1 | bytes 1 | tf_op jit(solution)/shard_map/norm_and_split/pallas_call | solution.py:153
  22.4 2.6 copy-done.3
  29.9 47.8 %all-gather.5.cloned.1.call-done.b = bf16[4096,768]{1,0:T(8,128)(2,1)} async-done(((bf16[512,768]{1,0:T(8,128)(2,1)}), bf16[4096,768]{1,0:T(8,128)(2,1)}) %all-gather.5.cloned.1.call-update) | async-done | bytes 6291472 | tf_op jit(solution)/shard_map/all_gather | solution.py:385
  77.7 2.8 copy-done.4
  80.5 2.8 copy-done.30
  83.3 6.9 %product.4.qkv_ref = bf16[768,768]{1,0:T(8,128)(2,1)S(1)} custom-call(bf16[768,4096]{1,0:T(8,128)(2,1)S(1)} %copy-done.4, bf16[4096,768]{1,0:T(8,128)(2,1)S(1)} %copy-done.30), custom_call_target="tpu_custom_call" | custom-call | flops 1 | bytes 1 | tf_op jit(solution)/shard_map/product/pallas_call | solution.py:191
  90.3 5.2 attend_forward.2
  95.4 3.3 term.8
  102.1 2.3 term.9
  104.4 2.3 fusion.25
  109.5 22.2 %collective-permute-done.1 = bf16[512,512]{1,0:T(8,128)(2,1)S(1)} collective-permute-done((bf16[512,512]{1,0:T(8,128)(2,1)}, bf16[512,512]{1,0:T(8,128)(2,1)S(1)}, u32[]{:S(2)}, u32[]{:S(2)}) %collective-permute-start.1) | collective-permute-done | bytes 524320 | tf_op jit(solution)/shard_map/ppermute | solution.py:313
  131.7 2.6 fusion.18
  134.3 5.1 collective-permute-start.3
  140.8 2.8 copy-done
  143.6 2.5 copy-done.6
  146.2 5.0 product.5.grad_ref
  151.1 4.1 collective-permute-done.3
  155.2 2.7 fusion.15
  158.0 20.5 %collective-permute-start.5 = (bf16[512,512]{1,0:T(8,128)(2,1)}, bf16[512,512]{1,0:T(8,128)(2,1)}, u32[]{:S(2)}, u32[]{:S(2)}) collective-permute-start(bf16[512,512]{1,0:T(8,128)(2,1)} %get-tuple-element.94), channel_id=1, source_target_pairs={{0,8},{4,12},{8,16},{12,20},{16,24},{20,28},{1,9},{5,13},{9,17},{1... | collective-permute-start | bytes 1572872 | tf_op jit(solution)/shard_map/ppermute | solution.py:313
  179.9 17.9 %collective-permute-done.5 = bf16[512,512]{1,0:T(8,128)(2,1)} collective-permute-done((bf16[512,512]{1,0:T(8,128)(2,1)}, bf16[512,512]{1,0:T(8,128)(2,1)}, u32[]{:S(2)}, u32[]{:S(2)}) %collective-permute-start.5) | collective-permute-done | bytes 524320 | tf_op jit(solution)/shard_map/ppermute | solution.py:313
  197.8 7.8 %collective-permute-done.6 = bf16[512,512]{1,0:T(8,128)(2,1)} collective-permute-done((bf16[512,512]{1,0:T(8,128)(2,1)S(1)}, bf16[512,512]{1,0:T(8,128)(2,1)}, u32[]{:S(2)}, u32[]{:S(2)}) %collective-permute-start.6) | collective-permute-done | bytes 524320 | tf_op jit(solution)/shard_map/ppermute | solution.py:314
  205.7 2.6 fusion.17
  208.3 6.1 %attend_backward.2.b = bf16[768,768]{1,0:T(8,128)(2,1)S(1)} custom-call(bf16[768,768]{1,0:T(8,128)(2,1)S(1)} %copy-done.23, bf16[768,512]{1,0:T(8,128)(2,1)S(1)} %product.5.grad_ref, f32[4,768]{1,0:T(4,128)S(1)} %get-tuple-element.98.lse_ref), custom_call_target="tpu_custom_call" | custom-call | flops 1 | bytes 1 | tf_op jit(solution)/shard_map/attend_backward/pallas_call | solution.py:111
  214.4 4.2 term.10
  221.8 3.1 term.11
  226.7 12.5 %collective-permute-start.8 = (bf16[512,768]{1,0:T(8,128)(2,1)S(1)}, bf16[512,768]{1,0:T(8,128)(2,1)S(1)}, u32[]{:S(2)}, u32[]{:S(2)}) collective-permute-start(bf16[512,768]{1,0:T(8,128)(2,1)S(1)} %get-tuple-element.102), channel_id=1, source_target_pairs={{0,8},{4,12},{1,9},{5,13},{2,10},{6,14},{3,11},{7,15}} | collective-permute-start | bytes 2359304 | tf_op jit(solution)/shard_map/ppermute | solution.py:313
  240.0 33.8 %collective-permute-done.8 = bf16[512,768]{1,0:T(8,128)(2,1)S(1)} collective-permute-done((bf16[512,768]{1,0:T(8,128)(2,1)S(1)}, bf16[512,768]{1,0:T(8,128)(2,1)S(1)}, u32[]{:S(2)}, u32[]{:S(2)}) %collective-permute-start.8) | collective-permute-done | bytes 786464 | tf_op jit(solution)/shard_map/ppermute | solution.py:313
  273.8 3.1 fusion.8
  276.9 5.3 %collective-permute-start.10 = (bf16[512,768]{1,0:T(8,128)(2,1)}, bf16[512,768]{1,0:T(8,128)(2,1)}, u32[]{:S(2)}, u32[]{:S(2)}) collective-permute-start(bf16[512,768]{1,0:T(8,128)(2,1)} %get-tuple-element.105), channel_id=1, source_target_pairs={{0,8},{4,12},{8,16},{12,20},{1,9},{5,13},{9,17},{13,21},{2,10},{6,... | collective-permute-start | bytes 2359304 | tf_op jit(solution)/shard_map/ppermute | solution.py:313
  283.8 2.8 copy-done.5
  286.6 2.8 copy-done.29
  289.3 6.9 %product.6.qkv_ref = bf16[768,768]{1,0:T(8,128)(2,1)S(1)} custom-call(bf16[768,4096]{1,0:T(8,128)(2,1)S(1)} %copy-done.5, bf16[4096,768]{1,0:T(8,128)(2,1)S(1)} %copy-done.29), custom_call_target="tpu_custom_call" | custom-call | flops 1 | bytes 1 | tf_op jit(solution)/shard_map/product/pallas_call | solution.py:191
  296.3 6.5 %collective-permute-done.10 = bf16[512,768]{1,0:T(8,128)(2,1)} collective-permute-done((bf16[512,768]{1,0:T(8,128)(2,1)}, bf16[512,768]{1,0:T(8,128)(2,1)}, u32[]{:S(2)}, u32[]{:S(2)}) %collective-permute-start.10) | collective-permute-done | bytes 786464 | tf_op jit(solution)/shard_map/ppermute | solution.py:313
  302.8 2.4 fusion.5
  305.2 4.4 collective-permute-start.12
  311.2 15.1 %collective-permute-done.12 = bf16[512,768]{1,0:T(8,128)(2,1)S(1)} collective-permute-done((bf16[512,768]{1,0:T(8,128)(2,1)S(1)}, bf16[512,768]{1,0:T(8,128)(2,1)S(1)}, u32[]{:S(2)}, u32[]{:S(2)}) %collective-permute-start.12) | collective-permute-done | bytes 786464 | tf_op jit(solution)/shard_map/ppermute | solution.py:313
  326.3 5.0 collective-permute-done.13
  331.3 2.8 fusion.7
  334.1 5.2 attend_forward.3
  339.2 2.3 term.12
  341.7 2.3 term.13
  346.1 3.7 collective-permute-start.15
  350.5 10.7 %collective-permute-done.15 = bf16[512,512]{1,0:T(8,128)(2,1)S(1)} collective-permute-done((bf16[512,512]{1,0:T(8,128)(2,1)S(1)}, bf16[512,512]{1,0:T(8,128)(2,1)S(1)}, u32[]{:S(2)}, u32[]{:S(2)}) %collective-permute-start.15) | collective-permute-done | bytes 524320 | tf_op jit(solution)/shard_map/ppermute | solution.py:313
  362.5 2.8 copy-done.1
  367.4 5.0 product.7.grad_ref
  373.3 8.5 %project.1 = bf16[768,4096]{1,0:T(8,128)(2,1)S(1)} custom-call(bf16[768,512]{1,0:T(8,128)(2,1)S(1)} %copy-done.28, bf16[768,512]{1,0:T(8,128)(2,1)S(1)} %get-tuple-element.116.b.refs_1_, bf16[4096,512]{1,0:T(8,128)(2,1)S(1)} %copy-done.7, bf16[4096,512]{1,0:T(8,128)(2,1)S(1)} %copy-done.8), custom_call_target="tpu_custom_call" | custom-call | flops 1 | bytes 1 | tf_op jit(solution)/shard_map/project/pallas_call | solution.py:244
  381.9 2.6 copy-done.2
  385.5 4.4 collective-permute-start.17
  390.6 9.9 %collective-permute-done.17 = bf16[512,512]{1,0:T(8,128)(2,1)S(1)} collective-permute-done((bf16[512,512]{1,0:T(8,128)(2,1)S(1)}, bf16[512,512]{1,0:T(8,128)(2,1)S(1)}, u32[]{:S(2)}, u32[]{:S(2)}) %collective-permute-start.17) | collective-permute-done | bytes 524320 | tf_op jit(solution)/shard_map/ppermute | solution.py:313
  402.2 7.2 %collective-permute-start.19 = (bf16[512,512]{1,0:T(8,128)(2,1)S(1)}, bf16[512,512]{1,0:T(8,128)(2,1)S(1)}, u32[]{:S(2)}, u32[]{:S(2)}) collective-permute-start(bf16[512,512]{1,0:T(8,128)(2,1)S(1)} %get-tuple-element.127), channel_id=1, source_target_pairs={{0,8},{4,12},{8,16},{12,20},{16,24},{20,28},{1,9},{5,13},{9,17},{1... | collective-permute-start | bytes 1572872 | tf_op jit(solution)/shard_map/ppermute | solution.py:313
  411.0 7.9 %collective-permute-done.19 = bf16[512,512]{1,0:T(8,128)(2,1)S(1)} collective-permute-done((bf16[512,512]{1,0:T(8,128)(2,1)S(1)}, bf16[512,512]{1,0:T(8,128)(2,1)S(1)}, u32[]{:S(2)}, u32[]{:S(2)}) %collective-permute-start.19) | collective-permute-done | bytes 524320 | tf_op jit(solution)/shard_map/ppermute | solution.py:313
  418.9 4.1 collective-permute-done.20
  425.3 6.1 %attend_backward.3.b = bf16[768,768]{1,0:T(8,128)(2,1)S(1)} custom-call(bf16[768,768]{1,0:T(8,128)(2,1)S(1)} %copy-done.25, bf16[768,512]{1,0:T(8,128)(2,1)S(1)} %copy-done.32, f32[4,768]{1,0:T(4,128)S(1)} %get-tuple-element.131.lse_ref), custom_call_target="tpu_custom_call" | custom-call | flops 1 | bytes 1 | tf_op jit(solution)/shard_map/attend_backward/pallas_call | solution.py:111
  431.4 3.2 term.14
  434.6 3.2 term.15
  437.8 2.5 collective-permute-done.21
  443.6 16.3 %collective-permute-done.22 = bf16[512,768]{1,0:T(8,128)(2,1)S(1)} collective-permute-done((bf16[512,768]{1,0:T(8,128)(2,1)S(1)}, bf16[512,768]{1,0:T(8,128)(2,1)S(1)}, u32[]{:S(2)}, u32[]{:S(2)}) %collective-permute-start.22) | collective-permute-done | bytes 786464 | tf_op jit(solution)/shard_map/ppermute | solution.py:313
  460.5 4.4 collective-permute-start.24
  465.7 15.5 %collective-permute-done.24 = bf16[512,768]{1,0:T(8,128)(2,1)S(1)} collective-permute-done((bf16[512,768]{1,0:T(8,128)(2,1)S(1)}, bf16[512,768]{1,0:T(8,128)(2,1)S(1)}, u32[]{:S(2)}, u32[]{:S(2)}) %collective-permute-start.24) | collective-permute-done | bytes 786464 | tf_op jit(solution)/shard_map/ppermute | solution.py:313
  483.1 7.6 %collective-permute-start.26 = (bf16[512,768]{1,0:T(8,128)(2,1)}, bf16[512,768]{1,0:T(8,128)(2,1)}, u32[]{:S(2)}, u32[]{:S(2)}) collective-permute-start(bf16[512,768]{1,0:T(8,128)(2,1)} %get-tuple-element.141), channel_id=1, source_target_pairs={{0,8},{4,12},{8,16},{12,20},{16,24},{20,28},{1,9},{5,13},{9,17},{1... | collective-permute-start | bytes 2359304 | tf_op jit(solution)/shard_map/ppermute | solution.py:313
  494.1 2.7 pad_maximum_fusion.1
  496.9 3.7 add_convert_fusion
  500.6 4.6 collective-permute-done.26
  505.2 5.0 collective-permute-done.27
  (146 shorter events, 58.4 us)
Async XLA Ops:
  7.2 70.5 %all-gather.5.cloned.1.call-start = ((), (), s32[]{:S(2)}) async-start(), calls=%async_computation.1 | async-start | bytes 7077888 | tf_op jit(solution)/shard_map/all_gather | solution.py:385
  9.7 131.2 %all-gather.7.cloned.1.call-start = ((), (), s32[]{:S(2)}) async-start(), calls=%async_computation.2 | async-start | bytes 4718592 | tf_op jit(solution)/shard_map/all_gather | solution.py:385
  11.2 272.6 %all-gather.9.cloned.1.call-start = ((), (), s32[]{:S(2)}) async-start(), calls=%async_computation.3 | async-start | bytes 7077888 | tf_op jit(solution)/shard_map/all_gather | solution.py:385
  12.2 350.3 %all-gather.11.cloned.1.call-start = ((), (), s32[]{:S(2)}) async-start(), calls=%async_computation.4 | async-start | bytes 4718592 | tf_op jit(solution)/shard_map/all_gather | solution.py:385
  22.4 2.7 copy-start.3
  29.9 65.5 %copy-start.18 = (bf16[2048,768]{1,0:T(8,128)(2,1)}, bf16[2048,768]{1,0:T(8,128)(2,1)S(1)}, u32[]{:S(2)}) copy-start(bf16[2048,768]{1,0:T(8,128)(2,1)S(1)} %get-tuple-element.80.a) | copy-start | bytes 9437188
  77.7 2.8 copy-start.4
  80.5 2.8 copy-start.30
  90.2 8.5 %copy-start.22 = (bf16[768,768]{1,0:T(8,128)(2,1)}, bf16[768,768]{1,0:T(8,128)(2,1)S(1)}, u32[]{:S(2)}) copy-start(bf16[768,768]{1,0:T(8,128)(2,1)S(1)} %product.4.qkv_ref) | copy-start | bytes 3538948
  95.4 3.4 copy-start.26
  98.8 5.6 %collective-permute-start = (bf16[2048,512]{1,0:T(8,128)(2,1)}, bf16[2048,512]{1,0:T(8,128)(2,1)}, u32[]{:S(2)}, u32[]{:S(2)}) collective-permute-start(bf16[2048,512]{1,0:T(8,128)(2,1)} %term.8), channel_id=1, source_target_pairs={{0,4},{4,0},{8,12},{12,8},{16,20},{20,16},{24,28},{28,24},{1,5},{5... | collective-permute-start | bytes 6291464 | tf_op jit(solution)/shard_map/ppermute | solution.py:278
  99.0 1.9 copy-start.16
  106.7 25.0 %collective-permute-start.1 = (bf16[512,512]{1,0:T(8,128)(2,1)}, bf16[512,512]{1,0:T(8,128)(2,1)S(1)}, u32[]{:S(2)}, u32[]{:S(2)}) collective-permute-start(bf16[512,512]{1,0:T(8,128)(2,1)} %get-tuple-element.86), channel_id=1, source_target_pairs={{0,8},{4,12},{1,9},{5,13},{2,10},{6,14},{3,11},{7,15}} | collective-permute-start | bytes 1572872 | tf_op jit(solution)/shard_map/ppermute | solution.py:313
  108.0 23.6 %collective-permute-start.2 = (bf16[512,512]{1,0:T(8,128)(2,1)S(1)}, bf16[512,512]{1,0:T(8,128)(2,1)}, u32[]{:S(2)}, u32[]{:S(2)}) collective-permute-start(bf16[512,512]{1,0:T(8,128)(2,1)S(1)} %get-tuple-element.88), channel_id=1, source_target_pairs={{24,16},{28,20},{25,17},{29,21},{26,18},{30,22},{27,19},{31,23}} | collective-permute-start | bytes 1572872 | tf_op jit(solution)/shard_map/ppermute | solution.py:314
  134.3 20.9 %collective-permute-start.3 = (bf16[512,512]{1,0:T(8,128)(2,1)}, bf16[512,512]{1,0:T(8,128)(2,1)}, u32[]{:S(2)}, u32[]{:S(2)}) collective-permute-start(bf16[512,512]{1,0:T(8,128)(2,1)} %get-tuple-element.89), channel_id=1, source_target_pairs={{0,8},{4,12},{8,16},{12,20},{1,9},{5,13},{9,17},{13,21},{2,10},{6,... | collective-permute-start | bytes 1572872 | tf_op jit(solution)/shard_map/ppermute | solution.py:313
  139.4 15.8 %collective-permute-start.4 = (bf16[512,512]{1,0:T(8,128)(2,1)S(1)}, bf16[512,512]{1,0:T(8,128)(2,1)}, u32[]{:S(2)}, u32[]{:S(2)}) collective-permute-start(bf16[512,512]{1,0:T(8,128)(2,1)S(1)} %get-tuple-element.93), channel_id=1, source_target_pairs={{16,8},{20,12},{24,16},{28,20},{17,9},{21,13},{25,17},{29,21},{18,... | collective-permute-start | bytes 1572872 | tf_op jit(solution)/shard_map/ppermute | solution.py:314
  140.8 2.8 copy-start
  143.6 2.5 copy-start.6
  158.0 39.9 %collective-permute-start.5 = (bf16[512,512]{1,0:T(8,128)(2,1)}, bf16[512,512]{1,0:T(8,128)(2,1)}, u32[]{:S(2)}, u32[]{:S(2)}) collective-permute-start(bf16[512,512]{1,0:T(8,128)(2,1)} %get-tuple-element.94), channel_id=1, source_target_pairs={{0,8},{4,12},{8,16},{12,20},{16,24},{20,28},{1,9},{5,13},{9,17},{1... | collective-permute-start | bytes 1572872 | tf_op jit(solution)/shard_map/ppermute | solution.py:313
  178.5 27.2 %collective-permute-start.6 = (bf16[512,512]{1,0:T(8,128)(2,1)S(1)}, bf16[512,512]{1,0:T(8,128)(2,1)}, u32[]{:S(2)}, u32[]{:S(2)}) collective-permute-start(bf16[512,512]{1,0:T(8,128)(2,1)S(1)} %get-tuple-element.96), channel_id=1, source_target_pairs={{8,0},{12,4},{16,8},{20,12},{24,16},{28,20},{9,1},{13,5},{17,9},{2... | collective-permute-start | bytes 1572872 | tf_op jit(solution)/shard_map/ppermute | solution.py:314
  179.9 28.4 %copy-start.23 = (bf16[768,768]{1,0:T(8,128)(2,1)S(1)}, bf16[768,768]{1,0:T(8,128)(2,1)}, u32[]{:S(2)}) copy-start(bf16[768,768]{1,0:T(8,128)(2,1)} %copy-done.22) | copy-start | bytes 3538948
  208.3 6.1 %copy-start.13 = (bf16[2048,768]{1,0:T(8,128)(2,1)S(1)}, bf16[2048,768]{1,0:T(8,128)(2,1)}, u32[]{:S(2)}) copy-start(bf16[2048,768]{1,0:T(8,128)(2,1)} %copy-done.12) | copy-start | bytes 9437188
  214.4 4.2 copy-start.20
  218.6 6.4 %collective-permute-start.7 = (bf16[2048,768]{1,0:T(8,128)(2,1)}, bf16[2048,768]{1,0:T(8,128)(2,1)}, u32[]{:S(2)}, u32[]{:S(2)}) collective-permute-start(bf16[2048,768]{1,0:T(8,128)(2,1)} %term.10), channel_id=1, source_target_pairs={{0,4},{4,0},{8,12},{12,8},{16,20},{20,16},{24,28},{28,24},{1,5},{5... | collective-permute-start | bytes 9437192 | tf_op jit(solution)/shard_map/ppermute | solution.py:278
  218.6 278.3 %reduce-scatter.2.cloned.1.call-start = ((), (), s32[]{:S(2)}) async-start(), calls=%async_computation.5 | async-start | bytes 7864320 | tf_op jit(solution)/shard_map/reduce_scatter | solution.py:433
  218.6 1.9 copy-start.10
  226.7 47.1 %collective-permute-start.8 = (bf16[512,768]{1,0:T(8,128)(2,1)S(1)}, bf16[512,768]{1,0:T(8,128)(2,1)S(1)}, u32[]{:S(2)}, u32[]{:S(2)}) collective-permute-start(bf16[512,768]{1,0:T(8,128)(2,1)S(1)} %get-tuple-element.102), channel_id=1, source_target_pairs={{0,8},{4,12},{1,9},{5,13},{2,10},{6,14},{3,11},{7,15}} | collective-permute-start | bytes 2359304 | tf_op jit(solution)/shard_map/ppermute | solution.py:313
  239.3 34.5 %collective-permute-start.9 = (bf16[512,768]{1,0:T(8,128)(2,1)S(1)}, bf16[512,768]{1,0:T(8,128)(2,1)S(1)}, u32[]{:S(2)}, u32[]{:S(2)}) collective-permute-start(bf16[512,768]{1,0:T(8,128)(2,1)S(1)} %get-tuple-element.104), channel_id=1, source_target_pairs={{24,16},{28,20},{25,17},{29,21},{26,18},{30,22},{27,19},{31,23}} | collective-permute-start | bytes 2359304 | tf_op jit(solution)/shard_map/ppermute | solution.py:314
  276.9 25.9 %collective-permute-start.10 = (bf16[512,768]{1,0:T(8,128)(2,1)}, bf16[512,768]{1,0:T(8,128)(2,1)}, u32[]{:S(2)}, u32[]{:S(2)}) collective-permute-start(bf16[512,768]{1,0:T(8,128)(2,1)} %get-tuple-element.105), channel_id=1, source_target_pairs={{0,8},{4,12},{8,16},{12,20},{1,9},{5,13},{9,17},{13,21},{2,10},{6,... | collective-permute-start | bytes 2359304 | tf_op jit(solution)/shard_map/ppermute | solution.py:313
  282.2 20.6 %collective-permute-start.11 = (bf16[512,768]{1,0:T(8,128)(2,1)}, bf16[512,768]{1,0:T(8,128)(2,1)}, u32[]{:S(2)}, u32[]{:S(2)}) collective-permute-start(bf16[512,768]{1,0:T(8,128)(2,1)} %get-tuple-element.109), channel_id=1, source_target_pairs={{16,8},{20,12},{24,16},{28,20},{17,9},{21,13},{25,17},{29,21},{18,... | collective-permute-start | bytes 2359304 | tf_op jit(solution)/shard_map/ppermute | solution.py:314
  283.8 2.8 copy-start.5
  286.6 2.8 copy-start.29
  296.3 37.8 %copy-start.24 = (bf16[768,768]{1,0:T(8,128)(2,1)}, bf16[768,768]{1,0:T(8,128)(2,1)S(1)}, u32[]{:S(2)}) copy-start(bf16[768,768]{1,0:T(8,128)(2,1)S(1)} %product.6.qkv_ref) | copy-start | bytes 3538948
  305.2 21.0 %collective-permute-start.12 = (bf16[512,768]{1,0:T(8,128)(2,1)S(1)}, bf16[512,768]{1,0:T(8,128)(2,1)S(1)}, u32[]{:S(2)}, u32[]{:S(2)}) collective-permute-start(bf16[512,768]{1,0:T(8,128)(2,1)S(1)} %get-tuple-element.110), channel_id=1, source_target_pairs={{0,8},{4,12},{8,16},{12,20},{16,24},{20,28},{1,9},{5,13},{9,17},{1... | collective-permute-start | bytes 2359304 | tf_op jit(solution)/shard_map/ppermute | solution.py:313
  309.7 21.6 %collective-permute-start.13 = (bf16[512,768]{1,0:T(8,128)(2,1)S(1)}, bf16[512,768]{1,0:T(8,128)(2,1)S(1)}, u32[]{:S(2)}, u32[]{:S(2)}) collective-permute-start(bf16[512,768]{1,0:T(8,128)(2,1)S(1)} %get-tuple-element.112), channel_id=1, source_target_pairs={{8,0},{12,4},{16,8},{20,12},{24,16},{28,20},{9,1},{13,5},{17,9},{2... | collective-permute-start | bytes 2359304 | tf_op jit(solution)/shard_map/ppermute | solution.py:314
  331.3 8.0 %copy-start.19 = (bf16[2048,768]{1,0:T(8,128)(2,1)S(1)}, bf16[2048,768]{1,0:T(8,128)(2,1)}, u32[]{:S(2)}) copy-start(bf16[2048,768]{1,0:T(8,128)(2,1)} %copy-done.18) | copy-start | bytes 9437188
  339.2 2.4 copy-start.17
  341.6 4.2 collective-permute-start.14
  345.8 15.4 %copy-start.34 = (bf16[2048,512]{1,0:T(8,128)(2,1)}, bf16[2048,512]{1,0:T(8,128)(2,1)S(1)}, u32[]{:S(2)}) copy-start(bf16[2048,512]{1,0:T(8,128)(2,1)S(1)} %collective-permute-done.14) | copy-start | bytes 6291460
  346.1 15.1 %collective-permute-start.15 = (bf16[512,512]{1,0:T(8,128)(2,1)S(1)}, bf16[512,512]{1,0:T(8,128)(2,1)S(1)}, u32[]{:S(2)}, u32[]{:S(2)}) collective-permute-start(bf16[512,512]{1,0:T(8,128)(2,1)S(1)} %get-tuple-element.118), channel_id=1, source_target_pairs={{0,8},{4,12},{1,9},{5,13},{2,10},{6,14},{3,11},{7,15}} | collective-permute-start | bytes 1572872 | tf_op jit(solution)/shard_map/ppermute | solution.py:313
  349.8 11.4 %collective-permute-start.16 = (bf16[512,512]{1,0:T(8,128)(2,1)S(1)}, bf16[512,512]{1,0:T(8,128)(2,1)S(1)}, u32[]{:S(2)}, u32[]{:S(2)}) collective-permute-start(bf16[512,512]{1,0:T(8,128)(2,1)S(1)} %get-tuple-element.120), channel_id=1, source_target_pairs={{24,16},{28,20},{25,17},{29,21},{26,18},{30,22},{27,19},{31,23}} | collective-permute-start | bytes 1572872 | tf_op jit(solution)/shard_map/ppermute | solution.py:314
  362.5 2.8 copy-start.1
  365.2 2.2 copy-start.8
  367.4 5.9 %copy-start.7 = (bf16[4096,512]{1,0:T(8,128)(2,1)S(1)}, bf16[4096,512]{1,0:T(8,128)(2,1)}, u32[]{:S(2)}) copy-start(bf16[4096,512]{1,0:T(8,128)(2,1)} %all-gather.7.cloned.1.call-done.b.refs_2_) | copy-start | bytes 12582916
  367.4 5.9 %copy-start.28 = (bf16[768,512]{1,0:T(8,128)(2,1)S(1)}, bf16[768,512]{1,0:T(8,128)(2,1)}, u32[]{:S(2)}) copy-start(bf16[768,512]{1,0:T(8,128)(2,1)} %copy-done.26) | copy-start | bytes 2359300
  381.8 2.6 copy-start.2
  385.5 15.0 %collective-permute-start.17 = (bf16[512,512]{1,0:T(8,128)(2,1)S(1)}, bf16[512,512]{1,0:T(8,128)(2,1)S(1)}, u32[]{:S(2)}, u32[]{:S(2)}) collective-permute-start(bf16[512,512]{1,0:T(8,128)(2,1)S(1)} %copy-done.40), channel_id=1, source_target_pairs={{0,8},{4,12},{8,16},{12,20},{1,9},{5,13},{9,17},{13,21},{2,10},{6,... | collective-permute-start | bytes 1572872 | tf_op jit(solution)/shard_map/ppermute | solution.py:313
  389.9 10.6 %collective-permute-start.18 = (bf16[512,512]{1,0:T(8,128)(2,1)S(1)}, bf16[512,512]{1,0:T(8,128)(2,1)S(1)}, u32[]{:S(2)}, u32[]{:S(2)}) collective-permute-start(bf16[512,512]{1,0:T(8,128)(2,1)S(1)} %get-tuple-element.126), channel_id=1, source_target_pairs={{16,8},{20,12},{24,16},{28,20},{17,9},{21,13},{25,17},{29,21},{18,... | collective-permute-start | bytes 1572872 | tf_op jit(solution)/shard_map/ppermute | solution.py:314
  402.2 23.1 %copy-start.25 = (bf16[768,768]{1,0:T(8,128)(2,1)S(1)}, bf16[768,768]{1,0:T(8,128)(2,1)}, u32[]{:S(2)}) copy-start(bf16[768,768]{1,0:T(8,128)(2,1)} %copy-done.24) | copy-start | bytes 3538948
  402.2 23.1 %copy-start.32 = (bf16[768,512]{1,0:T(8,128)(2,1)S(1)}, bf16[768,512]{1,0:T(8,128)(2,1)}, u32[]{:S(2)}) copy-start(bf16[768,512]{1,0:T(8,128)(2,1)} %copy-done.31) | copy-start | bytes 2359300
  402.2 16.7 %collective-permute-start.19 = (bf16[512,512]{1,0:T(8,128)(2,1)S(1)}, bf16[512,512]{1,0:T(8,128)(2,1)S(1)}, u32[]{:S(2)}, u32[]{:S(2)}) collective-permute-start(bf16[512,512]{1,0:T(8,128)(2,1)S(1)} %get-tuple-element.127), channel_id=1, source_target_pairs={{0,8},{4,12},{8,16},{12,20},{16,24},{20,28},{1,9},{5,13},{9,17},{1... | collective-permute-start | bytes 1572872 | tf_op jit(solution)/shard_map/ppermute | solution.py:313
  409.4 13.6 %collective-permute-start.20 = (bf16[512,512]{1,0:T(8,128)(2,1)S(1)}, bf16[512,512]{1,0:T(8,128)(2,1)S(1)}, u32[]{:S(2)}, u32[]{:S(2)}) collective-permute-start(bf16[512,512]{1,0:T(8,128)(2,1)S(1)} %get-tuple-element.129), channel_id=1, source_target_pairs={{8,0},{12,4},{16,8},{20,12},{24,16},{28,20},{9,1},{13,5},{17,9},{2... | collective-permute-start | bytes 1572872 | tf_op jit(solution)/shard_map/ppermute | solution.py:314
  425.3 6.1 %copy-start.14 = (bf16[2048,768]{1,0:T(8,128)(2,1)S(1)}, bf16[2048,768]{1,0:T(8,128)(2,1)}, u32[]{:S(2)}) copy-start(bf16[2048,768]{1,0:T(8,128)(2,1)} %copy-done.12) | copy-start | bytes 9437188
  431.3 3.3 copy-start.11
  434.5 5.7 %collective-permute-start.21 = (bf16[2048,768]{1,0:T(8,128)(2,1)S(1)}, bf16[2048,768]{1,0:T(8,128)(2,1)S(1)}, u32[]{:S(2)}, u32[]{:S(2)}) collective-permute-start(bf16[2048,768]{1,0:T(8,128)(2,1)S(1)} %term.14), channel_id=1, source_target_pairs={{0,4},{4,0},{8,12},{12,8},{16,20},{20,16},{24,28},{28,24},{1,5},{5... | collective-permute-start | bytes 9437192 | tf_op jit(solution)/shard_map/ppermute | solution.py:278
  440.3 40.9 %copy-start.33 = (bf16[2048,768]{1,0:T(8,128)(2,1)}, bf16[2048,768]{1,0:T(8,128)(2,1)S(1)}, u32[]{:S(2)}) copy-start(bf16[2048,768]{1,0:T(8,128)(2,1)S(1)} %collective-permute-done.21) | copy-start | bytes 9437188
  440.6 19.3 %collective-permute-start.22 = (bf16[512,768]{1,0:T(8,128)(2,1)S(1)}, bf16[512,768]{1,0:T(8,128)(2,1)S(1)}, u32[]{:S(2)}, u32[]{:S(2)}) collective-permute-start(bf16[512,768]{1,0:T(8,128)(2,1)S(1)} %get-tuple-element.135), channel_id=1, source_target_pairs={{0,8},{4,12},{1,9},{5,13},{2,10},{6,14},{3,11},{7,15}} | collective-permute-start | bytes 2359304 | tf_op jit(solution)/shard_map/ppermute | solution.py:313
  442.9 17.0 %collective-permute-start.23 = (bf16[512,768]{1,0:T(8,128)(2,1)S(1)}, bf16[512,768]{1,0:T(8,128)(2,1)S(1)}, u32[]{:S(2)}, u32[]{:S(2)}) collective-permute-start(bf16[512,768]{1,0:T(8,128)(2,1)S(1)} %get-tuple-element.137), channel_id=1, source_target_pairs={{24,16},{28,20},{25,17},{29,21},{26,18},{30,22},{27,19},{31,23}} | collective-permute-start | bytes 2359304 | tf_op jit(solution)/shard_map/ppermute | solution.py:314
  460.5 20.6 %collective-permute-start.24 = (bf16[512,768]{1,0:T(8,128)(2,1)S(1)}, bf16[512,768]{1,0:T(8,128)(2,1)S(1)}, u32[]{:S(2)}, u32[]{:S(2)}) collective-permute-start(bf16[512,768]{1,0:T(8,128)(2,1)S(1)} %get-tuple-element.138), channel_id=1, source_target_pairs={{0,8},{4,12},{8,16},{12,20},{1,9},{5,13},{9,17},{13,21},{2,10},{6,... | collective-permute-start | bytes 2359304 | tf_op jit(solution)/shard_map/ppermute | solution.py:313
  465.0 16.2 %collective-permute-start.25 = (bf16[512,768]{1,0:T(8,128)(2,1)S(1)}, bf16[512,768]{1,0:T(8,128)(2,1)S(1)}, u32[]{:S(2)}, u32[]{:S(2)}) collective-permute-start(bf16[512,768]{1,0:T(8,128)(2,1)S(1)} %get-tuple-element.140), channel_id=1, source_target_pairs={{16,8},{20,12},{24,16},{28,20},{17,9},{21,13},{25,17},{29,21},{18,... | collective-permute-start | bytes 2359304 | tf_op jit(solution)/shard_map/ppermute | solution.py:314
  483.1 22.1 %collective-permute-start.26 = (bf16[512,768]{1,0:T(8,128)(2,1)}, bf16[512,768]{1,0:T(8,128)(2,1)}, u32[]{:S(2)}, u32[]{:S(2)}) collective-permute-start(bf16[512,768]{1,0:T(8,128)(2,1)} %get-tuple-element.141), channel_id=1, source_target_pairs={{0,8},{4,12},{8,16},{12,20},{16,24},{20,28},{1,9},{5,13},{9,17},{1... | collective-permute-start | bytes 2359304 | tf_op jit(solution)/shard_map/ppermute | solution.py:313
  490.7 19.5 %collective-permute-start.27 = (bf16[512,768]{1,0:T(8,128)(2,1)}, bf16[512,768]{1,0:T(8,128)(2,1)}, u32[]{:S(2)}, u32[]{:S(2)}) collective-permute-start(bf16[512,768]{1,0:T(8,128)(2,1)} %get-tuple-element.144), channel_id=1, source_target_pairs={{8,0},{12,4},{16,8},{20,12},{24,16},{28,20},{9,1},{13,5},{17,9},{2... | collective-permute-start | bytes 2359304 | tf_op jit(solution)/shard_map/ppermute | solution.py:314
  492.0 2.1 copy-start.37
  513.3 1.7 slice-start.1
  (15 other events, 20.0 us)
Sparse Core Ops, SparseCore 0:
  10.2 67.4 all-gather.4
  79.9 52.2 all-gather.6
  133.8 85.1 all-gather.8
  221.1 69.0 all-gather.10
  384.6 70.6 reduce-scatter.1
where the time goes:
time: 533 us; the launch traced here: 523 us
  waiting for transfers between devices  239 us (45%)
  starting transfers between devices  93.1 us (17%)
  Pallas kernels  88.8 us (17%)
  local copies, waits for them, and re-layouts  46 us (9%)
  other arithmetic  42.2 us (8%)
  between operations  14.9 us (3%)
    ppermute x12, waiting for transfers between devices, advance(): lax.ppermute(up, 'wide', [(w, w + 2) for w in range(2 * t)])  164 us
    ppermute x12, starting transfers between devices, advance(): lax.ppermute(up, 'wide', [(w, w + 2) for w in range(2 * t)])  78.7 us
    all_gather x4, waiting for transfers between devices, shards(): weights.append(lax.all_gather(piece, 'wide', axis=0, tiled=True))  47.8 us
    unnamed x88, local copies, waits for them, and re-layouts  42.7 us
    pallas_call x8, Pallas kernels, term(): pl.pallas_call(term_kernel, grid=(features // step,), out_shape=jax.Shape...  23.9 us
    pallas_call x4, Pallas kernels, product(): pl.pallas_call(product_kernel, grid=(depth // step,), out_shape=jax.Shape...  23.8 us
    ppermute x12, waiting for transfers between devices, advance(): lax.ppermute(down, 'wide', [(w, w - 2) for w in range(2 * far, 2 * chips)])  22 us
    convert_element_type x12, other arithmetic, messages(): sums.append(total.astype(BF16))  21 us
  transfers between devices with their start and end apart: 33, of which 19 were waited for; matrix products, arithmetic and copies ran while one was open for 7% of the time, Pallas kernels for 14%

commit v1 on v0

v1 whole, which is shorter than its diff:
```python
import functools
import jax
import jax.numpy as jnp
from jax import lax
from jax.experimental import pallas as pl
from jax.experimental.pallas import tpu as pltpu
from jax.sharding import PartitionSpec as P

HEAD_DIM = 128
BLOCK = 256
EPSILON = 1e-05
MASKED = -1e30
F32 = jnp.float32
BF16 = jnp.bfloat16
VMEM_LIMIT = 60 * 2**20
SHORT = pl.CostEstimate(flops=1, bytes_accessed=1, transcendentals=0)


def nt(a, b):
    return lax.dot_general(a, b, (((1,), (1,)), ((), ())), preferred_element_type=F32)


def nn(a, b):
    return lax.dot_general(a, b, (((1,), (0,)), ((), ())), preferred_element_type=F32)


def masked_scores(keys, queries, start, size):
    scores = nt(keys, queries) * HEAD_DIM ** (-0.5)
    key_at = lax.broadcasted_iota(jnp.int32, (size, size), 0)
    query_at = lax.broadcasted_iota(jnp.int32, (size, size), 1)
    last = jnp.where(key_at <= query_at, scores[start:], MASKED)
    if start == 0:
        return last
    return jnp.concatenate([scores[:start], last], axis=0)


def forward_kernel(members, block, qkv_ref, mixed_ref, lse_ref):
    length = qkv_ref.shape[0]
    width = HEAD_DIM
    key_col, value_col = members * width, (members + 1) * width
    values_t = qkv_ref[:, value_col : value_col + width].T
    for h in range(members):
        for start in range(0, length, block):
            stop = start + block
            queries = qkv_ref[start:stop, h * width : (h + 1) * width]
            keys = qkv_ref[:stop, key_col : key_col + width]
            scores = masked_scores(keys, queries, start, block)
            highest = jnp.max(scores, axis=0, keepdims=True)
            exponent = jnp.exp(scores - highest)
            total = jnp.sum(exponent, axis=0, keepdims=True)
            rounded = (exponent * (1.0 / total)).astype(BF16)
            mixed_t = nn(values_t[:, :stop], rounded)
            mixed_ref[start:stop, h * width : (h + 1) * width] = mixed_t.T.astype(BF16)
            lse_ref[h : h + 1, start:stop] = highest + jnp.log(total)


def attend_forward(qkv, members, block):
    length = qkv.shape[0]
    width = HEAD_DIM
    vmem = pl.BlockSpec(memory_space=pltpu.VMEM)
    return pl.pallas_call(
        functools.partial(forward_kernel, members, block),
        out_shape=(
            jax.ShapeDtypeStruct((length, members * width), BF16),
            jax.ShapeDtypeStruct((members, length), F32),
        ),
        in_specs=[vmem],
        out_specs=(vmem, vmem),
        compiler_params=pltpu.CompilerParams(vmem_limit_bytes=VMEM_LIMIT),
        cost_estimate=SHORT,
        name="attend_forward",
    )(qkv)


def backward_kernel(members, block, qkv_ref, grad_ref, lse_ref, out_ref, gk_ref, gv_ref):
    length = qkv_ref.shape[0]
    width = HEAD_DIM
    key_col, value_col = members * width, (members + 1) * width
    keys_t = qkv_ref[:, key_col : key_col + width].T
    gk_ref[...] = jnp.zeros_like(gk_ref)
    gv_ref[...] = jnp.zeros_like(gv_ref)
    for h in range(members):
        cols = slice(h * width, (h + 1) * width)
        for start in range(0, length, block):
            stop = start + block
            queries = qkv_ref[start:stop, cols]
            grads = grad_ref[start:stop, cols]
            keys = qkv_ref[:stop, key_col : key_col + width]
            values = qkv_ref[:stop, value_col : value_col + width]
            scores = masked_scores(keys, queries, start, block)
            probs = jnp.exp(scores - lse_ref[h : h + 1, start:stop])
            grad_probs = nt(values, grads)
            gv_ref[:stop, :] += nn(probs.astype(BF16), grads)
            inner = jnp.sum(grad_probs * probs, axis=0, keepdims=True)
            grad_scores = (probs * (grad_probs - inner) * width ** (-0.5)).astype(BF16)
            gk_ref[:stop, :] += nn(grad_scores, queries)
            out_ref[start:stop, cols] = nn(keys_t[:, :stop], grad_scores).T.astype(BF16)
    out_ref[:, key_col : key_col + width] = gk_ref[...].astype(BF16)
    out_ref[:, value_col : value_col + width] = gv_ref[...].astype(BF16)


def attend_backward(qkv, grad_mixed, lse, members, block):
    length = qkv.shape[0]
    width = HEAD_DIM
    vmem = pl.BlockSpec(memory_space=pltpu.VMEM)
    return pl.pallas_call(
        functools.partial(backward_kernel, members, block),
        out_shape=jax.ShapeDtypeStruct(qkv.shape, BF16),
        in_specs=[vmem, vmem, vmem],
        out_specs=vmem,
        scratch_shapes=[pltpu.VMEM((length, width), F32), pltpu.VMEM((length, width), F32)],
        compiler_params=pltpu.CompilerParams(vmem_limit_bytes=VMEM_LIMIT),
        cost_estimate=SHORT,
        name="attend_backward",
    )(qkv, grad_mixed, lse)


def pack_kernel(groups, query, key, value, out, first, second):
    width = HEAD_DIM
    span = query.shape[1] // groups
    at = 0

    def put(source, start, cols):
        nonlocal at
        first[:, at : at + cols] = source[:, start : start + cols]
        at += cols

    for g in range(groups):
        put(query, g * span, span)
        put(key, g * width, width)
        put(value, g * width, width)
    if groups > 1:
        put(out, 0, (groups - 1) * span)
    second[...] = out[:, (groups - 1) * span :]


def pack(query, key, value, out):
    rows, cols = query.shape
    groups = key.shape[1] // HEAD_DIM
    span = cols // groups
    early = 2 * cols - span + key.shape[1] + value.shape[1]
    return pl.pallas_call(
        functools.partial(pack_kernel, groups),
        out_shape=(
            jax.ShapeDtypeStruct((rows, early), BF16),
            jax.ShapeDtypeStruct((rows, span), BF16),
        ),
        compiler_params=pltpu.CompilerParams(vmem_limit_bytes=VMEM_LIMIT),
        cost_estimate=SHORT,
        name="pack",
    )(query, key, value, out)


def norm_kernel(x_ref, gain_ref, grad_ref, out, out_t, grad_t):
    features = x_ref.shape[1]
    step = 512 if features % 512 == 0 else features
    total = None
    for at in range(0, features, step):
        values = x_ref[:, at : at + step].astype(F32)
        part = jnp.sum(values * values, axis=-1, keepdims=True)
        total = part if total is None else total + part
    scale = lax.rsqrt(total / features + EPSILON)
    for at in range(0, features, step):
        cols = slice(at, at + step)
        normed = (x_ref[:, cols].astype(F32) * scale * gain_ref[:, cols]).astype(BF16)
        out[:, cols] = normed
        out_t[cols, :] = normed.T
        grad_t[cols, :] = grad_ref[:, cols].T


def normalize(activations, gain, cotangent):
    length, features = activations.shape
    step = 128 if length % 128 == 0 else length
    whole = pl.BlockSpec((step, features), lambda i: (i, 0))
    turned = pl.BlockSpec((features, step), lambda i: (0, i))
    shape_t = jax.ShapeDtypeStruct((features, length), BF16)
    return pl.pallas_call(
        norm_kernel,
        grid=(length // step,),
        out_shape=(jax.ShapeDtypeStruct((length, features), BF16), shape_t, shape_t),
        in_specs=[whole, pl.BlockSpec((1, features), lambda i: (0, 0)), whole],
        out_specs=(whole, turned, turned),
        compiler_params=pltpu.CompilerParams(vmem_limit_bytes=VMEM_LIMIT),
        cost_estimate=SHORT,
        name="normalize",
    )(activations, gain.astype(F32).reshape(1, -1), cotangent)


def product_kernel(a, b, out, total):
    part = nn(a[...], b[...])
    at = pl.program_id(0)

    @pl.when(at == 0)
    def _():
        total[...] = part

    @pl.when(at > 0)
    def _():
        total[...] += part

    @pl.when(at == pl.num_programs(0) - 1)
    def _():
        out[...] = total[...].astype(BF16)


def product(rows, weights, at, cols):
    length, depth = rows.shape
    step = 1024 if depth % 1024 == 0 else depth
    return pl.pallas_call(
        product_kernel,
        grid=(depth // step,),
        out_shape=jax.ShapeDtypeStruct((length, cols), BF16),
        in_specs=[
            pl.BlockSpec((length, step), lambda i: (0, i)),
            pl.BlockSpec((step, cols), lambda i: (i, at)),
        ],
        out_specs=pl.BlockSpec((length, cols), lambda i: (0, 0)),
        scratch_shapes=[pltpu.VMEM((length, cols), F32)],
        compiler_params=pltpu.CompilerParams(vmem_limit_bytes=VMEM_LIMIT),
        cost_estimate=SHORT,
        name="product",
    )(rows, weights)


def terms_kernel(count, *refs):
    lefts, rights, out = refs[:count], refs[count : 2 * count], refs[-1]
    at = 0
    for left, right in zip(lefts, rights):
        cols = right.shape[1]
        out[:, at : at + cols] = nn(left[...], right[...]).astype(BF16)
        at += cols


def terms(lefts, rights):
    features, length = lefts[0].shape
    cols = sum(right.shape[1] for right in rights)
    step = 512 if features % 512 == 0 else features
    count = len(lefts)
    return pl.pallas_call(
        functools.partial(terms_kernel, count),
        grid=(features // step,),
        out_shape=jax.ShapeDtypeStruct((features, cols), BF16),
        in_specs=[pl.BlockSpec((step, length), lambda i: (i, 0))] * count
        + [pl.BlockSpec(right.shape, lambda i: (0, 0)) for right in rights],
        out_specs=pl.BlockSpec((step, cols), lambda i: (i, 0)),
        compiler_params=pltpu.CompilerParams(vmem_limit_bytes=VMEM_LIMIT),
        cost_estimate=SHORT,
        name="terms",
    )(*lefts, *rights)


def project_kernel(count, *refs):
    out = refs[-1]
    total = None
    for mixed, side in zip(refs[:count], refs[count : 2 * count]):
        part = nt(mixed[...], side[...])
        total = part if total is None else total + part
    out[...] = total.astype(BF16)


def project(mixed, sides, places):
    length, span = mixed[0].shape
    features = sides[0].shape[0]
    step = 512 if features % 512 == 0 else features
    count = len(mixed)
    return pl.pallas_call(
        functools.partial(project_kernel, count),
        grid=(features // step,),
        out_shape=jax.ShapeDtypeStruct((length, features), BF16),
        in_specs=[pl.BlockSpec((length, span), lambda i: (0, 0))] * count
        + [pl.BlockSpec((step, span), lambda i, at=at: (i, at)) for at in places],
        out_specs=pl.BlockSpec((length, step), lambda i: (0, i)),
        compiler_params=pltpu.CompilerParams(vmem_limit_bytes=VMEM_LIMIT),
        cost_estimate=SHORT,
        name="project",
    )(*mixed, *sides)


class Order:
    def __init__(self):
        self.last = None

    def __call__(self, compute, *operands):
        result = compute(*self.after(*operands))
        leaves, form = jax.tree.flatten(result)
        if len(leaves) > 1:
            leaves = lax.optimization_barrier(tuple(leaves))
        self.last = leaves[0]
        return jax.tree.unflatten(form, leaves)

    def after(self, *operands):
        if self.last is None:
            return operands
        least = min(range(len(operands)), key=lambda i: operands[i].size)
        tied = lax.optimization_barrier((self.last, operands[least]))[1]
        return operands[:least] + (tied,) + operands[least + 1 :]


def narrow_sum(parts, size):
    own = lax.axis_index("narrow")
    share = parts.shape[1] // size
    even = size & (size - 1) == 0

    def columns_of(device):
        return lax.dynamic_slice_in_dim(parts, device * share, share, 1)

    arrived = []
    for shift in range(1, size):
        to = [n ^ shift if even else (n + shift) % size for n in range(size)]
        mine = own ^ shift if even else (own + shift) % size
        arrived.append(lax.ppermute(columns_of(mine), "narrow", list(enumerate(to))))
    return columns_of(own), arrived


def shards(sizes, activations, gain, w_query, w_key, w_value, w_out, cotangent):
    wide, narrow = sizes
    width = HEAD_DIM
    length, features = activations.shape
    groups = w_key.shape[1] // width
    members = w_query.shape[1] // w_key.shape[1]
    block = BLOCK if length % BLOCK == 0 else length
    span = members * width
    full = span + 2 * width
    order = Order()

    first, second = pack(w_query, w_key, w_value, w_out)
    first = lax.all_gather(first, "wide", axis=0, tiled=True)
    second = lax.all_gather(second, "wide", axis=0, tiled=True)

    def out_place(g):
        if g == groups - 1:
            return second, 0
        at = groups * full + g * span
        if at % span:
            return first[:, at : at + span], 0
        return first, at // span

    normed, normed_t, cotangent_t = order(normalize, activations, gain, cotangent)
    qkv, mixed, lse, back = [], [], [], []

    def backward(g):
        weights, at = out_place(g)
        grad_mixed = order(lambda a, b: product(a, b, at, span), cotangent, weights)
        back.append(
            order(
                lambda a, b, c: attend_backward(a, b, c, members, block),
                qkv[g],
                grad_mixed,
                lse[g],
            )
        )

    for g in range(groups):
        qkv.append(order(lambda a, b: product(a, b, g, full), normed, first))
        rows, stats = order(lambda a: attend_forward(a, members, block), qkv[g])
        mixed.append(rows)
        lse.append(stats)
        if g < groups - 1:
            backward(g)

    def combined(lefts, rights):
        count = len(lefts)
        return order(lambda *a: terms(a[:count], a[count:]), *lefts, *rights)

    def scattered(part):
        return lax.psum_scatter(part, "wide", scatter_dimension=0, tiled=True)

    early = scattered(
        combined([cotangent_t] * groups + [normed_t] * (groups - 1), mixed + back[: groups - 1])
    )
    backward(groups - 1)
    late = combined([normed_t], [back[groups - 1]])
    places = [out_place(g) for g in range(groups)]
    parts = order(
        lambda *a: project(a[:groups], a[groups:], [at for _, at in places]),
        *mixed,
        *[weights for weights, _ in places],
    )
    own, arrived = narrow_sum(parts, narrow)

    def finish_outputs(activations, *parts):
        share = parts[0].shape[1]
        at = lax.axis_index("narrow") * share
        result = lax.dynamic_slice_in_dim(activations, at, share, 1).astype(F32)
        return (result + sum(part.astype(F32) for part in parts)).astype(BF16)

    outputs = order(finish_outputs, activations, own, *arrived)
    outputs, early, late = lax.optimization_barrier((outputs, early, late))
    late = scattered(late)

    grad_out = early[:, : groups * span].astype(F32)
    sums = [
        early[:, groups * span + g * full : groups * span + (g + 1) * full]
        for g in range(groups - 1)
    ] + [late]

    def joined(pieces):
        pieces = [piece.astype(F32) for piece in pieces]
        return pieces[0] if len(pieces) == 1 else jnp.concatenate(pieces, axis=1)

    grad_query = joined([s[:, :span] for s in sums])
    grad_key = joined([s[:, span : span + width] for s in sums])
    grad_value = joined([s[:, span + width :] for s in sums])
    return (outputs, grad_query, grad_key, grad_value, grad_out)


def solution(mesh):
    return jax.shard_map(
        functools.partial(shards, (mesh.shape["wide"], mesh.shape["narrow"])),
        mesh=mesh,
        in_specs=(
            P("wide", None),
            P(),
            P("wide", "narrow"),
            P("wide", "narrow"),
            P("wide", "narrow"),
            P("wide", "narrow"),
            P("wide", None),
        ),
        out_specs=(
            P("wide", "narrow"),
            P("wide", "narrow"),
            P("wide", "narrow"),
            P("wide", "narrow"),
            P("wide", "narrow"),
        ),
        check_vma=False,
    )
```

time: 533 us -> 465 us (0.87); the launches traced: 523 us -> 464 us
  starting transfers between devices: 93.1 us -> 3.71 us
  waiting for transfers between devices: 239 us -> 302 us
  Pallas kernels: 88.8 us -> 128 us
  local copies, waits for them, and re-layouts: 46 us -> 7.13 us
  other arithmetic: 42.2 us -> 9.26 us
    ppermute x28 -> x3, waiting for transfers between devices: 191 us -> 67.8 us  [narrow_sum(): lax.ppermute(columns_of(mine), 'narrow', list(enumerate(to)))]
    reduce_scatter x1 -> x2, waiting for transfers between devices: 0.01 us -> 94.2 us  [scattered(): return lax.psum_scatter(part, 'wide', scatter_dimension=0, tiled=True)]
    all_gather x4 -> x2, waiting for transfers between devices: 47.8 us -> 139 us  [the longest x1 139 us: shards(): first = lax.all_gather(first, 'wide', axis=0, tiled=True)]
    ppermute x28 -> x3, starting transfers between devices: 92.9 us -> 3.55 us  [narrow_sum(): lax.ppermute(columns_of(mine), 'narrow', list(enumerate(to)))]
    unnamed x88 -> x4, local copies, waits for them, and re-layouts: 42.7 us -> 1.48 us
    convert_element_type x13 -> x2, other arithmetic: 24.7 us -> 6.02 us  [the longest x1 4.44 us: finish_outputs(): return (result + sum((part.astype(F32) for part in parts))).astype(BF16)]
    pallas_call x9 -> x4, Pallas kernels: 34 us -> 47.1 us  [the longest x2 30 us: terms(): pl.pallas_call(functools.partial(terms_kernel, count), grid=(features //...]
    pallas_call x4, Pallas kernels: 23.8 us -> 36.5 us  [product(): pl.pallas_call(product_kernel, grid=(depth // step,), out_shape=jax.Shape...]
  transfers between devices with their start and end apart: 33 -> 7, of which waited for: 19 -> 5; matrix products, arithmetic and copies ran while one was open for 7% -> 2% of each run, Pallas kernels for 14% -> 27%
where the time goes in v1:
time: 465 us; the launch traced here: 464 us
  waiting for transfers between devices  302 us (65%)
  Pallas kernels  128 us (28%)
  between operations  13.9 us (3%)
  other arithmetic  9.26 us (2%)
  local copies, waits for them, and re-layouts  7.13 us (2%)
    all_gather x1, waiting for transfers between devices, shards(): first = lax.all_gather(first, 'wide', axis=0, tiled=True)  139 us
    reduce_scatter x2, waiting for transfers between devices, scattered(): return lax.psum_scatter(part, 'wide', scatter_dimension=0, tiled=True)  94.2 us
    ppermute x3, waiting for transfers between devices, narrow_sum(): lax.ppermute(columns_of(mine), 'narrow', list(enumerate(to)))  67.8 us
    pallas_call x4, Pallas kernels, product(): pl.pallas_call(product_kernel, grid=(depth // step,), out_shape=jax.Shape...  36.5 us
    pallas_call x2, Pallas kernels, terms(): pl.pallas_call(functools.partial(terms_kernel, count), grid=(features //...  30 us
    pallas_call x2, Pallas kernels, attend_backward(): pl.pallas_call(functools.partial(backward_kernel, members, block), out_sh...  17.2 us
    pallas_call x2, Pallas kernels, attend_forward(): pl.pallas_call(functools.partial(forward_kernel, members, block), out_sha...  14.6 us
    pallas_call x1, Pallas kernels, normalize(): pl.pallas_call(norm_kernel, grid=(length // step,), out_shape=(jax.ShapeD...  13.6 us
  transfers between devices with their start and end apart: 7, of which 5 were waited for; matrix products, arithmetic and copies ran while one was open for 2% of the time, Pallas kernels for 27%

profile of v1, /device:TPU:0, one launch (start us, length us, event | category | flops | bytes accessed | tf_op | source)
XLA Modules:
  0.0 463.6 jit_solution(2922237858063203916)
XLA Ops:
  7.2 0.0 copy-start.1
  7.2 0.0 all-gather.3.cloned.1.call-start
  7.2 3.5 pack.1
  10.7 0.0 all-gather.3.cloned.1.call-update
  10.7 0.0 all-gather.5.cloned.1.call-start
  10.8 0.7 all-gather.5.cloned.1.call-update
  11.5 0.0 reduce-scatter.3.cloned.1.call-start
  11.5 0.0 copy-done.1
  11.5 0.6 reshape.17
  12.1 13.6 %normalize.1 = (bf16[768,4096]{1,0:T(8,128)(2,1)}, bf16[4096,768]{1,0:T(8,128)(2,1)}, bf16[4096,768]{1,0:T(8,128)(2,1)}) custom-call(bf16[768,4096]{1,0:T(8,128)(2,1)} %x_ref.1, f32[1,4096]{1,0:T(1,128)} %bitcast.1, bf16[768,4096]{1,0:T(8,128)(2,1)} %a.2), custom_call_target="tpu_custom_call" | custom-call | flops 1 | bytes 1 | tf_op jit(solution)/shard_map/normalize/pallas_call | solution.py:177
  25.8 138.9 %all-gather.3.cloned.1.call-done.b.refs_2_ = bf16[4096,2048]{1,0:T(8,128)(2,1)} async-done(((bf16[512,2048]{1,0:T(8,128)(2,1)}), bf16[4096,2048]{1,0:T(8,128)(2,1)}) %all-gather.3.cloned.1.call-update) | async-done | bytes 16777232 | tf_op jit(solution)/shard_map/all_gather | solution.py:327
  164.7 9.8 %product.4.qkv_ref = bf16[768,768]{1,0:T(8,128)(2,1)} custom-call(bf16[768,4096]{1,0:T(8,128)(2,1)} %get-tuple-element.37.a, bf16[4096,2048]{1,0:T(8,128)(2,1)} %all-gather.3.cloned.1.call-done.b.refs_2_), custom_call_target="tpu_custom_call" | custom-call | flops 1 | bytes 1 | tf_op jit(solution)/shard_map/product/pallas_call | solution.py:209
  174.5 7.3 %attend_forward.2 = (bf16[768,512]{1,0:T(8,128)(2,1)}, f32[4,768]{1,0:T(4,128)}) custom-call(bf16[768,768]{1,0:T(8,128)(2,1)} %product.4.qkv_ref), custom_call_target="tpu_custom_call" | custom-call | flops 1 | bytes 1 | tf_op jit(solution)/shard_map/attend_forward/pallas_call | solution.py:61
  181.8 7.9 %product.5.grad_ref = bf16[768,512]{1,0:T(8,128)(2,1)} custom-call(bf16[768,4096]{1,0:T(8,128)(2,1)} %a.2, bf16[4096,2048]{1,0:T(8,128)(2,1)} %all-gather.3.cloned.1.call-done.b.refs_2_), custom_call_target="tpu_custom_call" | custom-call | flops 1 | bytes 1 | tf_op jit(solution)/shard_map/product/pallas_call | solution.py:209
  189.7 8.6 %attend_backward.2.refs_5_ = bf16[768,768]{1,0:T(8,128)(2,1)} custom-call(bf16[768,768]{1,0:T(8,128)(2,1)} %product.4.qkv_ref, bf16[768,512]{1,0:T(8,128)(2,1)} %product.5.grad_ref, f32[4,768]{1,0:T(4,128)} %get-tuple-element.36.lse_ref), custom_call_target="tpu_custom_call" | custom-call | flops 1 | bytes 1 | tf_op jit(solution)/shard_map/attend_backward/pallas_call | solution.py:106
  198.3 9.7 %product.6.qkv_ref = bf16[768,768]{1,0:T(8,128)(2,1)} custom-call(bf16[768,4096]{1,0:T(8,128)(2,1)} %get-tuple-element.37.a, bf16[4096,2048]{1,0:T(8,128)(2,1)} %all-gather.3.cloned.1.call-done.b.refs_2_), custom_call_target="tpu_custom_call" | custom-call | flops 1 | bytes 1 | tf_op jit(solution)/shard_map/product/pallas_call | solution.py:209
  208.0 7.3 %attend_forward.3 = (bf16[768,512]{1,0:T(8,128)(2,1)}, f32[4,768]{1,0:T(4,128)}) custom-call(bf16[768,768]{1,0:T(8,128)(2,1)} %product.6.qkv_ref), custom_call_target="tpu_custom_call" | custom-call | flops 1 | bytes 1 | tf_op jit(solution)/shard_map/attend_forward/pallas_call | solution.py:61
  215.3 19.2 %terms.2 = bf16[4096,1792]{1,0:T(8,128)(2,1)} custom-call(bf16[4096,768]{1,0:T(8,128)(2,1)} %get-tuple-element.38.refs_0_.refs_1_, bf16[4096,768]{1,0:T(8,128)(2,1)} %get-tuple-element.38.refs_0_.refs_1_, bf16[4096,768]{1,0:T(8,128)(2,1)} %get-tuple-element.28.refs_2_.refs_0_, bf16[768,512]{1,0:T(8,128)(2,1)} %get-tuple-element.46.refs_3_.refs_0_, ...), custom_call_target="tpu_custom_call" | custom-call | flops 1 | bytes 1 | tf_op jit(solution)/shard_map/terms/pallas_call | solution.py:239
  234.5 0.0 reduce-scatter.3.cloned.1.call-update
  234.5 0.0 reduce-scatter.5.cloned.1.call-start
  234.6 0.0 all-gather.5.cloned.1.call-done.b.refs_3_
  234.6 9.1 %product.7.grad_ref = bf16[768,512]{1,0:T(8,128)(2,1)} custom-call(bf16[768,4096]{1,0:T(8,128)(2,1)} %a.2, bf16[4096,512]{1,0:T(8,128)(2,1)} %all-gather.5.cloned.1.call-done.b.refs_3_), custom_call_target="tpu_custom_call" | custom-call | flops 1 | bytes 1 | tf_op jit(solution)/shard_map/product/pallas_call | solution.py:209
  243.7 8.6 %attend_backward.3.refs_1_ = bf16[768,768]{1,0:T(8,128)(2,1)} custom-call(bf16[768,768]{1,0:T(8,128)(2,1)} %product.6.qkv_ref, bf16[768,512]{1,0:T(8,128)(2,1)} %product.7.grad_ref, f32[4,768]{1,0:T(4,128)} %get-tuple-element.45.lse_ref), custom_call_target="tpu_custom_call" | custom-call | flops 1 | bytes 1 | tf_op jit(solution)/shard_map/attend_backward/pallas_call | solution.py:106
  252.3 10.8 %terms.3 = bf16[4096,768]{1,0:T(8,128)(2,1)} custom-call(bf16[4096,768]{1,0:T(8,128)(2,1)} %get-tuple-element.28.refs_2_.refs_0_, bf16[768,768]{1,0:T(8,128)(2,1)} %attend_backward.3.refs_1_), custom_call_target="tpu_custom_call" | custom-call | flops 1 | bytes 1 | tf_op jit(solution)/shard_map/terms/pallas_call | solution.py:239
  263.1 12.6 %project.1 = bf16[768,4096]{1,0:T(8,128)(2,1)} custom-call(bf16[768,512]{1,0:T(8,128)(2,1)} %get-tuple-element.46.refs_3_.refs_0_, bf16[768,512]{1,0:T(8,128)(2,1)} %get-tuple-element.40.refs_4_.refs_1_, bf16[4096,2048]{1,0:T(8,128)(2,1)} %all-gather.3.cloned.1.call-done.b.refs_2_, bf16[4096,512]{1,0:T(8,128)(2,1)} %all-gather.5.cloned.1.call-done.b.refs_3_), custom_call_target="tpu_custom_call" | custom-call | flops 1 | bytes 1 | tf_op jit(solution)/shard_map/project/pallas_call | solution.py:266
  275.7 3.6 constant_dynamic-slice_fusion.3
  279.3 1.2 collective-permute-start
  280.5 1.5 collective-permute-start.1
  282.0 0.8 collective-permute-start.2
  282.8 33.7 %collective-permute-done = bf16[768,1024]{1,0:T(8,128)(2,1)S(1)} collective-permute-done((bf16[768,1024]{1,0:T(8,128)(2,1)S(1)}, bf16[768,1024]{1,0:T(8,128)(2,1)S(1)}, u32[]{:S(2)}, u32[]{:S(2)}) %collective-permute-start) | collective-permute-done | bytes 1572896 | tf_op jit(solution)/shard_map/ppermute | solution.py:311
  316.6 34.0 %collective-permute-done.1 = bf16[768,1024]{1,0:T(8,128)(2,1)S(1)} collective-permute-done((bf16[768,1024]{1,0:T(8,128)(2,1)S(1)}, bf16[768,1024]{1,0:T(8,128)(2,1)S(1)}, u32[]{:S(2)}, u32[]{:S(2)}) %collective-permute-start.1) | collective-permute-done | bytes 1572896 | tf_op jit(solution)/shard_map/ppermute | solution.py:311
  350.6 0.0 collective-permute-done.2
  350.6 4.4 add_convert_fusion
  355.0 26.9 %reduce-scatter.3.cloned.1.call-done = bf16[512,1792]{1,0:T(8,128)(2,1)} async-done(((bf16[4096,1792]{1,0:T(8,128)(2,1)}), bf16[512,1792]{1,0:T(8,128)(2,1)}) %reduce-scatter.3.cloned.1.call-update) | async-done | bytes 1835024 | tf_op jit(solution)/shard_map/reduce_scatter | solution.py:366
  382.0 0.0 copy-start
  382.0 0.0 reduce-scatter.5.cloned.1.call-update
  382.0 1.5 copy-done
  383.5 0.0 slice-start
  383.5 1.6 slice_convert_fusion
  385.1 67.3 %reduce-scatter.5.cloned.1.call-done = bf16[512,768]{1,0:T(8,128)(2,1)} async-done(((bf16[4096,768]{1,0:T(8,128)(2,1)}), bf16[512,768]{1,0:T(8,128)(2,1)}) %reduce-scatter.5.cloned.1.call-update) | async-done | bytes 786448 | tf_op jit(solution)/shard_map/reduce_scatter | solution.py:366
  452.4 1.1 slice.32
  453.4 0.0 slice-done
  453.4 1.6 maximum_convert_fusion
  455.0 1.0 fusion.1
  456.0 1.0 maximum_convert_fusion.1
  (1 shorter events, 0.0 us)
Async XLA Ops:
  7.2 4.4 copy-start.1
  7.2 157.5 %all-gather.3.cloned.1.call-start = ((), (), s32[]{:S(2)}) async-start(), calls=%async_computation.2 | async-start | bytes 18874368 | tf_op jit(solution)/shard_map/all_gather | solution.py:327
  10.7 223.9 %all-gather.5.cloned.1.call-start = ((), (), s32[]{:S(2)}) async-start(), calls=%async_computation.3 | async-start | bytes 4718592 | tf_op jit(solution)/shard_map/all_gather | solution.py:328
  11.5 370.5 %reduce-scatter.3.cloned.1.call-start = ((), (), s32[]{:S(2)}) async-start(), calls=%async_computation.4 | async-start | bytes 16515072 | tf_op jit(solution)/shard_map/reduce_scatter | solution.py:366
  234.5 217.8 %reduce-scatter.5.cloned.1.call-start = ((), (), s32[]{:S(2)}) async-start(), calls=%async_computation.5 | async-start | bytes 7077888 | tf_op jit(solution)/shard_map/reduce_scatter | solution.py:366
  279.3 37.3 %collective-permute-start = (bf16[768,1024]{1,0:T(8,128)(2,1)S(1)}, bf16[768,1024]{1,0:T(8,128)(2,1)S(1)}, u32[]{:S(2)}, u32[]{:S(2)}) collective-permute-start(bf16[768,1024]{1,0:T(8,128)(2,1)S(1)} %get-tuple-element.54), channel_id=1, source_target_pairs={{0,1},{1,0},{2,3},{3,2},{4,5},{5,4},{6,7},{7,6},{8,9},{9,8},{10,11... | collective-permute-start | bytes 4718600 | tf_op jit(solution)/shard_map/ppermute | solution.py:311
  280.5 70.1 %collective-permute-start.1 = (bf16[768,1024]{1,0:T(8,128)(2,1)S(1)}, bf16[768,1024]{1,0:T(8,128)(2,1)S(1)}, u32[]{:S(2)}, u32[]{:S(2)}) collective-permute-start(bf16[768,1024]{1,0:T(8,128)(2,1)S(1)} %get-tuple-element.53), channel_id=1, source_target_pairs={{0,2},{1,3},{2,0},{3,1},{4,6},{5,7},{6,4},{7,5},{8,10},{9,11},{10,... | collective-permute-start | bytes 4718600 | tf_op jit(solution)/shard_map/ppermute | solution.py:311
  282.0 68.6 %collective-permute-start.2 = (bf16[768,1024]{1,0:T(8,128)(2,1)S(1)}, bf16[768,1024]{1,0:T(8,128)(2,1)S(1)}, u32[]{:S(2)}, u32[]{:S(2)}) collective-permute-start(bf16[768,1024]{1,0:T(8,128)(2,1)S(1)} %get-tuple-element.52), channel_id=1, source_target_pairs={{0,3},{1,2},{2,1},{3,0},{4,7},{5,6},{6,5},{7,4},{8,11},{9,10},{10,... | collective-permute-start | bytes 4718600 | tf_op jit(solution)/shard_map/ppermute | solution.py:311
  382.0 1.5 copy-start
  383.5 69.9 %slice-start = ((bf16[512,1792]{1,0:T(8,128)(2,1)}), bf16[512,512]{1,0:T(8,128)(2,1)S(1)}, s32[]{:S(2)}) async-start(bf16[512,1792]{1,0:T(8,128)(2,1)} %reduce-scatter.3.cloned.1.call-done), calls=%async_computation.6 | async-start | bytes 1048576 | tf_op jit(solution)/shard_map/slice | solution.py:401
Sparse Core Ops, SparseCore 0:
  10.8 153.7 all-gather.2
  166.9 45.4 all-gather.4
  234.7 147.2 reduce-scatter.2
  384.1 68.1 reduce-scatter.4

commit v2 on v1

--- a/solution.py
+++ b/solution.py
@@ -115,40 +115,62 @@
     )(qkv, grad_mixed, lse)
 
 
-def pack_kernel(groups, query, key, value, out, first, second):
+def pack_kernel(groups, query, key, value, out, *packed):
     width = HEAD_DIM
     span = query.shape[1] // groups
-    at = 0
-
-    def put(source, start, cols):
-        nonlocal at
-        first[:, at : at + cols] = source[:, start : start + cols]
-        at += cols
-
-    for g in range(groups):
-        put(query, g * span, span)
-        put(key, g * width, width)
-        put(value, g * width, width)
-    if groups > 1:
-        put(out, 0, (groups - 1) * span)
-    second[...] = out[:, (groups - 1) * span :]
+    for g, piece in enumerate(packed):
+        heads = slice(g * span, (g + 1) * span)
+        group = slice(g * width, (g + 1) * width)
+        piece[:, :span] = query[:, heads]
+        piece[:, span : span + width] = key[:, group]
+        piece[:, span + width : span + 2 * width] = value[:, group]
+        piece[:, span + 2 * width :] = out[:, heads]
 
 
 def pack(query, key, value, out):
     rows, cols = query.shape
     groups = key.shape[1] // HEAD_DIM
-    span = cols // groups
-    early = 2 * cols - span + key.shape[1] + value.shape[1]
+    wide = 2 * cols // groups + 2 * HEAD_DIM
     return pl.pallas_call(
         functools.partial(pack_kernel, groups),
-        out_shape=(
-            jax.ShapeDtypeStruct((rows, early), BF16),
-            jax.ShapeDtypeStruct((rows, span), BF16),
-        ),
+        out_shape=(jax.ShapeDtypeStruct((rows, wide), BF16),) * groups,
         compiler_params=pltpu.CompilerParams(vmem_limit_bytes=VMEM_LIMIT),
         cost_estimate=SHORT,
         name="pack",
     )(query, key, value, out)
+
+
+def unpack_kernel(*refs):
+    sums, (grad_query, grad_key, grad_value, grad_out) = refs[:-4], refs[-4:]
+    width = HEAD_DIM
+    span = grad_query.shape[1] // len(sums)
+    for g, part in enumerate(sums):
+        heads = slice(g * span, (g + 1) * span)
+        group = slice(g * width, (g + 1) * width)
+        grad_query[:, heads] = part[:, :span].astype(F32)
+        grad_key[:, group] = part[:, span : span + width].astype(F32)
+        grad_value[:, group] = part[:, span + width : span + 2 * width].astype(F32)
+        grad_out[:, heads] = part[:, span + 2 * width :].astype(F32)
+
+
+def unpack(sums, span):
+    rows = sums[0].shape[0]
+    groups = len(sums)
+    shapes = [
+        jax.ShapeDtypeStruct((rows, groups * cols), F32)
+        for cols in (span, HEAD_DIM, HEAD_DIM, span)
+    ]
+    step = 128 if rows % 128 == 0 else rows
+    return pl.pallas_call(
+        unpack_kernel,
+        grid=(rows // step,),
+        out_shape=shapes,
+        in_specs=[pl.BlockSpec((step, part.shape[1]), lambda i: (i, 0)) for part in sums],
+        out_specs=[pl.BlockSpec((step, shape.shape[1]), lambda i: (i, 0)) for shape in shapes],
+        compiler_params=pltpu.CompilerParams(vmem_limit_bytes=VMEM_LIMIT),
+        cost_estimate=SHORT,
+        name="unpack",
+    )(*sums)
 
 
 def norm_kernel(x_ref, gain_ref, grad_ref, out, out_t, grad_t):
@@ -186,8 +208,8 @@
     )(activations, gain.astype(F32).reshape(1, -1), cotangent)
 
 
-def product_kernel(a, b, out, total):
-    part = nn(a[...], b[...])
+def product_kernel(first, a, b, out, total):
+    part = nn(a[...], b[:, first : first + out.shape[1]])
     at = pl.program_id(0)
 
     @pl.when(at == 0)
@@ -203,16 +225,16 @@
         out[...] = total[...].astype(BF16)
 
 
-def product(rows, weights, at, cols):
+def product(rows, weights, first, cols):
     length, depth = rows.shape
     step = 1024 if depth % 1024 == 0 else depth
     return pl.pallas_call(
-        product_kernel,
+        functools.partial(product_kernel, first),
         grid=(depth // step,),
         out_shape=jax.ShapeDtypeStruct((length, cols), BF16),
         in_specs=[
             pl.BlockSpec((length, step), lambda i: (0, i)),
-            pl.BlockSpec((step, cols), lambda i: (i, at)),
+            pl.BlockSpec((step, weights.shape[1]), lambda i: (i, 0)),
         ],
         out_specs=pl.BlockSpec((length, cols), lambda i: (0, 0)),
         scratch_shapes=[pltpu.VMEM((length, cols), F32)],
@@ -253,12 +275,12 @@
     out = refs[-1]
     total = None
     for mixed, side in zip(refs[:count], refs[count : 2 * count]):
-        part = nt(mixed[...], side[...])
+        part = nt(mixed[...], side[:, side.shape[1] - mixed.shape[1] :])
         total = part if total is None else total + part
     out[...] = total.astype(BF16)
 
 
-def project(mixed, sides, places):
+def project(mixed, sides):
     length, span = mixed[0].shape
     features = sides[0].shape[0]
     step = 512 if features % 512 == 0 else features
@@ -268,7 +290,7 @@
         grid=(features // step,),
         out_shape=jax.ShapeDtypeStruct((length, features), BF16),
         in_specs=[pl.BlockSpec((length, span), lambda i: (0, 0))] * count
-        + [pl.BlockSpec((step, span), lambda i, at=at: (i, at)) for at in places],
+        + [pl.BlockSpec((step, side.shape[1]), lambda i: (i, 0)) for side in sides],
         out_specs=pl.BlockSpec((length, step), lambda i: (0, i)),
         compiler_params=pltpu.CompilerParams(vmem_limit_bytes=VMEM_LIMIT),
         cost_estimate=SHORT,
@@ -323,60 +345,30 @@
     full = span + 2 * width
     order = Order()
 
-    first, second = pack(w_query, w_key, w_value, w_out)
-    first = lax.all_gather(first, "wide", axis=0, tiled=True)
-    second = lax.all_gather(second, "wide", axis=0, tiled=True)
-
-    def out_place(g):
+    pieces = pack(w_query, w_key, w_value, w_out)
+    weights = [lax.all_gather(piece, "wide", axis=0, tiled=True) for piece in pieces]
+    normed, normed_t, cotangent_t = order(normalize, activations, gain, cotangent)
+
+    mixed, sums = [], []
+    for g in range(groups):
+        qkv = order(lambda a, b: product(a, b, 0, full), normed, weights[g])
+        rows, lse = order(lambda a: attend_forward(a, members, block), qkv)
+        mixed.append(rows)
+        grad_mixed = order(lambda a, b: product(a, b, full, span), cotangent, weights[g])
+        back = order(
+            lambda a, b, c: attend_backward(a, b, c, members, block), qkv, grad_mixed, lse
+        )
+        part = order(
+            lambda *a: terms(a[:2], a[2:]), normed_t, cotangent_t, back, rows
+        )
         if g == groups - 1:
-            return second, 0
-        at = groups * full + g * span
-        if at % span:
-            return first[:, at : at + span], 0
-        return first, at // span
-
-    normed, normed_t, cotangent_t = order(normalize, activations, gain, cotangent)
-    qkv, mixed, lse, back = [], [], [], []
-
-    def backward(g):
-        weights, at = out_place(g)
-        grad_mixed = order(lambda a, b: product(a, b, at, span), cotangent, weights)
-        back.append(
-            order(
-                lambda a, b, c: attend_backward(a, b, c, members, block),
-                qkv[g],
-                grad_mixed,
-                lse[g],
+            parts = order(
+                lambda *a: project(a[:groups], a[groups:]), *mixed, *weights
             )
-        )
-
-    for g in range(groups):
-        qkv.append(order(lambda a, b: product(a, b, g, full), normed, first))
-        rows, stats = order(lambda a: attend_forward(a, members, block), qkv[g])
-        mixed.append(rows)
-        lse.append(stats)
-        if g < groups - 1:
-            backward(g)
-
-    def combined(lefts, rights):
-        count = len(lefts)
-        return order(lambda *a: terms(a[:count], a[count:]), *lefts, *rights)
-
-    def scattered(part):
-        return lax.psum_scatter(part, "wide", scatter_dimension=0, tiled=True)
-
-    early = scattered(
-        combined([cotangent_t] * groups + [normed_t] * (groups - 1), mixed + back[: groups - 1])
-    )
-    backward(groups - 1)
-    late = combined([normed_t], [back[groups - 1]])
-    places = [out_place(g) for g in range(groups)]
-    parts = order(
-        lambda *a: project(a[:groups], a[groups:], [at for _, at in places]),
-        *mixed,
-        *[weights for weights, _ in places],
-    )
-    own, arrived = narrow_sum(parts, narrow)
+            own, arrived = narrow_sum(parts, narrow)
+        if sums:
+            part = lax.optimization_barrier((sums[-1], part))[1]
+        sums.append(lax.psum_scatter(part, "wide", scatter_dimension=0, tiled=True))
 
     def finish_outputs(activations, *parts):
         share = parts[0].shape[1]
@@ -385,22 +377,7 @@
         return (result + sum(part.astype(F32) for part in parts)).astype(BF16)
 
     outputs = order(finish_outputs, activations, own, *arrived)
-    outputs, early, late = lax.optimization_barrier((outputs, early, late))
-    late = scattered(late)
-
-    grad_out = early[:, : groups * span].astype(F32)
-    sums = [
-        early[:, groups * span + g * full : groups * span + (g + 1) * full]
-        for g in range(groups - 1)
-    ] + [late]
-
-    def joined(pieces):
-        pieces = [piece.astype(F32) for piece in pieces]
-        return pieces[0] if len(pieces) == 1 else jnp.concatenate(pieces, axis=1)
-
-    grad_query = joined([s[:, :span] for s in sums])
-    grad_key = joined([s[:, span : span + width] for s in sums])
-    grad_value = joined([s[:, span + width :] for s in sums])
+    grad_query, grad_key, grad_value, grad_out = unpack(sums, span)
     return (outputs, grad_query, grad_key, grad_value, grad_out)
 
 

time: 465 us -> 445 us (0.957)
  waiting for transfers between devices: 302 us -> 279 us
  Pallas kernels: 128 us -> 139 us
    reduce_scatter x2, waiting for transfers between devices: 94.2 us -> 76.9 us  [shards(): sums.append(lax.psum_scatter(part, 'wide', scatter_dimension=0, tiled=True))]
    pallas_call x4 -> x5, Pallas kernels: 36.5 us -> 45 us  [the longest x4 40.5 us: product(): pl.pallas_call(functools.partial(product_kernel, first), grid=(depth // s...]
  transfers between devices with their start and end apart: 7 -> 7, of which waited for: 5 -> 6; matrix products, arithmetic and copies ran while one was open for 2% -> 2% of each run, Pallas kernels for 27% -> 30%
where the time goes in v2:
time: 445 us; the launch traced here: 444 us
  waiting for transfers between devices  279 us (63%)
  Pallas kernels  139 us (31%)
  between operations  13.8 us (3%)
  other arithmetic  5.05 us (1%)
    all_gather x2, waiting for transfers between devices, shards(): lax.all_gather(piece, 'wide', axis=0, tiled=True)  136 us
    reduce_scatter x2, waiting for transfers between devices, shards(): sums.append(lax.psum_scatter(part, 'wide', scatter_dimension=0, tiled=True))  76.9 us
    ppermute x3, waiting for transfers between devices, narrow_sum(): lax.ppermute(columns_of(mine), 'narrow', list(enumerate(to)))  65.2 us
    pallas_call x4, Pallas kernels, product(): pl.pallas_call(functools.partial(product_kernel, first), grid=(depth // s...  40.5 us
    pallas_call x2, Pallas kernels, terms(): pl.pallas_call(functools.partial(terms_kernel, count), grid=(features //...  30 us
    pallas_call x2, Pallas kernels, attend_backward(): pl.pallas_call(functools.partial(backward_kernel, members, block), out_sh...  17.2 us
    pallas_call x1, Pallas kernels, project(): pl.pallas_call(functools.partial(project_kernel, count), grid=(features /...  15.1 us
    pallas_call x2, Pallas kernels, attend_forward(): pl.pallas_call(functools.partial(forward_kernel, members, block), out_sha...  14.7 us
  transfers between devices with their start and end apart: 7, of which 6 were waited for; matrix products, arithmetic and copies ran while one was open for 2% of the time, Pallas kernels for 30%

profile of v2, /device:TPU:0, one launch (start us, length us, event | category | flops | bytes accessed | tf_op | source)
XLA Modules:
  0.0 444.0 jit_solution(3730721821547090020)
XLA Ops:
  7.2 0.0 all-gather.3.cloned.1.call-start
  7.2 3.3 pack.1
  10.5 0.0 copy-start
  10.5 0.0 all-gather.3.cloned.1.call-update
  10.5 0.0 all-gather.5.cloned.1.call-start
  10.6 0.7 all-gather.5.cloned.1.call-update
  11.3 0.0 reduce-scatter.3.cloned.1.call-start
  11.3 0.0 copy-done
  11.4 0.6 reshape.17
  12.0 13.4 %normalize.1 = (bf16[768,4096]{1,0:T(8,128)(2,1)}, bf16[4096,768]{1,0:T(8,128)(2,1)}, bf16[4096,768]{1,0:T(8,128)(2,1)}) custom-call(bf16[768,4096]{1,0:T(8,128)(2,1)} %x_ref.1, f32[1,4096]{1,0:T(1,128)} %bitcast.1, bf16[768,4096]{1,0:T(8,128)(2,1)} %a.1), custom_call_target="tpu_custom_call" | custom-call | flops 1 | bytes 1 | tf_op jit(solution)/shard_map/normalize/pallas_call | solution.py:199
  25.4 87.4 %all-gather.3.cloned.1.call-done.b.refs_2_ = bf16[4096,1280]{1,0:T(8,128)(2,1)} async-done(((bf16[512,1280]{1,0:T(8,128)(2,1)}), bf16[4096,1280]{1,0:T(8,128)(2,1)}) %all-gather.3.cloned.1.call-update) | async-done | bytes 10485776 | tf_op jit(solution)/shard_map/all_gather | solution.py:349
  112.8 10.7 %product.4.qkv_ref = bf16[768,768]{1,0:T(8,128)(2,1)} custom-call(bf16[768,4096]{1,0:T(8,128)(2,1)} %get-tuple-element.42.a, bf16[4096,1280]{1,0:T(8,128)(2,1)} %all-gather.3.cloned.1.call-done.b.refs_2_), custom_call_target="tpu_custom_call" | custom-call | flops 1 | bytes 1 | tf_op jit(solution)/shard_map/product/pallas_call | solution.py:231
  123.5 7.4 %attend_forward.2 = (bf16[768,512]{1,0:T(8,128)(2,1)}, f32[4,768]{1,0:T(4,128)}) custom-call(bf16[768,768]{1,0:T(8,128)(2,1)} %product.4.qkv_ref), custom_call_target="tpu_custom_call" | custom-call | flops 1 | bytes 1 | tf_op jit(solution)/shard_map/attend_forward/pallas_call | solution.py:61
  130.9 9.2 %product.5.grad_ref = bf16[768,512]{1,0:T(8,128)(2,1)} custom-call(bf16[768,4096]{1,0:T(8,128)(2,1)} %a.1, bf16[4096,1280]{1,0:T(8,128)(2,1)} %all-gather.3.cloned.1.call-done.b.refs_2_), custom_call_target="tpu_custom_call" | custom-call | flops 1 | bytes 1 | tf_op jit(solution)/shard_map/product/pallas_call | solution.py:231
  140.1 8.6 %attend_backward.2.refs_2_ = bf16[768,768]{1,0:T(8,128)(2,1)} custom-call(bf16[768,768]{1,0:T(8,128)(2,1)} %product.4.qkv_ref, bf16[768,512]{1,0:T(8,128)(2,1)} %product.5.grad_ref, f32[4,768]{1,0:T(4,128)} %get-tuple-element.40.lse_ref), custom_call_target="tpu_custom_call" | custom-call | flops 1 | bytes 1 | tf_op jit(solution)/shard_map/attend_backward/pallas_call | solution.py:106
  148.7 15.1 %terms.2 = bf16[4096,1280]{1,0:T(8,128)(2,1)} custom-call(bf16[4096,768]{1,0:T(8,128)(2,1)} %get-tuple-element.31.refs_0_, bf16[4096,768]{1,0:T(8,128)(2,1)} %get-tuple-element.32.refs_1_, bf16[768,768]{1,0:T(8,128)(2,1)} %attend_backward.2.refs_2_, bf16[768,512]{1,0:T(8,128)(2,1)} %get-tuple-element.50.refs_3_.refs_0_), custom_call_target="tpu_custom_call" | custom-call | flops 1 | bytes 1 | tf_op jit(solution)/shard_map/terms/pallas_call | solution.py:261
  163.8 0.0 reduce-scatter.3.cloned.1.call-update
  163.9 0.0 reduce-scatter.5.cloned.1.call-start
  163.9 48.9 %all-gather.5.cloned.1.call-done.b.refs_3_ = bf16[4096,1280]{1,0:T(8,128)(2,1)} async-done(((bf16[512,1280]{1,0:T(8,128)(2,1)}), bf16[4096,1280]{1,0:T(8,128)(2,1)}) %all-gather.5.cloned.1.call-update) | async-done | bytes 10485776 | tf_op jit(solution)/shard_map/all_gather | solution.py:349
  212.8 11.4 %product.6.qkv_ref = bf16[768,768]{1,0:T(8,128)(2,1)} custom-call(bf16[768,4096]{1,0:T(8,128)(2,1)} %get-tuple-element.42.a, bf16[4096,1280]{1,0:T(8,128)(2,1)} %all-gather.5.cloned.1.call-done.b.refs_3_), custom_call_target="tpu_custom_call" | custom-call | flops 1 | bytes 1 | tf_op jit(solution)/shard_map/product/pallas_call | solution.py:231
  224.2 7.3 %attend_forward.3 = (bf16[768,512]{1,0:T(8,128)(2,1)}, f32[4,768]{1,0:T(4,128)}) custom-call(bf16[768,768]{1,0:T(8,128)(2,1)} %product.6.qkv_ref), custom_call_target="tpu_custom_call" | custom-call | flops 1 | bytes 1 | tf_op jit(solution)/shard_map/attend_forward/pallas_call | solution.py:61
  231.5 9.2 %product.7.grad_ref = bf16[768,512]{1,0:T(8,128)(2,1)} custom-call(bf16[768,4096]{1,0:T(8,128)(2,1)} %a.1, bf16[4096,1280]{1,0:T(8,128)(2,1)} %all-gather.5.cloned.1.call-done.b.refs_3_), custom_call_target="tpu_custom_call" | custom-call | flops 1 | bytes 1 | tf_op jit(solution)/shard_map/product/pallas_call | solution.py:231
  240.7 8.6 %attend_backward.3.refs_2_ = bf16[768,768]{1,0:T(8,128)(2,1)} custom-call(bf16[768,768]{1,0:T(8,128)(2,1)} %product.6.qkv_ref, bf16[768,512]{1,0:T(8,128)(2,1)} %product.7.grad_ref, f32[4,768]{1,0:T(4,128)} %get-tuple-element.48.lse_ref), custom_call_target="tpu_custom_call" | custom-call | flops 1 | bytes 1 | tf_op jit(solution)/shard_map/attend_backward/pallas_call | solution.py:106
  249.3 15.0 %terms.3 = bf16[4096,1280]{1,0:T(8,128)(2,1)} custom-call(bf16[4096,768]{1,0:T(8,128)(2,1)} %get-tuple-element.31.refs_0_, bf16[4096,768]{1,0:T(8,128)(2,1)} %get-tuple-element.32.refs_1_, bf16[768,768]{1,0:T(8,128)(2,1)} %attend_backward.3.refs_2_, bf16[768,512]{1,0:T(8,128)(2,1)} %get-tuple-element.49.refs_3_.refs_1_), custom_call_target="tpu_custom_call" | custom-call | flops 1 | bytes 1 | tf_op jit(solution)/shard_map/terms/pallas_call | solution.py:261
  264.2 58.8 %reduce-scatter.3.cloned.1.call-done.refs_0_ = bf16[512,1280]{1,0:T(8,128)(2,1)} async-done(((bf16[4096,1280]{1,0:T(8,128)(2,1)}), bf16[512,1280]{1,0:T(8,128)(2,1)}) %reduce-scatter.3.cloned.1.call-update) | async-done | bytes 1310736 | tf_op jit(solution)/shard_map/reduce_scatter | solution.py:371
  323.0 0.0 reduce-scatter.5.cloned.1.call-update
  323.1 15.1 %project.1 = bf16[768,4096]{1,0:T(8,128)(2,1)} custom-call(bf16[768,512]{1,0:T(8,128)(2,1)} %get-tuple-element.50.refs_3_.refs_0_, bf16[768,512]{1,0:T(8,128)(2,1)} %get-tuple-element.49.refs_3_.refs_1_, bf16[4096,1280]{1,0:T(8,128)(2,1)} %all-gather.3.cloned.1.call-done.b.refs_2_, bf16[4096,1280]{1,0:T(8,128)(2,1)} %all-gather.5.cloned.1.call-done.b.refs_3_), custom_call_target="tpu_custom_call" | custom-call | flops 1 | bytes 1 | tf_op jit(solution)/shard_map/project/pallas_call | solution.py:288
  338.2 3.6 constant_dynamic-slice_fusion.3
  341.8 2.5 collective-permute-start.2
  344.3 0.5 collective-permute-start.1
  344.8 0.5 collective-permute-start
  345.3 34.7 %collective-permute-done.2 = bf16[768,1024]{1,0:T(8,128)(2,1)S(1)} collective-permute-done((bf16[768,1024]{1,0:T(8,128)(2,1)S(1)}, bf16[768,1024]{1,0:T(8,128)(2,1)S(1)}, u32[]{:S(2)}, u32[]{:S(2)}) %collective-permute-start.2) | collective-permute-done | bytes 1572896 | tf_op jit(solution)/shard_map/ppermute | solution.py:333
  380.1 30.4 %collective-permute-done.1 = bf16[768,1024]{1,0:T(8,128)(2,1)S(1)} collective-permute-done((bf16[768,1024]{1,0:T(8,128)(2,1)S(1)}, bf16[768,1024]{1,0:T(8,128)(2,1)S(1)}, u32[]{:S(2)}, u32[]{:S(2)}) %collective-permute-start.1) | collective-permute-done | bytes 1572896 | tf_op jit(solution)/shard_map/ppermute | solution.py:333
  410.5 0.0 collective-permute-done
  410.5 4.4 add_convert_fusion
  414.9 18.1 %reduce-scatter.5.cloned.1.call-done.refs_1_ = bf16[512,1280]{1,0:T(8,128)(2,1)} async-done(((bf16[4096,1280]{1,0:T(8,128)(2,1)}), bf16[512,1280]{1,0:T(8,128)(2,1)}) %reduce-scatter.5.cloned.1.call-update) | async-done | bytes 1310736 | tf_op jit(solution)/shard_map/reduce_scatter | solution.py:371
  433.0 4.5 %unpack.1 = (f32[512,1024]{1,0:T(8,128)}, f32[512,256]{1,0:T(8,128)}, f32[512,256]{1,0:T(8,128)}, f32[512,1024]{1,0:T(8,128)}) custom-call(bf16[512,1280]{1,0:T(8,128)(2,1)} %reduce-scatter.3.cloned.1.call-done.refs_0_, bf16[512,1280]{1,0:T(8,128)(2,1)} %reduce-scatter.5.cloned.1.call-done.refs_1_), custom_call_target="tpu_custom_call" | custom-call | flops 1 | bytes 1 | tf_op jit(solution)/shard_map/unpack/pallas_call | solution.py:164
Async XLA Ops:
  7.2 105.6 %all-gather.3.cloned.1.call-start = ((), (), s32[]{:S(2)}) async-start(), calls=%async_computation.2 | async-start | bytes 11796480 | tf_op jit(solution)/shard_map/all_gather | solution.py:349
  10.5 0.8 copy-start
  10.5 202.3 %all-gather.5.cloned.1.call-start = ((), (), s32[]{:S(2)}) async-start(), calls=%async_computation.3 | async-start | bytes 11796480 | tf_op jit(solution)/shard_map/all_gather | solution.py:349
  11.3 311.7 %reduce-scatter.3.cloned.1.call-start = ((), (), s32[]{:S(2)}) async-start(), calls=%async_computation.4 | async-start | bytes 11796480 | tf_op jit(solution)/shard_map/reduce_scatter | solution.py:371
  163.9 269.2 %reduce-scatter.5.cloned.1.call-start = ((), (), s32[]{:S(2)}) async-start(), calls=%async_computation.5 | async-start | bytes 11796480 | tf_op jit(solution)/shard_map/reduce_scatter | solution.py:371
  341.8 38.3 %collective-permute-start.2 = (bf16[768,1024]{1,0:T(8,128)(2,1)S(1)}, bf16[768,1024]{1,0:T(8,128)(2,1)S(1)}, u32[]{:S(2)}, u32[]{:S(2)}) collective-permute-start(bf16[768,1024]{1,0:T(8,128)(2,1)S(1)} %get-tuple-element.58), channel_id=1, source_target_pairs={{0,3},{1,2},{2,1},{3,0},{4,7},{5,6},{6,5},{7,4},{8,11},{9,10},{10,... | collective-permute-start | bytes 4718600 | tf_op jit(solution)/shard_map/ppermute | solution.py:333
  344.3 66.2 %collective-permute-start.1 = (bf16[768,1024]{1,0:T(8,128)(2,1)S(1)}, bf16[768,1024]{1,0:T(8,128)(2,1)S(1)}, u32[]{:S(2)}, u32[]{:S(2)}) collective-permute-start(bf16[768,1024]{1,0:T(8,128)(2,1)S(1)} %get-tuple-element.59), channel_id=1, source_target_pairs={{0,2},{1,3},{2,0},{3,1},{4,6},{5,7},{6,4},{7,5},{8,10},{9,11},{10,... | collective-permute-start | bytes 4718600 | tf_op jit(solution)/shard_map/ppermute | solution.py:333
  344.8 65.7 %collective-permute-start = (bf16[768,1024]{1,0:T(8,128)(2,1)S(1)}, bf16[768,1024]{1,0:T(8,128)(2,1)S(1)}, u32[]{:S(2)}, u32[]{:S(2)}) collective-permute-start(bf16[768,1024]{1,0:T(8,128)(2,1)S(1)} %get-tuple-element.60), channel_id=1, source_target_pairs={{0,1},{1,0},{2,3},{3,2},{4,5},{5,4},{6,7},{7,6},{8,9},{9,8},{10,11... | collective-permute-start | bytes 4718600 | tf_op jit(solution)/shard_map/ppermute | solution.py:333
Sparse Core Ops, SparseCore 0:
  10.7 102.0 all-gather.2
  115.0 97.7 all-gather.4
  215.1 107.8 reduce-scatter.2
  325.2 107.7 reduce-scatter.4

commit v3 on v2

--- a/solution.py
+++ b/solution.py
@@ -271,6 +271,31 @@
     )(*lefts, *rights)
 
 
+def side_terms_kernel(count, side, *refs):
+    terms_kernel(count, *refs)
+
+
+def side_terms(side, lefts, rights, wide):
+    features, length = lefts[0].shape
+    cols = sum(right.shape[1] for right in rights)
+    rows = features // wide
+    count = len(lefts)
+    return pl.pallas_call(
+        functools.partial(side_terms_kernel, count),
+        grid_spec=pltpu.PrefetchScalarGridSpec(
+            num_scalar_prefetch=1,
+            grid=(wide // 2,),
+            in_specs=[pl.BlockSpec((rows, length), lambda i, side: (2 * i + side[0], 0))] * count
+            + [pl.BlockSpec(right.shape, lambda i, side: (0, 0)) for right in rights],
+            out_specs=pl.BlockSpec((rows, cols), lambda i, side: (i, 0)),
+        ),
+        out_shape=jax.ShapeDtypeStruct((features // 2, cols), BF16),
+        compiler_params=pltpu.CompilerParams(vmem_limit_bytes=VMEM_LIMIT),
+        cost_estimate=SHORT,
+        name="side_terms",
+    )(side.reshape(1), *lefts, *rights)
+
+
 def project_kernel(count, *refs):
     out = refs[-1]
     total = None
@@ -318,6 +343,60 @@
         return operands[:least] + (tied,) + operands[least + 1 :]
 
 
+def take(blocks, at):
+    return lax.dynamic_index_in_dim(blocks, at, 0, keepdims=False)
+
+
+def swap_cores(array, chips):
+    return lax.ppermute(array, "wide", [(w, w ^ 1) for w in range(2 * chips)])
+
+
+class LineSum:
+    def __init__(self, order, chips):
+        self.order, self.chips = order, chips
+        self.chip = lax.axis_index("wide") // 2
+        self.arrived = ()
+        self.hops = 0
+
+    def blocks(self, array):
+        return array.reshape(self.chips, -1, array.shape[-1])
+
+    def swap(self, send):
+        self.received = self.blocks(swap_cores(send, self.chips))
+
+    def hold(self, keep):
+        self.keep = self.blocks(keep)
+
+    def advance(self):
+        self.hops += 1
+        t, chips, chip = self.hops, self.chips, self.chip
+        far = chips - t
+
+        def messages(keep, received, *arrived):
+            sums = []
+            for i, at in enumerate((jnp.minimum(chip + far, chips - 1), jnp.maximum(chip - far, 0))):
+                total = take(keep, at).astype(F32) + take(received, at).astype(F32)
+                if arrived:
+                    total = total + arrived[i].astype(F32)
+                sums.append(total.astype(BF16))
+            return tuple(sums)
+
+        up, down = self.order(messages, self.keep, self.received, *self.arrived)
+        self.arrived = (
+            lax.ppermute(up, "wide", [(w, w + 2) for w in range(2 * t)]),
+            lax.ppermute(down, "wide", [(w, w - 2) for w in range(2 * far, 2 * chips)]),
+        )
+
+    def total(self):
+        def add(keep, received, *arrived):
+            result = take(keep, self.chip).astype(F32) + take(received, self.chip).astype(F32)
+            for part in arrived:
+                result = result + part.astype(F32)
+            return result
+
+        return self.order(add, self.keep, self.received, *self.arrived)
+
+
 def narrow_sum(parts, size):
     own = lax.axis_index("narrow")
     share = parts.shape[1] // size
@@ -349,26 +428,45 @@
     weights = [lax.all_gather(piece, "wide", axis=0, tiled=True) for piece in pieces]
     normed, normed_t, cotangent_t = order(normalize, activations, gain, cotangent)
 
+    core = lax.axis_index("wide") % 2
+    chips = wide // 2
     mixed, sums = [], []
+    line = None
     for g in range(groups):
+        if line is not None and line.hops < chips - 1:
+            line.advance()
         qkv = order(lambda a, b: product(a, b, 0, full), normed, weights[g])
         rows, lse = order(lambda a: attend_forward(a, members, block), qkv)
         mixed.append(rows)
         grad_mixed = order(lambda a, b: product(a, b, full, span), cotangent, weights[g])
+        while line is not None and line.hops < chips - 1:
+            line.advance()
         back = order(
             lambda a, b, c: attend_backward(a, b, c, members, block), qkv, grad_mixed, lse
         )
-        part = order(
-            lambda *a: terms(a[:2], a[2:]), normed_t, cotangent_t, back, rows
-        )
-        if g == groups - 1:
-            parts = order(
-                lambda *a: project(a[:groups], a[groups:]), *mixed, *weights
+
+        def side(which):
+            return order(
+                lambda *a: side_terms(which, a[:2], a[2:], wide), normed_t, cotangent_t, back, rows
             )
-            own, arrived = narrow_sum(parts, narrow)
-        if sums:
-            part = lax.optimization_barrier((sums[-1], part))[1]
-        sums.append(lax.psum_scatter(part, "wide", scatter_dimension=0, tiled=True))
+
+        if g < groups - 1:
+            if line is not None:
+                sums.append(line.total())
+            line = LineSum(order, chips)
+            line.swap(side(1 - core))
+            line.hold(side(core))
+            line.advance()
+            continue
+        part = order(lambda *a: terms(a[:2], a[2:]), normed_t, cotangent_t, back, rows)
+        if line is not None:
+            part, *line.arrived = lax.optimization_barrier((part, *line.arrived))
+        last = lax.psum_scatter(part, "wide", scatter_dimension=0, tiled=True)
+        if line is not None:
+            sums.append(line.total())
+        sums.append(last)
+        parts = order(lambda *a: project(a[:groups], a[groups:]), *mixed, *weights)
+        own, arrived = narrow_sum(parts, narrow)
 
     def finish_outputs(activations, *parts):
         share = parts[0].shape[1]

time: 445 us -> 438 us (0.984); the launches traced: 444 us -> 431 us
  waiting for transfers between devices: 279 us -> 225 us
  starting transfers between devices: 3.71 us -> 24.1 us
  other arithmetic: 5.05 us -> 22.5 us
    reduce_scatter x2 -> x1, waiting for transfers between devices: 76.9 us -> 12.1 us  [shards(): last = lax.psum_scatter(part, 'wide', scatter_dimension=0, tiled=True)]
    ppermute x0 -> x7, waiting for transfers between devices: none -> 60 us  [the longest x3 55.8 us: advance(): lax.ppermute(up, 'wide', [(w, w + 2) for w in range(2 * t)])]
    all_gather x2, waiting for transfers between devices: 136 us -> 87.5 us  [shards(): lax.all_gather(piece, 'wide', axis=0, tiled=True)]
    ppermute x0 -> x7, starting transfers between devices: none -> 20.5 us  [the longest x3 15.2 us: advance(): lax.ppermute(up, 'wide', [(w, w + 2) for w in range(2 * t)])]
    pallas_call x0 -> x2, Pallas kernels: none -> 17.3 us  [side_terms(): pl.pallas_call(functools.partial(side_terms_kernel, count), grid_spec=plt...]
    pallas_call x2 -> x1, Pallas kernels: 30 us -> 15 us  [terms(): pl.pallas_call(functools.partial(terms_kernel, count), grid=(features //...]
    convert_element_type x0 -> x3, other arithmetic: none -> 13.7 us  [messages(): sums.append(total.astype(BF16))]
  transfers between devices with their start and end apart: 7 -> 13, of which waited for: 6 -> 8; matrix products, arithmetic and copies ran while one was open for 2% -> 5% of each run, Pallas kernels for 30% -> 31%
where the time goes in v3:
time: 438 us; the launch traced here: 431 us
  waiting for transfers between devices  225 us (51%)
  Pallas kernels  141 us (32%)
  starting transfers between devices  24.1 us (6%)
  other arithmetic  22.5 us (5%)
  between operations  14.1 us (3%)
    all_gather x2, waiting for transfers between devices, shards(): lax.all_gather(piece, 'wide', axis=0, tiled=True)  87.5 us
    ppermute x3, waiting for transfers between devices, narrow_sum(): lax.ppermute(columns_of(mine), 'narrow', list(enumerate(to)))  64.8 us
    ppermute x3, waiting for transfers between devices, advance(): lax.ppermute(up, 'wide', [(w, w + 2) for w in range(2 * t)])  55.8 us
    pallas_call x4, Pallas kernels, product(): pl.pallas_call(functools.partial(product_kernel, first), grid=(depth // s...  40.2 us
    pallas_call x2, Pallas kernels, side_terms(): pl.pallas_call(functools.partial(side_terms_kernel, count), grid_spec=plt...  17.3 us
    pallas_call x2, Pallas kernels, attend_backward(): pl.pallas_call(functools.partial(backward_kernel, members, block), out_sh...  17.2 us
    pallas_call x1, Pallas kernels, project(): pl.pallas_call(functools.partial(project_kernel, count), grid=(features /...  15.5 us
    ppermute x3, starting transfers between devices, advance(): lax.ppermute(up, 'wide', [(w, w + 2) for w in range(2 * t)])  15.2 us
  transfers between devices with their start and end apart: 13, of which 8 were waited for; matrix products, arithmetic and copies ran while one was open for 5% of the time, Pallas kernels for 31%

profile of v3, /device:TPU:0, one launch (start us, length us, event | category | flops | bytes accessed | tf_op | source)
XLA Modules:
  0.0 430.9 jit_solution(7792728241458722815)
XLA Ops:
  7.2 0.0 copy-start
  7.2 0.0 all-gather.3.cloned.1.call-start
  7.2 3.3 pack.1
  10.5 0.0 all-gather.3.cloned.1.call-update
  10.6 0.0 all-gather.5.cloned.1.call-start
  10.6 0.7 all-gather.5.cloned.1.call-update
  11.3 0.0 reduce-scatter.2.cloned.1.call-start
  11.4 0.0 copy-done
  11.4 0.6 reshape.56
  12.0 13.3 %normalize.1 = (bf16[768,4096]{1,0:T(8,128)(2,1)}, bf16[4096,768]{1,0:T(8,128)(2,1)}, bf16[4096,768]{1,0:T(8,128)(2,1)}) custom-call(bf16[768,4096]{1,0:T(8,128)(2,1)} %x_ref.1, f32[1,4096]{1,0:T(1,128)} %bitcast.33, bf16[768,4096]{1,0:T(8,128)(2,1)} %a.1), custom_call_target="tpu_custom_call" | custom-call | flops 1 | bytes 1 | tf_op jit(solution)/shard_map/normalize/pallas_call | solution.py:199
  25.3 87.5 %all-gather.3.cloned.1.call-done.b.refs_2_ = bf16[4096,1280]{1,0:T(8,128)(2,1)} async-done(((bf16[512,1280]{1,0:T(8,128)(2,1)}), bf16[4096,1280]{1,0:T(8,128)(2,1)}) %all-gather.3.cloned.1.call-update) | async-done | bytes 10485776 | tf_op jit(solution)/shard_map/all_gather | solution.py:428
  112.8 10.7 %product.4.qkv_ref = bf16[768,768]{1,0:T(8,128)(2,1)} custom-call(bf16[768,4096]{1,0:T(8,128)(2,1)} %get-tuple-element.61.a, bf16[4096,1280]{1,0:T(8,128)(2,1)} %all-gather.3.cloned.1.call-done.b.refs_2_), custom_call_target="tpu_custom_call" | custom-call | flops 1 | bytes 1 | tf_op jit(solution)/shard_map/product/pallas_call | solution.py:231
  123.5 7.4 %attend_forward.2 = (bf16[768,512]{1,0:T(8,128)(2,1)}, f32[4,768]{1,0:T(4,128)}) custom-call(bf16[768,768]{1,0:T(8,128)(2,1)} %product.4.qkv_ref), custom_call_target="tpu_custom_call" | custom-call | flops 1 | bytes 1 | tf_op jit(solution)/shard_map/attend_forward/pallas_call | solution.py:61
  130.9 9.7 %product.5.grad_ref = bf16[768,512]{1,0:T(8,128)(2,1)} custom-call(bf16[768,4096]{1,0:T(8,128)(2,1)} %a.1, bf16[4096,1280]{1,0:T(8,128)(2,1)} %all-gather.3.cloned.1.call-done.b.refs_2_), custom_call_target="tpu_custom_call" | custom-call | flops 1 | bytes 1 | tf_op jit(solution)/shard_map/product/pallas_call | solution.py:231
  140.7 8.6 %attend_backward.2.refs_2_ = bf16[768,768]{1,0:T(8,128)(2,1)} custom-call(bf16[768,768]{1,0:T(8,128)(2,1)} %product.4.qkv_ref, bf16[768,512]{1,0:T(8,128)(2,1)} %product.5.grad_ref, f32[4,768]{1,0:T(4,128)} %get-tuple-element.53.lse_ref), custom_call_target="tpu_custom_call" | custom-call | flops 1 | bytes 1 | tf_op jit(solution)/shard_map/attend_backward/pallas_call | solution.py:106
  149.3 8.7 %side_terms.2 = bf16[2048,1280]{1,0:T(8,128)(2,1)} custom-call(s32[1]{0:T(128)} %bitcast.2.side, bf16[4096,768]{1,0:T(8,128)(2,1)} %get-tuple-element.44.refs_0_, bf16[4096,768]{1,0:T(8,128)(2,1)} %get-tuple-element.45.refs_1_, bf16[768,768]{1,0:T(8,128)(2,1)} %attend_backward.2.refs_2_, bf16[768,512]{1,0:T(8,128)(2,1)} %get-tuple-element.76.refs_3_.refs_0_), custom_call_target="tpu_custom_call" | custom-call | flops 1 | bytes 1 | tf_op jit(solution)/shard_map/side_terms/pallas_call | solution.py:283
  157.9 0.3 collective-permute-start
  158.2 8.6 %side_terms.3 = bf16[2048,1280]{1,0:T(8,128)(2,1)} custom-call(s32[1]{0:T(128)} %bitcast.side, bf16[4096,768]{1,0:T(8,128)(2,1)} %get-tuple-element.44.refs_0_, bf16[4096,768]{1,0:T(8,128)(2,1)} %get-tuple-element.45.refs_1_, bf16[768,768]{1,0:T(8,128)(2,1)} %attend_backward.2.refs_2_, bf16[768,512]{1,0:T(8,128)(2,1)} %get-tuple-element.76.refs_3_.refs_0_), custom_call_target="tpu_custom_call" | custom-call | flops 1 | bytes 1 | tf_op jit(solution)/shard_map/side_terms/pallas_call | solution.py:283
  166.8 0.1 collective-permute-done
  166.9 3.1 fusion.6
  170.1 2.4 collective-permute-start.1
  172.4 1.7 collective-permute-start.2
  174.2 54.3 %collective-permute-done.1 = bf16[512,1280]{1,0:T(8,128)(2,1)} collective-permute-done((bf16[512,1280]{1,0:T(8,128)(2,1)S(1)}, bf16[512,1280]{1,0:T(8,128)(2,1)}, u32[]{:S(2)}, u32[]{:S(2)}) %collective-permute-start.1) | collective-permute-done | bytes 1310752 | tf_op jit(solution)/shard_map/ppermute | solution.py:386
  228.4 0.0 collective-permute-done.2
  228.4 5.3 %fusion.2 = (bf16[512,1280]{1,0:T(8,128)(2,1)S(1)}, bf16[512,1280]{1,0:T(8,128)(2,1)}) fusion(bf16[512,1280]{1,0:T(8,128)(2,1)} %collective-permute-done.2, bf16[4,512,1280]{2,1,0:T(8,128)(2,1)} %bitcast.4, s32[]{:T(128)S(6)} %max.10, bf16[4,512,1280]{2,1,0:T(8,128)(2,1)} %bitcast.30, bf16[512,1280]{1,0:T(8,128)(2,1)} %collective-permute-done.1, s32[]{:T(128)S(6)} %select_n.51), kind=kLoop, calls=%fused_computation.6 | loop fusion | flops 7864320 | bytes 10485768 | tf_op jit(solution)/shard_map/convert_element_type | solution.py:381
  233.7 4.6 %collective-permute-start.3 = (bf16[512,1280]{1,0:T(8,128)(2,1)}, bf16[512,1280]{1,0:T(8,128)(2,1)S(1)}, u32[]{:S(2)}, u32[]{:S(2)}) collective-permute-start(bf16[512,1280]{1,0:T(8,128)(2,1)} %get-tuple-element.60), channel_id=1, source_target_pairs={{0,8},{4,12},{8,16},{12,20},{1,9},{5,13},{9,17},{13,21},{2,10},{6,... | collective-permute-start | bytes 3932168 | tf_op jit(solution)/shard_map/ppermute | solution.py:386
  238.3 1.7 collective-permute-start.4
  240.0 0.0 all-gather.5.cloned.1.call-done.b.refs_3_
  240.0 10.6 %product.6.qkv_ref = bf16[768,768]{1,0:T(8,128)(2,1)} custom-call(bf16[768,4096]{1,0:T(8,128)(2,1)} %get-tuple-element.61.a, bf16[4096,1280]{1,0:T(8,128)(2,1)} %all-gather.5.cloned.1.call-done.b.refs_3_), custom_call_target="tpu_custom_call" | custom-call | flops 1 | bytes 1 | tf_op jit(solution)/shard_map/product/pallas_call | solution.py:231
  250.7 7.3 %attend_forward.3 = (bf16[768,512]{1,0:T(8,128)(2,1)}, f32[4,768]{1,0:T(4,128)}) custom-call(bf16[768,768]{1,0:T(8,128)(2,1)} %product.6.qkv_ref), custom_call_target="tpu_custom_call" | custom-call | flops 1 | bytes 1 | tf_op jit(solution)/shard_map/attend_forward/pallas_call | solution.py:61
  258.0 9.1 %product.7.grad_ref = bf16[768,512]{1,0:T(8,128)(2,1)} custom-call(bf16[768,4096]{1,0:T(8,128)(2,1)} %a.1, bf16[4096,1280]{1,0:T(8,128)(2,1)} %all-gather.5.cloned.1.call-done.b.refs_3_), custom_call_target="tpu_custom_call" | custom-call | flops 1 | bytes 1 | tf_op jit(solution)/shard_map/product/pallas_call | solution.py:231
  267.1 0.0 collective-permute-done.3
  267.1 0.0 collective-permute-done.4
  267.1 5.3 %fusion = (bf16[512,1280]{1,0:T(8,128)(2,1)}, bf16[512,1280]{1,0:T(8,128)(2,1)}) fusion(bf16[512,1280]{1,0:T(8,128)(2,1)} %collective-permute-done.4, bf16[4,512,1280]{2,1,0:T(8,128)(2,1)} %bitcast.4, s32[]{:T(128)S(6)} %max.11, bf16[4,512,1280]{2,1,0:T(8,128)(2,1)} %bitcast.31, bf16[512,1280]{1,0:T(8,128)(2,1)S(1)} %collective-permute-done.3, s32[]{:T(128)S(6)} %select_n.53), kind=kLoop, calls=%fused_computation.2 | loop fusion | flops 7864320 | bytes 10485768 | tf_op jit(solution)/shard_map/convert_element_type | solution.py:381
  272.5 8.3 %collective-permute-start.5 = (bf16[512,1280]{1,0:T(8,128)(2,1)}, bf16[512,1280]{1,0:T(8,128)(2,1)S(1)}, u32[]{:S(2)}, u32[]{:S(2)}) collective-permute-start(bf16[512,1280]{1,0:T(8,128)(2,1)} %get-tuple-element.68), channel_id=1, source_target_pairs={{0,8},{4,12},{8,16},{12,20},{16,24},{20,28},{1,9},{5,13},{9,17},{1... | collective-permute-start | bytes 3932168 | tf_op jit(solution)/shard_map/ppermute | solution.py:386
  280.7 1.5 collective-permute-start.6
  282.2 8.6 %attend_backward.3.refs_2_ = bf16[768,768]{1,0:T(8,128)(2,1)} custom-call(bf16[768,768]{1,0:T(8,128)(2,1)} %product.6.qkv_ref, bf16[768,512]{1,0:T(8,128)(2,1)} %product.7.grad_ref, f32[4,768]{1,0:T(4,128)} %get-tuple-element.70.lse_ref), custom_call_target="tpu_custom_call" | custom-call | flops 1 | bytes 1 | tf_op jit(solution)/shard_map/attend_backward/pallas_call | solution.py:106
  290.9 15.0 %terms.1 = bf16[4096,1280]{1,0:T(8,128)(2,1)} custom-call(bf16[4096,768]{1,0:T(8,128)(2,1)} %get-tuple-element.44.refs_0_, bf16[4096,768]{1,0:T(8,128)(2,1)} %get-tuple-element.45.refs_1_, bf16[768,768]{1,0:T(8,128)(2,1)} %attend_backward.3.refs_2_, bf16[768,512]{1,0:T(8,128)(2,1)} %get-tuple-element.71.refs_3_.refs_1_), custom_call_target="tpu_custom_call" | custom-call | flops 1 | bytes 1 | tf_op jit(solution)/shard_map/terms/pallas_call | solution.py:261
  305.8 1.6 collective-permute-done.5
  307.4 4.1 collective-permute-done.6
  311.5 0.0 reduce-scatter.2.cloned.1.call-update
  311.5 3.8 fusion.4.refs_0_
  315.3 15.5 %project.1 = bf16[768,4096]{1,0:T(8,128)(2,1)} custom-call(bf16[768,512]{1,0:T(8,128)(2,1)} %get-tuple-element.76.refs_3_.refs_0_, bf16[768,512]{1,0:T(8,128)(2,1)} %get-tuple-element.71.refs_3_.refs_1_, bf16[4096,1280]{1,0:T(8,128)(2,1)} %all-gather.3.cloned.1.call-done.b.refs_2_, bf16[4096,1280]{1,0:T(8,128)(2,1)} %all-gather.5.cloned.1.call-done.b.refs_3_), custom_call_target="tpu_custom_call" | custom-call | flops 1 | bytes 1 | tf_op jit(solution)/shard_map/project/pallas_call | solution.py:313
  330.8 3.6 constant_dynamic-slice_fusion.3
  334.5 1.8 collective-permute-start.7
  336.3 1.5 collective-permute-start.8
  337.8 0.2 collective-permute-start.9
  338.0 33.8 %collective-permute-done.7 = bf16[768,1024]{1,0:T(8,128)(2,1)S(1)} collective-permute-done((bf16[768,1024]{1,0:T(8,128)(2,1)S(1)}, bf16[768,1024]{1,0:T(8,128)(2,1)S(1)}, u32[]{:S(2)}, u32[]{:S(2)}) %collective-permute-start.7) | collective-permute-done | bytes 1572896 | tf_op jit(solution)/shard_map/ppermute | solution.py:412
  371.9 30.9 %collective-permute-done.8 = bf16[768,1024]{1,0:T(8,128)(2,1)S(1)} collective-permute-done((bf16[768,1024]{1,0:T(8,128)(2,1)S(1)}, bf16[768,1024]{1,0:T(8,128)(2,1)S(1)}, u32[]{:S(2)}, u32[]{:S(2)}) %collective-permute-start.8) | collective-permute-done | bytes 1572896 | tf_op jit(solution)/shard_map/ppermute | solution.py:412
  402.8 0.0 collective-permute-done.9
  402.8 4.4 %add_convert_fusion = bf16[768,1024]{1,0:T(8,128)(2,1)} fusion(bf16[768,1024]{1,0:T(8,128)(2,1)S(1)} %collective-permute-done.9, bf16[768,1024]{1,0:T(8,128)(2,1)S(1)} %collective-permute-done.8, bf16[768,1024]{1,0:T(8,128)(2,1)S(1)} %collective-permute-done.7, bf16[768,1024]{1,0:T(8,128)(2,1)S(1)} %get-tuple-element.77, bf16[768,4096]{1,0:T(8,128)(2,1)} %x_ref.1, ...), kind=kLoop, calls=%fused_computation | loop fusion | flops 7864320 | bytes 9437188 | tf_op jit(solution)/shard_map/convert_element_type | solution.py:475
  407.2 12.1 %reduce-scatter.2.cloned.1.call-done.refs_1_ = bf16[512,1280]{1,0:T(8,128)(2,1)} async-done(((bf16[4096,1280]{1,0:T(8,128)(2,1)}), bf16[512,1280]{1,0:T(8,128)(2,1)}) %reduce-scatter.2.cloned.1.call-update) | async-done | bytes 1310736 | tf_op jit(solution)/shard_map/reduce_scatter | solution.py:464
  419.3 4.8 %unpack.1 = (f32[512,1024]{1,0:T(8,128)}, f32[512,256]{1,0:T(8,128)}, f32[512,256]{1,0:T(8,128)}, f32[512,1024]{1,0:T(8,128)}) custom-call(f32[512,1280]{1,0:T(8,128)} %fusion.4.refs_0_, bf16[512,1280]{1,0:T(8,128)(2,1)} %reduce-scatter.2.cloned.1.call-done.refs_1_), custom_call_target="tpu_custom_call" | custom-call | flops 1 | bytes 1 | tf_op jit(solution)/shard_map/unpack/pallas_call | solution.py:164
Async XLA Ops:
  7.2 4.2 copy-start
  7.2 105.6 %all-gather.3.cloned.1.call-start = ((), (), s32[]{:S(2)}) async-start(), calls=%async_computation.1 | async-start | bytes 11796480 | tf_op jit(solution)/shard_map/all_gather | solution.py:428
  10.6 229.5 %all-gather.5.cloned.1.call-start = ((), (), s32[]{:S(2)}) async-start(), calls=%async_computation.2 | async-start | bytes 11796480 | tf_op jit(solution)/shard_map/all_gather | solution.py:428
  11.3 408.0 %reduce-scatter.2.cloned.1.call-start = ((), (), s32[]{:S(2)}) async-start(), calls=%async_computation.3 | async-start | bytes 11796480 | tf_op jit(solution)/shard_map/reduce_scatter | solution.py:464
  157.9 9.0 %collective-permute-start = (bf16[2048,1280]{1,0:T(8,128)(2,1)}, bf16[2048,1280]{1,0:T(8,128)(2,1)}, u32[]{:S(2)}, u32[]{:S(2)}) collective-permute-start(bf16[2048,1280]{1,0:T(8,128)(2,1)} %side_terms.2), channel_id=1, source_target_pairs={{0,4},{4,0},{8,12},{12,8},{16,20},{20,16},{24,28},{28,24},{1,5},{5... | collective-permute-start | bytes 15728648 | tf_op jit(solution)/shard_map/ppermute | solution.py:351
  170.1 58.4 %collective-permute-start.1 = (bf16[512,1280]{1,0:T(8,128)(2,1)S(1)}, bf16[512,1280]{1,0:T(8,128)(2,1)}, u32[]{:S(2)}, u32[]{:S(2)}) collective-permute-start(bf16[512,1280]{1,0:T(8,128)(2,1)S(1)} %get-tuple-element.57), channel_id=1, source_target_pairs={{0,8},{4,12},{1,9},{5,13},{2,10},{6,14},{3,11},{7,15}} | collective-permute-start | bytes 3932168 | tf_op jit(solution)/shard_map/ppermute | solution.py:386
  172.4 56.0 %collective-permute-start.2 = (bf16[512,1280]{1,0:T(8,128)(2,1)S(1)}, bf16[512,1280]{1,0:T(8,128)(2,1)}, u32[]{:S(2)}, u32[]{:S(2)}) collective-permute-start(bf16[512,1280]{1,0:T(8,128)(2,1)S(1)} %get-tuple-element.59), channel_id=1, source_target_pairs={{24,16},{28,20},{25,17},{29,21},{26,18},{30,22},{27,19},{31,23}} | collective-permute-start | bytes 3932168 | tf_op jit(solution)/shard_map/ppermute | solution.py:387
  233.7 33.4 %collective-permute-start.3 = (bf16[512,1280]{1,0:T(8,128)(2,1)}, bf16[512,1280]{1,0:T(8,128)(2,1)S(1)}, u32[]{:S(2)}, u32[]{:S(2)}) collective-permute-start(bf16[512,1280]{1,0:T(8,128)(2,1)} %get-tuple-element.60), channel_id=1, source_target_pairs={{0,8},{4,12},{8,16},{12,20},{1,9},{5,13},{9,17},{13,21},{2,10},{6,... | collective-permute-start | bytes 3932168 | tf_op jit(solution)/shard_map/ppermute | solution.py:386
  238.3 28.8 %collective-permute-start.4 = (bf16[512,1280]{1,0:T(8,128)(2,1)S(1)}, bf16[512,1280]{1,0:T(8,128)(2,1)}, u32[]{:S(2)}, u32[]{:S(2)}) collective-permute-start(bf16[512,1280]{1,0:T(8,128)(2,1)S(1)} %get-tuple-element.67), channel_id=1, source_target_pairs={{16,8},{20,12},{24,16},{28,20},{17,9},{21,13},{25,17},{29,21},{18,... | collective-permute-start | bytes 3932168 | tf_op jit(solution)/shard_map/ppermute | solution.py:387
  272.5 34.9 %collective-permute-start.5 = (bf16[512,1280]{1,0:T(8,128)(2,1)}, bf16[512,1280]{1,0:T(8,128)(2,1)S(1)}, u32[]{:S(2)}, u32[]{:S(2)}) collective-permute-start(bf16[512,1280]{1,0:T(8,128)(2,1)} %get-tuple-element.68), channel_id=1, source_target_pairs={{0,8},{4,12},{8,16},{12,20},{16,24},{20,28},{1,9},{5,13},{9,17},{1... | collective-permute-start | bytes 3932168 | tf_op jit(solution)/shard_map/ppermute | solution.py:386
  280.7 30.7 %collective-permute-start.6 = (bf16[512,1280]{1,0:T(8,128)(2,1)}, bf16[512,1280]{1,0:T(8,128)(2,1)S(1)}, u32[]{:S(2)}, u32[]{:S(2)}) collective-permute-start(bf16[512,1280]{1,0:T(8,128)(2,1)} %get-tuple-element.72), channel_id=1, source_target_pairs={{8,0},{12,4},{16,8},{20,12},{24,16},{28,20},{9,1},{13,5},{17,9},{2... | collective-permute-start | bytes 3932168 | tf_op jit(solution)/shard_map/ppermute | solution.py:387
  334.5 37.4 %collective-permute-start.7 = (bf16[768,1024]{1,0:T(8,128)(2,1)S(1)}, bf16[768,1024]{1,0:T(8,128)(2,1)S(1)}, u32[]{:S(2)}, u32[]{:S(2)}) collective-permute-start(bf16[768,1024]{1,0:T(8,128)(2,1)S(1)} %get-tuple-element.92), channel_id=1, source_target_pairs={{0,1},{1,0},{2,3},{3,2},{4,5},{5,4},{6,7},{7,6},{8,9},{9,8},{10,11... | collective-permute-start | bytes 4718600 | tf_op jit(solution)/shard_map/ppermute | solution.py:412
  336.3 66.5 %collective-permute-start.8 = (bf16[768,1024]{1,0:T(8,128)(2,1)S(1)}, bf16[768,1024]{1,0:T(8,128)(2,1)S(1)}, u32[]{:S(2)}, u32[]{:S(2)}) collective-permute-start(bf16[768,1024]{1,0:T(8,128)(2,1)S(1)} %get-tuple-element.91), channel_id=1, source_target_pairs={{0,2},{1,3},{2,0},{3,1},{4,6},{5,7},{6,4},{7,5},{8,10},{9,11},{10,... | collective-permute-start | bytes 4718600 | tf_op jit(solution)/shard_map/ppermute | solution.py:412
  337.8 65.0 %collective-permute-start.9 = (bf16[768,1024]{1,0:T(8,128)(2,1)S(1)}, bf16[768,1024]{1,0:T(8,128)(2,1)S(1)}, u32[]{:S(2)}, u32[]{:S(2)}) collective-permute-start(bf16[768,1024]{1,0:T(8,128)(2,1)S(1)} %get-tuple-element.90), channel_id=1, source_target_pairs={{0,3},{1,2},{2,1},{3,0},{4,7},{5,6},{6,5},{7,4},{8,11},{9,10},{10,... | collective-permute-start | bytes 4718600 | tf_op jit(solution)/shard_map/ppermute | solution.py:412
Sparse Core Ops, SparseCore 0:
  10.7 102.0 all-gather.2
  115.0 120.2 all-gather.4
  311.6 107.6 reduce-scatter.1

commit v4 on v3

--- a/solution.py
+++ b/solution.py
@@ -12,7 +12,7 @@
 MASKED = -1e30
 F32 = jnp.float32
 BF16 = jnp.bfloat16
-VMEM_LIMIT = 60 * 2**20
+VMEM_LIMIT = 51 * 2**20
 SHORT = pl.CostEstimate(flops=1, bytes_accessed=1, transcendentals=0)
 
 
@@ -134,7 +134,7 @@
     return pl.pallas_call(
         functools.partial(pack_kernel, groups),
         out_shape=(jax.ShapeDtypeStruct((rows, wide), BF16),) * groups,
-        compiler_params=pltpu.CompilerParams(vmem_limit_bytes=VMEM_LIMIT),
+        compiler_params=pltpu.CompilerParams(vmem_limit_bytes=60 * 2**20),
         cost_estimate=SHORT,
         name="pack",
     )(query, key, value, out)
@@ -208,36 +208,22 @@
     )(activations, gain.astype(F32).reshape(1, -1), cotangent)
 
 
-def product_kernel(first, a, b, out, total):
-    part = nn(a[...], b[:, first : first + out.shape[1]])
-    at = pl.program_id(0)
-
-    @pl.when(at == 0)
-    def _():
-        total[...] = part
-
-    @pl.when(at > 0)
-    def _():
-        total[...] += part
-
-    @pl.when(at == pl.num_programs(0) - 1)
-    def _():
-        out[...] = total[...].astype(BF16)
+def product_kernel(a, b, out):
+    out[...] = nn(a[...], b[...]).astype(BF16)
 
 
 def product(rows, weights, first, cols):
     length, depth = rows.shape
-    step = 1024 if depth % 1024 == 0 else depth
-    return pl.pallas_call(
-        functools.partial(product_kernel, first),
-        grid=(depth // step,),
+    step = 256 if first % 256 == 0 and cols % 256 == 0 else HEAD_DIM
+    return pl.pallas_call(
+        product_kernel,
+        grid=(cols // step,),
         out_shape=jax.ShapeDtypeStruct((length, cols), BF16),
         in_specs=[
-            pl.BlockSpec((length, step), lambda i: (0, i)),
-            pl.BlockSpec((step, weights.shape[1]), lambda i: (i, 0)),
+            pl.BlockSpec((length, depth), lambda i: (0, 0)),
+            pl.BlockSpec((depth, step), lambda i: (0, i + first // step)),
         ],
-        out_specs=pl.BlockSpec((length, cols), lambda i: (0, 0)),
-        scratch_shapes=[pltpu.VMEM((length, cols), F32)],
+        out_specs=pl.BlockSpec((length, step), lambda i: (0, i)),
         compiler_params=pltpu.CompilerParams(vmem_limit_bytes=VMEM_LIMIT),
         cost_estimate=SHORT,
         name="product",
@@ -256,7 +242,7 @@
 def terms(lefts, rights):
     features, length = lefts[0].shape
     cols = sum(right.shape[1] for right in rights)
-    step = 512 if features % 512 == 0 else features
+    step = 1024 if features % 1024 == 0 else features
     count = len(lefts)
     return pl.pallas_call(
         functools.partial(terms_kernel, count),

time: 438 us -> 434 us (level)
  Pallas kernels: 141 us -> 123 us
  waiting for transfers between devices: 225 us -> 242 us
    pallas_call x4, Pallas kernels: 40.2 us -> 32.5 us  [product(): pl.pallas_call(product_kernel, grid=(cols // step,), out_shape=jax.ShapeD...]
    all_gather x2, waiting for transfers between devices: 87.5 us -> 95.1 us  [shards(): lax.all_gather(piece, 'wide', axis=0, tiled=True)]
    ppermute x3, waiting for transfers between devices: 55.8 us -> 62.7 us  [advance(): lax.ppermute(up, 'wide', [(w, w + 2) for w in range(2 * t)])]
    pallas_call x2, Pallas kernels: 14.8 us -> 10.3 us  [attend_forward(): pl.pallas_call(functools.partial(forward_kernel, members, block), out_sha...]
  transfers between devices with their start and end apart: 13 -> 13, of which waited for: 8 -> 10; matrix products, arithmetic and copies ran while one was open for 5% -> 5% of each run, Pallas kernels for 31% -> 27%
where the time goes in v4:
time: 434 us; the launch traced here: 428 us
  waiting for transfers between devices  242 us (56%)
  Pallas kernels  123 us (28%)
  other arithmetic  22 us (5%)
  starting transfers between devices  21.3 us (5%)
  between operations  14.4 us (3%)
  local copies, waits for them, and re-layouts  5.01 us (1%)
    all_gather x2, waiting for transfers between devices, shards(): lax.all_gather(piece, 'wide', axis=0, tiled=True)  95.1 us
    ppermute x3, waiting for transfers between devices, narrow_sum(): lax.ppermute(columns_of(mine), 'narrow', list(enumerate(to)))  66.4 us
    ppermute x3, waiting for transfers between devices, advance(): lax.ppermute(up, 'wide', [(w, w + 2) for w in range(2 * t)])  62.7 us
    pallas_call x4, Pallas kernels, product(): pl.pallas_call(product_kernel, grid=(cols // step,), out_shape=jax.ShapeD...  32.5 us
    pallas_call x2, Pallas kernels, side_terms(): pl.pallas_call(functools.partial(side_terms_kernel, count), grid_spec=plt...  16.1 us
    pallas_call x1, Pallas kernels, project(): pl.pallas_call(functools.partial(project_kernel, count), grid=(features /...  15 us
    pallas_call x2, Pallas kernels, attend_backward(): pl.pallas_call(functools.partial(backward_kernel, members, block), out_sh...  14.7 us
    convert_element_type x3, other arithmetic, messages(): sums.append(total.astype(BF16))  13.4 us
  transfers between devices with their start and end apart: 13, of which 10 were waited for; matrix products, arithmetic and copies ran while one was open for 5% of the time, Pallas kernels for 27%

profile of v4, /device:TPU:0, one launch (start us, length us, event | category | flops | bytes accessed | tf_op | source)
XLA Modules:
  0.0 427.6 jit_solution(18127291393841392584)
XLA Ops:
  7.2 0.0 copy-start.3
  7.2 0.0 all-gather.3.cloned.1.call-start
  7.2 3.3 pack.1
  10.5 0.0 all-gather.3.cloned.1.call-update
  10.6 0.0 all-gather.5.cloned.1.call-start
  10.6 0.7 all-gather.5.cloned.1.call-update
  11.3 0.0 reduce-scatter.2.cloned.1.call-start
  11.4 0.0 copy-done.3
  11.4 13.4 %normalize.1 = (bf16[768,4096]{1,0:T(8,128)(2,1)}, bf16[4096,768]{1,0:T(8,128)(2,1)}, bf16[4096,768]{1,0:T(8,128)(2,1)}) custom-call(bf16[768,4096]{1,0:T(8,128)(2,1)} %x_ref.1, f32[1,4096]{1,0:T(1,128)S(1)} %bitcast.29, bf16[768,4096]{1,0:T(8,128)(2,1)} %a.1), custom_call_target="tpu_custom_call" | custom-call | flops 1 | bytes 1 | tf_op jit(solution)/shard_map/normalize/pallas_call | solution.py:199
  24.8 88.0 %all-gather.3.cloned.1.call-done.b.refs_2_ = bf16[4096,1280]{1,0:T(8,128)(2,1)} async-done(((bf16[512,1280]{1,0:T(8,128)(2,1)}), bf16[4096,1280]{1,0:T(8,128)(2,1)}) %all-gather.3.cloned.1.call-update) | async-done | bytes 10485776 | tf_op jit(solution)/shard_map/all_gather | solution.py:414
  112.8 8.9 %product.4.qkv_ref = bf16[768,768]{1,0:T(8,128)(2,1)S(1)} custom-call(bf16[768,4096]{1,0:T(8,128)(2,1)} %get-tuple-element.61.a, bf16[4096,1280]{1,0:T(8,128)(2,1)} %all-gather.3.cloned.1.call-done.b.refs_2_), custom_call_target="tpu_custom_call" | custom-call | flops 1 | bytes 1 | tf_op jit(solution)/shard_map/product/pallas_call | solution.py:218
  121.7 0.0 copy-start.1
  121.7 5.2 %attend_forward.2 = (bf16[768,512]{1,0:T(8,128)(2,1)S(1)}, f32[4,768]{1,0:T(4,128)S(1)}) custom-call(bf16[768,768]{1,0:T(8,128)(2,1)S(1)} %product.4.qkv_ref), custom_call_target="tpu_custom_call" | custom-call | flops 1 | bytes 1 | tf_op jit(solution)/shard_map/attend_forward/pallas_call | solution.py:61
  126.9 7.3 %product.5.grad_ref = bf16[768,512]{1,0:T(8,128)(2,1)S(1)} custom-call(bf16[768,4096]{1,0:T(8,128)(2,1)} %a.1, bf16[4096,1280]{1,0:T(8,128)(2,1)} %all-gather.3.cloned.1.call-done.b.refs_2_), custom_call_target="tpu_custom_call" | custom-call | flops 1 | bytes 1 | tf_op jit(solution)/shard_map/product/pallas_call | solution.py:218
  134.2 0.0 copy-done.1
  134.2 7.4 %attend_backward.2.refs_2_ = bf16[768,768]{1,0:T(8,128)(2,1)S(1)} custom-call(bf16[768,768]{1,0:T(8,128)(2,1)} %copy-done.1, bf16[768,512]{1,0:T(8,128)(2,1)S(1)} %product.5.grad_ref, f32[4,768]{1,0:T(4,128)S(1)} %get-tuple-element.53.lse_ref), custom_call_target="tpu_custom_call" | custom-call | flops 1 | bytes 1 | tf_op jit(solution)/shard_map/attend_backward/pallas_call | solution.py:106
  141.6 8.1 %side_terms.2 = bf16[2048,1280]{1,0:T(8,128)(2,1)} custom-call(s32[1]{0:T(128)} %bitcast.2.side, bf16[4096,768]{1,0:T(8,128)(2,1)} %get-tuple-element.44.refs_0_, bf16[4096,768]{1,0:T(8,128)(2,1)} %get-tuple-element.45.refs_1_, bf16[768,768]{1,0:T(8,128)(2,1)S(1)} %attend_backward.2.refs_2_, bf16[768,512]{1,0:T(8,128)(2,1)S(1)} %get-tuple-element.76.refs_3_.refs_0_), custom_call_target="tpu_custom_call" | custom-call | flops 1 | bytes 1 | tf_op jit(solution)/shard_map/side_terms/pallas_call | solution.py:269
  149.7 0.3 collective-permute-start
  149.9 8.1 %side_terms.3 = bf16[2048,1280]{1,0:T(8,128)(2,1)} custom-call(s32[1]{0:T(128)} %bitcast.side, bf16[4096,768]{1,0:T(8,128)(2,1)} %get-tuple-element.44.refs_0_, bf16[4096,768]{1,0:T(8,128)(2,1)} %get-tuple-element.45.refs_1_, bf16[768,768]{1,0:T(8,128)(2,1)S(1)} %attend_backward.2.refs_2_, bf16[768,512]{1,0:T(8,128)(2,1)S(1)} %get-tuple-element.76.refs_3_.refs_0_), custom_call_target="tpu_custom_call" | custom-call | flops 1 | bytes 1 | tf_op jit(solution)/shard_map/side_terms/pallas_call | solution.py:269
  158.0 0.8 collective-permute-done
  158.8 3.1 fusion.6
  161.9 2.4 collective-permute-start.1
  164.3 1.7 collective-permute-start.2
  166.0 54.3 %collective-permute-done.1 = bf16[512,1280]{1,0:T(8,128)(2,1)} collective-permute-done((bf16[512,1280]{1,0:T(8,128)(2,1)S(1)}, bf16[512,1280]{1,0:T(8,128)(2,1)}, u32[]{:S(2)}, u32[]{:S(2)}) %collective-permute-start.1) | collective-permute-done | bytes 1310752 | tf_op jit(solution)/shard_map/ppermute | solution.py:372
  220.3 0.0 collective-permute-done.2
  220.3 5.3 %fusion.2 = (bf16[512,1280]{1,0:T(8,128)(2,1)S(1)}, bf16[512,1280]{1,0:T(8,128)(2,1)}) fusion(bf16[512,1280]{1,0:T(8,128)(2,1)} %collective-permute-done.2, bf16[4,512,1280]{2,1,0:T(8,128)(2,1)} %bitcast.4, s32[]{:T(128)S(6)} %max.10, bf16[4,512,1280]{2,1,0:T(8,128)(2,1)} %bitcast.31, bf16[512,1280]{1,0:T(8,128)(2,1)} %collective-permute-done.1, s32[]{:T(128)S(6)} %select_n.51), kind=kLoop, calls=%fused_computation.6 | loop fusion | flops 7864320 | bytes 10485768 | tf_op jit(solution)/shard_map/convert_element_type | solution.py:367
  225.6 5.6 %collective-permute-start.3 = (bf16[512,1280]{1,0:T(8,128)(2,1)}, bf16[512,1280]{1,0:T(8,128)(2,1)}, u32[]{:S(2)}, u32[]{:S(2)}) collective-permute-start(bf16[512,1280]{1,0:T(8,128)(2,1)} %get-tuple-element.60), channel_id=1, source_target_pairs={{0,8},{4,12},{8,16},{12,20},{1,9},{5,13},{9,17},{13,21},{2,10},{6,... | collective-permute-start | bytes 3932168 | tf_op jit(solution)/shard_map/ppermute | solution.py:372
  231.2 1.7 collective-permute-start.4
  232.9 7.1 %all-gather.5.cloned.1.call-done.b.refs_3_ = bf16[4096,1280]{1,0:T(8,128)(2,1)} async-done(((bf16[512,1280]{1,0:T(8,128)(2,1)}), bf16[4096,1280]{1,0:T(8,128)(2,1)}) %all-gather.5.cloned.1.call-update) | async-done | bytes 10485776 | tf_op jit(solution)/shard_map/all_gather | solution.py:414
  240.0 9.1 %product.6.qkv_ref = bf16[768,768]{1,0:T(8,128)(2,1)S(1)} custom-call(bf16[768,4096]{1,0:T(8,128)(2,1)} %get-tuple-element.61.a, bf16[4096,1280]{1,0:T(8,128)(2,1)} %all-gather.5.cloned.1.call-done.b.refs_3_), custom_call_target="tpu_custom_call" | custom-call | flops 1 | bytes 1 | tf_op jit(solution)/shard_map/product/pallas_call | solution.py:218
  249.1 0.0 copy-start
  249.1 0.0 slice-start
  249.1 5.2 %attend_forward.3 = (bf16[768,512]{1,0:T(8,128)(2,1)S(1)}, f32[4,768]{1,0:T(4,128)S(1)}) custom-call(bf16[768,768]{1,0:T(8,128)(2,1)S(1)} %product.6.qkv_ref), custom_call_target="tpu_custom_call" | custom-call | flops 1 | bytes 1 | tf_op jit(solution)/shard_map/attend_forward/pallas_call | solution.py:61
  254.3 0.0 slice-start.1
  254.3 7.2 %product.7.grad_ref = bf16[768,512]{1,0:T(8,128)(2,1)S(1)} custom-call(bf16[768,4096]{1,0:T(8,128)(2,1)} %a.1, bf16[4096,1280]{1,0:T(8,128)(2,1)} %all-gather.5.cloned.1.call-done.b.refs_3_), custom_call_target="tpu_custom_call" | custom-call | flops 1 | bytes 1 | tf_op jit(solution)/shard_map/product/pallas_call | solution.py:218
  261.5 0.0 copy-done
  261.5 1.9 collective-permute-done.3
  263.4 0.0 collective-permute-done.4
  263.4 0.0 slice-done
  263.4 0.0 slice-done.1
  263.4 5.0 %fusion = (bf16[512,1280]{1,0:T(8,128)(2,1)}, bf16[512,1280]{1,0:T(8,128)(2,1)}) fusion(bf16[512,1280]{1,0:T(8,128)(2,1)} %collective-permute-done.4, bf16[4,512,1280]{2,1,0:T(8,128)(2,1)} %bitcast.4, s32[]{:T(128)S(6)} %max.11, bf16[4,512,1280]{2,1,0:T(8,128)(2,1)S(1)} %bitcast.35, bf16[512,1280]{1,0:T(8,128)(2,1)} %collective-permute-done.3, s32[]{:T(128)S(6)} %select_n.53), kind=kLoop, calls=%fused_computation.2 | loop fusion | flops 7864320 | bytes 10485768 | tf_op jit(solution)/shard_map/convert_element_type | solution.py:367
  268.4 4.5 %collective-permute-start.5 = (bf16[512,1280]{1,0:T(8,128)(2,1)}, bf16[512,1280]{1,0:T(8,128)(2,1)S(1)}, u32[]{:S(2)}, u32[]{:S(2)}) collective-permute-start(bf16[512,1280]{1,0:T(8,128)(2,1)} %get-tuple-element.68), channel_id=1, source_target_pairs={{0,8},{4,12},{8,16},{12,20},{16,24},{20,28},{1,9},{5,13},{9,17},{1... | collective-permute-start | bytes 3932168 | tf_op jit(solution)/shard_map/ppermute | solution.py:372
  272.9 1.5 collective-permute-start.6
  274.4 7.3 %attend_backward.3.refs_2_ = bf16[768,768]{1,0:T(8,128)(2,1)S(1)} custom-call(bf16[768,768]{1,0:T(8,128)(2,1)} %copy-done, bf16[768,512]{1,0:T(8,128)(2,1)S(1)} %product.7.grad_ref, f32[4,768]{1,0:T(4,128)S(1)} %get-tuple-element.70.lse_ref), custom_call_target="tpu_custom_call" | custom-call | flops 1 | bytes 1 | tf_op jit(solution)/shard_map/attend_backward/pallas_call | solution.py:106
  281.7 13.1 %terms.1 = bf16[4096,1280]{1,0:T(8,128)(2,1)} custom-call(bf16[4096,768]{1,0:T(8,128)(2,1)} %get-tuple-element.44.refs_0_, bf16[4096,768]{1,0:T(8,128)(2,1)} %get-tuple-element.45.refs_1_, bf16[768,768]{1,0:T(8,128)(2,1)S(1)} %attend_backward.3.refs_2_, bf16[768,512]{1,0:T(8,128)(2,1)S(1)} %get-tuple-element.71.refs_3_.refs_1_), custom_call_target="tpu_custom_call" | custom-call | flops 1 | bytes 1 | tf_op jit(solution)/shard_map/terms/pallas_call | solution.py:247
  294.8 6.5 %collective-permute-done.5 = bf16[512,1280]{1,0:T(8,128)(2,1)S(1)} collective-permute-done((bf16[512,1280]{1,0:T(8,128)(2,1)}, bf16[512,1280]{1,0:T(8,128)(2,1)S(1)}, u32[]{:S(2)}, u32[]{:S(2)}) %collective-permute-start.5) | collective-permute-done | bytes 1310752 | tf_op jit(solution)/shard_map/ppermute | solution.py:372
  301.3 4.7 %collective-permute-done.6 = bf16[512,1280]{1,0:T(8,128)(2,1)} collective-permute-done((bf16[512,1280]{1,0:T(8,128)(2,1)}, bf16[512,1280]{1,0:T(8,128)(2,1)}, u32[]{:S(2)}, u32[]{:S(2)}) %collective-permute-start.6) | collective-permute-done | bytes 1310752 | tf_op jit(solution)/shard_map/ppermute | solution.py:373
  305.9 0.0 reduce-scatter.2.cloned.1.call-update
  306.0 4.2 fusion.4.refs_0_
  310.1 15.0 %project.1 = bf16[768,4096]{1,0:T(8,128)(2,1)} custom-call(bf16[768,512]{1,0:T(8,128)(2,1)S(1)} %get-tuple-element.76.refs_3_.refs_0_, bf16[768,512]{1,0:T(8,128)(2,1)S(1)} %get-tuple-element.71.refs_3_.refs_1_, bf16[4096,1280]{1,0:T(8,128)(2,1)} %all-gather.3.cloned.1.call-done.b.refs_2_, bf16[4096,1280]{1,0:T(8,128)(2,1)} %all-gather.5.cloned.1.call-done.b.refs_3_), custom_call_target="tpu_custom_call" | custom-call | flops 1 | bytes 1 | tf_op jit(solution)/shard_map/project/pallas_call | solution.py:299
  325.2 3.7 constant_dynamic-slice_fusion.3
  328.8 1.6 collective-permute-start.7
  330.4 1.5 collective-permute-start.8
  331.9 0.5 collective-permute-start.9
  332.4 33.8 %collective-permute-done.7 = bf16[768,1024]{1,0:T(8,128)(2,1)S(1)} collective-permute-done((bf16[768,1024]{1,0:T(8,128)(2,1)S(1)}, bf16[768,1024]{1,0:T(8,128)(2,1)S(1)}, u32[]{:S(2)}, u32[]{:S(2)}) %collective-permute-start.7) | collective-permute-done | bytes 1572896 | tf_op jit(solution)/shard_map/ppermute | solution.py:398
  366.2 32.5 %collective-permute-done.8 = bf16[768,1024]{1,0:T(8,128)(2,1)S(1)} collective-permute-done((bf16[768,1024]{1,0:T(8,128)(2,1)S(1)}, bf16[768,1024]{1,0:T(8,128)(2,1)S(1)}, u32[]{:S(2)}, u32[]{:S(2)}) %collective-permute-start.8) | collective-permute-done | bytes 1572896 | tf_op jit(solution)/shard_map/ppermute | solution.py:398
  398.8 0.0 collective-permute-done.9
  398.8 4.4 %add_convert_fusion = bf16[768,1024]{1,0:T(8,128)(2,1)} fusion(bf16[768,1024]{1,0:T(8,128)(2,1)S(1)} %collective-permute-done.9, bf16[768,1024]{1,0:T(8,128)(2,1)S(1)} %collective-permute-done.8, bf16[768,1024]{1,0:T(8,128)(2,1)S(1)} %collective-permute-done.7, bf16[768,1024]{1,0:T(8,128)(2,1)S(1)} %get-tuple-element.77, bf16[768,4096]{1,0:T(8,128)(2,1)} %x_ref.1, ...), kind=kLoop, calls=%fused_computation | loop fusion | flops 7864320 | bytes 9437188 | tf_op jit(solution)/shard_map/convert_element_type | solution.py:461
  403.2 11.5 %reduce-scatter.2.cloned.1.call-done.refs_1_ = bf16[512,1280]{1,0:T(8,128)(2,1)} async-done(((bf16[4096,1280]{1,0:T(8,128)(2,1)}), bf16[512,1280]{1,0:T(8,128)(2,1)}) %reduce-scatter.2.cloned.1.call-update) | async-done | bytes 1310736 | tf_op jit(solution)/shard_map/reduce_scatter | solution.py:450
  414.8 0.0 copy-start.2
  414.8 1.3 copy-done.2
  416.1 4.5 %unpack.1 = (f32[512,1024]{1,0:T(8,128)}, f32[512,256]{1,0:T(8,128)}, f32[512,256]{1,0:T(8,128)}, f32[512,1024]{1,0:T(8,128)}) custom-call(f32[512,1280]{1,0:T(8,128)} %fusion.4.refs_0_, bf16[512,1280]{1,0:T(8,128)(2,1)S(1)} %copy-done.2), custom_call_target="tpu_custom_call" | custom-call | flops 1 | bytes 1 | tf_op jit(solution)/shard_map/unpack/pallas_call | solution.py:164
  (2 shorter events, 0.0 us)
Async XLA Ops:
  7.2 4.2 copy-start.3
  7.2 105.6 %all-gather.3.cloned.1.call-start = ((), (), s32[]{:S(2)}) async-start(), calls=%async_computation.1 | async-start | bytes 11796480 | tf_op jit(solution)/shard_map/all_gather | solution.py:414
  10.6 229.4 %all-gather.5.cloned.1.call-start = ((), (), s32[]{:S(2)}) async-start(), calls=%async_computation.2 | async-start | bytes 11796480 | tf_op jit(solution)/shard_map/all_gather | solution.py:414
  11.3 403.5 %reduce-scatter.2.cloned.1.call-start = ((), (), s32[]{:S(2)}) async-start(), calls=%async_computation.3 | async-start | bytes 11796480 | tf_op jit(solution)/shard_map/reduce_scatter | solution.py:450
  121.7 12.5 %copy-start.1 = (bf16[768,768]{1,0:T(8,128)(2,1)}, bf16[768,768]{1,0:T(8,128)(2,1)S(1)}, u32[]{:S(2)}) copy-start(bf16[768,768]{1,0:T(8,128)(2,1)S(1)} %product.4.qkv_ref) | copy-start | bytes 3538948
  149.7 9.1 %collective-permute-start = (bf16[2048,1280]{1,0:T(8,128)(2,1)}, bf16[2048,1280]{1,0:T(8,128)(2,1)}, u32[]{:S(2)}, u32[]{:S(2)}) collective-permute-start(bf16[2048,1280]{1,0:T(8,128)(2,1)} %side_terms.2), channel_id=1, source_target_pairs={{0,4},{4,0},{8,12},{12,8},{16,20},{20,16},{24,28},{28,24},{1,5},{5... | collective-permute-start | bytes 15728648 | tf_op jit(solution)/shard_map/ppermute | solution.py:337
  161.9 58.4 %collective-permute-start.1 = (bf16[512,1280]{1,0:T(8,128)(2,1)S(1)}, bf16[512,1280]{1,0:T(8,128)(2,1)}, u32[]{:S(2)}, u32[]{:S(2)}) collective-permute-start(bf16[512,1280]{1,0:T(8,128)(2,1)S(1)} %get-tuple-element.57), channel_id=1, source_target_pairs={{0,8},{4,12},{1,9},{5,13},{2,10},{6,14},{3,11},{7,15}} | collective-permute-start | bytes 3932168 | tf_op jit(solution)/shard_map/ppermute | solution.py:372
  164.3 56.0 %collective-permute-start.2 = (bf16[512,1280]{1,0:T(8,128)(2,1)S(1)}, bf16[512,1280]{1,0:T(8,128)(2,1)}, u32[]{:S(2)}, u32[]{:S(2)}) collective-permute-start(bf16[512,1280]{1,0:T(8,128)(2,1)S(1)} %get-tuple-element.59), channel_id=1, source_target_pairs={{24,16},{28,20},{25,17},{29,21},{26,18},{30,22},{27,19},{31,23}} | collective-permute-start | bytes 3932168 | tf_op jit(solution)/shard_map/ppermute | solution.py:373
  225.6 37.8 %collective-permute-start.3 = (bf16[512,1280]{1,0:T(8,128)(2,1)}, bf16[512,1280]{1,0:T(8,128)(2,1)}, u32[]{:S(2)}, u32[]{:S(2)}) collective-permute-start(bf16[512,1280]{1,0:T(8,128)(2,1)} %get-tuple-element.60), channel_id=1, source_target_pairs={{0,8},{4,12},{8,16},{12,20},{1,9},{5,13},{9,17},{13,21},{2,10},{6,... | collective-permute-start | bytes 3932168 | tf_op jit(solution)/shard_map/ppermute | solution.py:372
  231.2 32.2 %collective-permute-start.4 = (bf16[512,1280]{1,0:T(8,128)(2,1)S(1)}, bf16[512,1280]{1,0:T(8,128)(2,1)}, u32[]{:S(2)}, u32[]{:S(2)}) collective-permute-start(bf16[512,1280]{1,0:T(8,128)(2,1)S(1)} %get-tuple-element.67), channel_id=1, source_target_pairs={{16,8},{20,12},{24,16},{28,20},{17,9},{21,13},{25,17},{29,21},{18,... | collective-permute-start | bytes 3932168 | tf_op jit(solution)/shard_map/ppermute | solution.py:373
  249.1 12.4 %copy-start = (bf16[768,768]{1,0:T(8,128)(2,1)}, bf16[768,768]{1,0:T(8,128)(2,1)S(1)}, u32[]{:S(2)}) copy-start(bf16[768,768]{1,0:T(8,128)(2,1)S(1)} %product.6.qkv_ref) | copy-start | bytes 3538948
  249.1 14.3 %slice-start = ((s8[5242880]{0:T(1024)(128)(4,1)}), s8[4194304]{0:T(1024)(128)(4,1)S(1)}, s32[]{:S(2)}) async-start(s8[5242880]{0:T(1024)(128)(4,1)} %bitcast.33), calls=%async_computation.4 | async-start | bytes 8388608
  254.3 9.1 %slice-start.1 = ((s8[5242880]{0:T(1024)(128)(4,1)}), s8[1048576]{0:T(1024)(128)(4,1)S(1)}, s32[]{:S(2)}) async-start(s8[5242880]{0:T(1024)(128)(4,1)} %bitcast.33), calls=%async_computation.5 | async-start | bytes 2097152
  268.4 32.9 %collective-permute-start.5 = (bf16[512,1280]{1,0:T(8,128)(2,1)}, bf16[512,1280]{1,0:T(8,128)(2,1)S(1)}, u32[]{:S(2)}, u32[]{:S(2)}) collective-permute-start(bf16[512,1280]{1,0:T(8,128)(2,1)} %get-tuple-element.68), channel_id=1, source_target_pairs={{0,8},{4,12},{8,16},{12,20},{16,24},{20,28},{1,9},{5,13},{9,17},{1... | collective-permute-start | bytes 3932168 | tf_op jit(solution)/shard_map/ppermute | solution.py:372
  272.9 33.1 %collective-permute-start.6 = (bf16[512,1280]{1,0:T(8,128)(2,1)}, bf16[512,1280]{1,0:T(8,128)(2,1)}, u32[]{:S(2)}, u32[]{:S(2)}) collective-permute-start(bf16[512,1280]{1,0:T(8,128)(2,1)} %get-tuple-element.72), channel_id=1, source_target_pairs={{8,0},{12,4},{16,8},{20,12},{24,16},{28,20},{9,1},{13,5},{17,9},{2... | collective-permute-start | bytes 3932168 | tf_op jit(solution)/shard_map/ppermute | solution.py:373
  328.8 37.4 %collective-permute-start.7 = (bf16[768,1024]{1,0:T(8,128)(2,1)S(1)}, bf16[768,1024]{1,0:T(8,128)(2,1)S(1)}, u32[]{:S(2)}, u32[]{:S(2)}) collective-permute-start(bf16[768,1024]{1,0:T(8,128)(2,1)S(1)} %get-tuple-element.92), channel_id=1, source_target_pairs={{0,1},{1,0},{2,3},{3,2},{4,5},{5,4},{6,7},{7,6},{8,9},{9,8},{10,11... | collective-permute-start | bytes 4718600 | tf_op jit(solution)/shard_map/ppermute | solution.py:398
  330.4 68.4 %collective-permute-start.8 = (bf16[768,1024]{1,0:T(8,128)(2,1)S(1)}, bf16[768,1024]{1,0:T(8,128)(2,1)S(1)}, u32[]{:S(2)}, u32[]{:S(2)}) collective-permute-start(bf16[768,1024]{1,0:T(8,128)(2,1)S(1)} %get-tuple-element.91), channel_id=1, source_target_pairs={{0,2},{1,3},{2,0},{3,1},{4,6},{5,7},{6,4},{7,5},{8,10},{9,11},{10,... | collective-permute-start | bytes 4718600 | tf_op jit(solution)/shard_map/ppermute | solution.py:398
  331.9 66.9 %collective-permute-start.9 = (bf16[768,1024]{1,0:T(8,128)(2,1)S(1)}, bf16[768,1024]{1,0:T(8,128)(2,1)S(1)}, u32[]{:S(2)}, u32[]{:S(2)}) collective-permute-start(bf16[768,1024]{1,0:T(8,128)(2,1)S(1)} %get-tuple-element.90), channel_id=1, source_target_pairs={{0,3},{1,2},{2,1},{3,0},{4,7},{5,6},{6,5},{7,4},{8,11},{9,10},{10,... | collective-permute-start | bytes 4718600 | tf_op jit(solution)/shard_map/ppermute | solution.py:398
  414.8 1.3 copy-start.2
Sparse Core Ops, SparseCore 0:
  10.7 102.0 all-gather.2
  115.0 124.8 all-gather.4
  306.1 108.6 reduce-scatter.1

commit v5 on v4

--- a/solution.py
+++ b/solution.py
@@ -115,62 +115,64 @@
     )(qkv, grad_mixed, lse)
 
 
-def pack_kernel(groups, query, key, value, out, *packed):
-    width = HEAD_DIM
-    span = query.shape[1] // groups
-    for g, piece in enumerate(packed):
-        heads = slice(g * span, (g + 1) * span)
-        group = slice(g * width, (g + 1) * width)
-        piece[:, :span] = query[:, heads]
-        piece[:, span : span + width] = key[:, group]
-        piece[:, span + width : span + 2 * width] = value[:, group]
-        piece[:, span + 2 * width :] = out[:, heads]
-
-
-def pack(query, key, value, out):
-    rows, cols = query.shape
-    groups = key.shape[1] // HEAD_DIM
-    wide = 2 * cols // groups + 2 * HEAD_DIM
-    return pl.pallas_call(
-        functools.partial(pack_kernel, groups),
-        out_shape=(jax.ShapeDtypeStruct((rows, wide), BF16),) * groups,
+def group_specs(rows, span, g):
+    step = 128 if rows % 128 == 0 else rows
+    return [
+        pl.BlockSpec((step, cols), lambda i: (i, g))
+        for cols in (span, HEAD_DIM, HEAD_DIM, span)
+    ]
+
+
+def pack_kernel(query, key, value, out, piece):
+    at = 0
+    for part in (query, key, value, out):
+        piece[:, at : at + part.shape[1]] = part[...]
+        at += part.shape[1]
+
+
+def pack(query, key, value, out, span, g):
+    rows = query.shape[0]
+    cols = 2 * span + 2 * HEAD_DIM
+    specs = group_specs(rows, span, g)
+    step = specs[0].block_shape[0]
+    return pl.pallas_call(
+        pack_kernel,
+        grid=(rows // step,),
+        out_shape=jax.ShapeDtypeStruct((rows, cols), BF16),
+        in_specs=specs,
+        out_specs=pl.BlockSpec((step, cols), lambda i: (i, 0)),
         compiler_params=pltpu.CompilerParams(vmem_limit_bytes=60 * 2**20),
         cost_estimate=SHORT,
         name="pack",
     )(query, key, value, out)
 
 
-def unpack_kernel(*refs):
-    sums, (grad_query, grad_key, grad_value, grad_out) = refs[:-4], refs[-4:]
-    width = HEAD_DIM
-    span = grad_query.shape[1] // len(sums)
-    for g, part in enumerate(sums):
-        heads = slice(g * span, (g + 1) * span)
-        group = slice(g * width, (g + 1) * width)
-        grad_query[:, heads] = part[:, :span].astype(F32)
-        grad_key[:, group] = part[:, span : span + width].astype(F32)
-        grad_value[:, group] = part[:, span + width : span + 2 * width].astype(F32)
-        grad_out[:, heads] = part[:, span + 2 * width :].astype(F32)
-
-
-def unpack(sums, span):
-    rows = sums[0].shape[0]
-    groups = len(sums)
-    shapes = [
-        jax.ShapeDtypeStruct((rows, groups * cols), F32)
-        for cols in (span, HEAD_DIM, HEAD_DIM, span)
-    ]
-    step = 128 if rows % 128 == 0 else rows
+def unpack_kernel(piece, *refs):
+    at = 0
+    for part in refs[-4:]:
+        part[...] = piece[:, at : at + part.shape[1]].astype(F32)
+        at += part.shape[1]
+
+
+def unpack(piece, grads, span, groups, g):
+    rows = piece.shape[0]
+    specs = group_specs(rows, span, g)
+    step = specs[0].block_shape[0]
     return pl.pallas_call(
         unpack_kernel,
         grid=(rows // step,),
-        out_shape=shapes,
-        in_specs=[pl.BlockSpec((step, part.shape[1]), lambda i: (i, 0)) for part in sums],
-        out_specs=[pl.BlockSpec((step, shape.shape[1]), lambda i: (i, 0)) for shape in shapes],
-        compiler_params=pltpu.CompilerParams(vmem_limit_bytes=VMEM_LIMIT),
+        out_shape=[
+            jax.ShapeDtypeStruct((rows, groups * cols), F32)
+            for cols in (span, HEAD_DIM, HEAD_DIM, span)
+        ],
+        in_specs=[pl.BlockSpec((step, piece.shape[1]), lambda i: (i, 0))]
+        + [pl.BlockSpec(memory_space=pl.ANY)] * len(grads),
+        out_specs=specs,
+        input_output_aliases={1 + i: i for i in range(len(grads))},
+        compiler_params=pltpu.CompilerParams(vmem_limit_bytes=60 * 2**20),
         cost_estimate=SHORT,
         name="unpack",
-    )(*sums)
+    )(piece, *grads)
 
 
 def norm_kernel(x_ref, gain_ref, grad_ref, out, out_t, grad_t):
@@ -410,14 +412,18 @@
     full = span + 2 * width
     order = Order()
 
-    pieces = pack(w_query, w_key, w_value, w_out)
+    pieces = [pack(w_query, w_key, w_value, w_out, span, g) for g in range(groups)]
     weights = [lax.all_gather(piece, "wide", axis=0, tiled=True) for piece in pieces]
     normed, normed_t, cotangent_t = order(normalize, activations, gain, cotangent)
 
     core = lax.axis_index("wide") % 2
     chips = wide // 2
-    mixed, sums = [], []
+    mixed, grads = [], []
     line = None
+
+    def write(piece, g):
+        return order(lambda a, *b: unpack(a, b, span, groups, g), piece, *grads)
+
     for g in range(groups):
         if line is not None and line.hops < chips - 1:
             line.advance()
@@ -438,7 +444,7 @@
 
         if g < groups - 1:
             if line is not None:
-                sums.append(line.total())
+                grads = write(line.total(), g - 1)
             line = LineSum(order, chips)
             line.swap(side(1 - core))
             line.hold(side(core))
@@ -449,8 +455,7 @@
             part, *line.arrived = lax.optimization_barrier((part, *line.arrived))
         last = lax.psum_scatter(part, "wide", scatter_dimension=0, tiled=True)
         if line is not None:
-            sums.append(line.total())
-        sums.append(last)
+            grads = write(line.total(), g - 1)
         parts = order(lambda *a: project(a[:groups], a[groups:]), *mixed, *weights)
         own, arrived = narrow_sum(parts, narrow)
 
@@ -461,7 +466,7 @@
         return (result + sum(part.astype(F32) for part in parts)).astype(BF16)
 
     outputs = order(finish_outputs, activations, own, *arrived)
-    grad_query, grad_key, grad_value, grad_out = unpack(sums, span)
+    grad_query, grad_key, grad_value, grad_out = unpack(last, grads, span, groups, groups - 1)
     return (outputs, grad_query, grad_key, grad_value, grad_out)
 
 

time: 434 us -> 433 us (level)
  waiting for transfers between devices: 242 us -> 235 us
  Pallas kernels: 123 us -> 129 us
    pallas_call x2 -> x4, Pallas kernels: 7.86 us -> 14.9 us  [the longest x2 7.76 us: unpack(): pl.pallas_call(unpack_kernel, grid=(rows // step,), out_shape=[jax.ShapeD...]
  transfers between devices with their start and end apart: 13 -> 13, of which waited for: 10 -> 10; matrix products, arithmetic and copies ran while one was open for 5% -> 5% of each run, Pallas kernels for 27% -> 29%
where the time goes in v5:
time: 433 us; the launch traced here: 426 us
  waiting for transfers between devices  235 us (54%)
  Pallas kernels  129 us (30%)
  other arithmetic  22 us (5%)
  starting transfers between devices  21.3 us (5%)
  between operations  14.4 us (3%)
    all_gather x2, waiting for transfers between devices, shards(): lax.all_gather(piece, 'wide', axis=0, tiled=True)  92.1 us
    ppermute x3, waiting for transfers between devices, narrow_sum(): lax.ppermute(columns_of(mine), 'narrow', list(enumerate(to)))  67 us
    ppermute x3, waiting for transfers between devices, advance(): lax.ppermute(up, 'wide', [(w, w + 2) for w in range(2 * t)])  62.6 us
    pallas_call x4, Pallas kernels, product(): pl.pallas_call(product_kernel, grid=(cols // step,), out_shape=jax.ShapeD...  32.5 us
    pallas_call x2, Pallas kernels, side_terms(): pl.pallas_call(functools.partial(side_terms_kernel, count), grid_spec=plt...  16.1 us
    pallas_call x2, Pallas kernels, attend_backward(): pl.pallas_call(functools.partial(backward_kernel, members, block), out_sh...  14.7 us
    pallas_call x1, Pallas kernels, project(): pl.pallas_call(functools.partial(project_kernel, count), grid=(features /...  14.3 us
    pallas_call x1, Pallas kernels, normalize(): pl.pallas_call(norm_kernel, grid=(length // step,), out_shape=(jax.ShapeD...  13.5 us
  transfers between devices with their start and end apart: 13, of which 10 were waited for; matrix products, arithmetic and copies ran while one was open for 5% of the time, Pallas kernels for 29%

profile of v5, /device:TPU:0, one launch (start us, length us, event | category | flops | bytes accessed | tf_op | source)
XLA Modules:
  0.0 425.7 jit_solution(9265656028619562465)
XLA Ops:
  7.2 0.0 all-gather.3.cloned.1.call-start
  7.2 3.6 pack.2
  10.8 0.0 all-gather.3.cloned.1.call-update
  10.8 0.0 copy-start.2
  10.8 0.0 all-gather.5.cloned.1.call-start
  10.9 3.6 pack.3
  14.4 0.0 all-gather.5.cloned.1.call-update
  14.5 0.0 reduce-scatter.2.cloned.1.call-start
  14.5 0.0 copy-done.2
  14.5 13.5 %normalize.1 = (bf16[768,4096]{1,0:T(8,128)(2,1)}, bf16[4096,768]{1,0:T(8,128)(2,1)}, bf16[4096,768]{1,0:T(8,128)(2,1)}) custom-call(bf16[768,4096]{1,0:T(8,128)(2,1)} %x_ref.1, f32[1,4096]{1,0:T(1,128)S(1)} %bitcast.29, bf16[768,4096]{1,0:T(8,128)(2,1)} %a.1), custom_call_target="tpu_custom_call" | custom-call | flops 1 | bytes 1 | tf_op jit(solution)/shard_map/normalize/pallas_call | solution.py:201
  28.0 85.0 %all-gather.3.cloned.1.call-done.b.refs_2_ = bf16[4096,1280]{1,0:T(8,128)(2,1)} async-done(((bf16[512,1280]{1,0:T(8,128)(2,1)}), bf16[4096,1280]{1,0:T(8,128)(2,1)}) %all-gather.3.cloned.1.call-update) | async-done | bytes 10485776 | tf_op jit(solution)/shard_map/all_gather | solution.py:416
  113.1 8.9 %product.4.qkv_ref = bf16[768,768]{1,0:T(8,128)(2,1)S(1)} custom-call(bf16[768,4096]{1,0:T(8,128)(2,1)} %get-tuple-element.62.a, bf16[4096,1280]{1,0:T(8,128)(2,1)} %all-gather.3.cloned.1.call-done.b.refs_2_), custom_call_target="tpu_custom_call" | custom-call | flops 1 | bytes 1 | tf_op jit(solution)/shard_map/product/pallas_call | solution.py:220
  122.0 0.0 copy-start.1
  122.0 5.2 %attend_forward.2 = (bf16[768,512]{1,0:T(8,128)(2,1)S(1)}, f32[4,768]{1,0:T(4,128)S(1)}) custom-call(bf16[768,768]{1,0:T(8,128)(2,1)S(1)} %product.4.qkv_ref), custom_call_target="tpu_custom_call" | custom-call | flops 1 | bytes 1 | tf_op jit(solution)/shard_map/attend_forward/pallas_call | solution.py:61
  127.1 7.3 %product.5.grad_ref = bf16[768,512]{1,0:T(8,128)(2,1)S(1)} custom-call(bf16[768,4096]{1,0:T(8,128)(2,1)} %a.1, bf16[4096,1280]{1,0:T(8,128)(2,1)} %all-gather.3.cloned.1.call-done.b.refs_2_), custom_call_target="tpu_custom_call" | custom-call | flops 1 | bytes 1 | tf_op jit(solution)/shard_map/product/pallas_call | solution.py:220
  134.5 0.0 copy-done.1
  134.5 7.4 %attend_backward.2.refs_2_ = bf16[768,768]{1,0:T(8,128)(2,1)S(1)} custom-call(bf16[768,768]{1,0:T(8,128)(2,1)} %copy-done.1, bf16[768,512]{1,0:T(8,128)(2,1)S(1)} %product.5.grad_ref, f32[4,768]{1,0:T(4,128)S(1)} %get-tuple-element.54.lse_ref), custom_call_target="tpu_custom_call" | custom-call | flops 1 | bytes 1 | tf_op jit(solution)/shard_map/attend_backward/pallas_call | solution.py:106
  141.9 8.0 %side_terms.2 = bf16[2048,1280]{1,0:T(8,128)(2,1)} custom-call(s32[1]{0:T(128)} %bitcast.2.side, bf16[4096,768]{1,0:T(8,128)(2,1)} %get-tuple-element.46.refs_0_, bf16[4096,768]{1,0:T(8,128)(2,1)} %get-tuple-element.47.refs_1_, bf16[768,768]{1,0:T(8,128)(2,1)S(1)} %attend_backward.2.refs_2_, bf16[768,512]{1,0:T(8,128)(2,1)S(1)} %get-tuple-element.77.refs_3_.refs_0_), custom_call_target="tpu_custom_call" | custom-call | flops 1 | bytes 1 | tf_op jit(solution)/shard_map/side_terms/pallas_call | solution.py:271
  149.9 0.3 collective-permute-start
  150.2 8.1 %side_terms.3 = bf16[2048,1280]{1,0:T(8,128)(2,1)} custom-call(s32[1]{0:T(128)} %bitcast.side, bf16[4096,768]{1,0:T(8,128)(2,1)} %get-tuple-element.46.refs_0_, bf16[4096,768]{1,0:T(8,128)(2,1)} %get-tuple-element.47.refs_1_, bf16[768,768]{1,0:T(8,128)(2,1)S(1)} %attend_backward.2.refs_2_, bf16[768,512]{1,0:T(8,128)(2,1)S(1)} %get-tuple-element.77.refs_3_.refs_0_), custom_call_target="tpu_custom_call" | custom-call | flops 1 | bytes 1 | tf_op jit(solution)/shard_map/side_terms/pallas_call | solution.py:271
  158.2 0.8 collective-permute-done
  159.0 3.1 fusion.6
  162.1 2.4 collective-permute-start.1
  164.5 1.7 collective-permute-start.2
  166.2 54.3 %collective-permute-done.1 = bf16[512,1280]{1,0:T(8,128)(2,1)} collective-permute-done((bf16[512,1280]{1,0:T(8,128)(2,1)S(1)}, bf16[512,1280]{1,0:T(8,128)(2,1)}, u32[]{:S(2)}, u32[]{:S(2)}) %collective-permute-start.1) | collective-permute-done | bytes 1310752 | tf_op jit(solution)/shard_map/ppermute | solution.py:374
  220.5 0.0 collective-permute-done.2
  220.5 5.3 %fusion.2 = (bf16[512,1280]{1,0:T(8,128)(2,1)S(1)}, bf16[512,1280]{1,0:T(8,128)(2,1)}) fusion(bf16[512,1280]{1,0:T(8,128)(2,1)} %collective-permute-done.2, bf16[4,512,1280]{2,1,0:T(8,128)(2,1)} %bitcast.4, s32[]{:T(128)S(6)} %max.10, bf16[4,512,1280]{2,1,0:T(8,128)(2,1)} %bitcast.31, bf16[512,1280]{1,0:T(8,128)(2,1)} %collective-permute-done.1, s32[]{:T(128)S(6)} %select_n.51), kind=kLoop, calls=%fused_computation.6 | loop fusion | flops 7864320 | bytes 10485768 | tf_op jit(solution)/shard_map/convert_element_type | solution.py:369
  225.8 5.6 %collective-permute-start.3 = (bf16[512,1280]{1,0:T(8,128)(2,1)}, bf16[512,1280]{1,0:T(8,128)(2,1)}, u32[]{:S(2)}, u32[]{:S(2)}) collective-permute-start(bf16[512,1280]{1,0:T(8,128)(2,1)} %get-tuple-element.61), channel_id=1, source_target_pairs={{0,8},{4,12},{8,16},{12,20},{1,9},{5,13},{9,17},{13,21},{2,10},{6,... | collective-permute-start | bytes 3932168 | tf_op jit(solution)/shard_map/ppermute | solution.py:374
  231.4 1.7 collective-permute-start.4
  233.1 7.1 %all-gather.5.cloned.1.call-done.b.refs_3_ = bf16[4096,1280]{1,0:T(8,128)(2,1)} async-done(((bf16[512,1280]{1,0:T(8,128)(2,1)}), bf16[4096,1280]{1,0:T(8,128)(2,1)}) %all-gather.5.cloned.1.call-update) | async-done | bytes 10485776 | tf_op jit(solution)/shard_map/all_gather | solution.py:416
  240.2 9.1 %product.6.qkv_ref = bf16[768,768]{1,0:T(8,128)(2,1)S(1)} custom-call(bf16[768,4096]{1,0:T(8,128)(2,1)} %get-tuple-element.62.a, bf16[4096,1280]{1,0:T(8,128)(2,1)} %all-gather.5.cloned.1.call-done.b.refs_3_), custom_call_target="tpu_custom_call" | custom-call | flops 1 | bytes 1 | tf_op jit(solution)/shard_map/product/pallas_call | solution.py:220
  249.3 0.0 copy-start
  249.3 0.0 slice-start
  249.3 5.2 %attend_forward.3 = (bf16[768,512]{1,0:T(8,128)(2,1)S(1)}, f32[4,768]{1,0:T(4,128)S(1)}) custom-call(bf16[768,768]{1,0:T(8,128)(2,1)S(1)} %product.6.qkv_ref), custom_call_target="tpu_custom_call" | custom-call | flops 1 | bytes 1 | tf_op jit(solution)/shard_map/attend_forward/pallas_call | solution.py:61
  254.5 0.0 slice-start.1
  254.5 7.2 %product.7.grad_ref = bf16[768,512]{1,0:T(8,128)(2,1)S(1)} custom-call(bf16[768,4096]{1,0:T(8,128)(2,1)} %a.1, bf16[4096,1280]{1,0:T(8,128)(2,1)} %all-gather.5.cloned.1.call-done.b.refs_3_), custom_call_target="tpu_custom_call" | custom-call | flops 1 | bytes 1 | tf_op jit(solution)/shard_map/product/pallas_call | solution.py:220
  261.7 0.0 copy-done
  261.7 1.9 collective-permute-done.3
  263.6 0.0 collective-permute-done.4
  263.6 0.0 slice-done
  263.6 0.0 slice-done.1
  263.6 5.0 %fusion = (bf16[512,1280]{1,0:T(8,128)(2,1)}, bf16[512,1280]{1,0:T(8,128)(2,1)}) fusion(bf16[512,1280]{1,0:T(8,128)(2,1)} %collective-permute-done.4, bf16[4,512,1280]{2,1,0:T(8,128)(2,1)} %bitcast.4, s32[]{:T(128)S(6)} %max.11, bf16[4,512,1280]{2,1,0:T(8,128)(2,1)S(1)} %bitcast.35, bf16[512,1280]{1,0:T(8,128)(2,1)} %collective-permute-done.3, s32[]{:T(128)S(6)} %select_n.53), kind=kLoop, calls=%fused_computation.2 | loop fusion | flops 7864320 | bytes 10485768 | tf_op jit(solution)/shard_map/convert_element_type | solution.py:369
  268.6 4.5 %collective-permute-start.5 = (bf16[512,1280]{1,0:T(8,128)(2,1)}, bf16[512,1280]{1,0:T(8,128)(2,1)S(1)}, u32[]{:S(2)}, u32[]{:S(2)}) collective-permute-start(bf16[512,1280]{1,0:T(8,128)(2,1)} %get-tuple-element.68), channel_id=1, source_target_pairs={{0,8},{4,12},{8,16},{12,20},{16,24},{20,28},{1,9},{5,13},{9,17},{1... | collective-permute-start | bytes 3932168 | tf_op jit(solution)/shard_map/ppermute | solution.py:374
  273.1 1.5 collective-permute-start.6
  274.7 7.3 %attend_backward.3.refs_2_ = bf16[768,768]{1,0:T(8,128)(2,1)S(1)} custom-call(bf16[768,768]{1,0:T(8,128)(2,1)} %copy-done, bf16[768,512]{1,0:T(8,128)(2,1)S(1)} %product.7.grad_ref, f32[4,768]{1,0:T(4,128)S(1)} %get-tuple-element.70.lse_ref), custom_call_target="tpu_custom_call" | custom-call | flops 1 | bytes 1 | tf_op jit(solution)/shard_map/attend_backward/pallas_call | solution.py:106
  282.0 13.1 %terms.1 = bf16[4096,1280]{1,0:T(8,128)(2,1)} custom-call(bf16[4096,768]{1,0:T(8,128)(2,1)} %get-tuple-element.46.refs_0_, bf16[4096,768]{1,0:T(8,128)(2,1)} %get-tuple-element.47.refs_1_, bf16[768,768]{1,0:T(8,128)(2,1)S(1)} %attend_backward.3.refs_2_, bf16[768,512]{1,0:T(8,128)(2,1)S(1)} %get-tuple-element.71.refs_3_.refs_1_), custom_call_target="tpu_custom_call" | custom-call | flops 1 | bytes 1 | tf_op jit(solution)/shard_map/terms/pallas_call | solution.py:249
  295.1 6.4 %collective-permute-done.5 = bf16[512,1280]{1,0:T(8,128)(2,1)S(1)} collective-permute-done((bf16[512,1280]{1,0:T(8,128)(2,1)}, bf16[512,1280]{1,0:T(8,128)(2,1)S(1)}, u32[]{:S(2)}, u32[]{:S(2)}) %collective-permute-start.5) | collective-permute-done | bytes 1310752 | tf_op jit(solution)/shard_map/ppermute | solution.py:374
  301.5 4.7 %collective-permute-done.6 = bf16[512,1280]{1,0:T(8,128)(2,1)} collective-permute-done((bf16[512,1280]{1,0:T(8,128)(2,1)}, bf16[512,1280]{1,0:T(8,128)(2,1)}, u32[]{:S(2)}, u32[]{:S(2)}) %collective-permute-start.6) | collective-permute-done | bytes 1310752 | tf_op jit(solution)/shard_map/ppermute | solution.py:375
  306.2 0.0 reduce-scatter.2.cloned.1.call-update
  306.2 4.2 fusion.4.piece
  310.4 4.1 unpack.2
  314.5 14.3 %project.1 = bf16[768,4096]{1,0:T(8,128)(2,1)} custom-call(bf16[768,512]{1,0:T(8,128)(2,1)S(1)} %get-tuple-element.77.refs_3_.refs_0_, bf16[768,512]{1,0:T(8,128)(2,1)S(1)} %get-tuple-element.71.refs_3_.refs_1_, bf16[4096,1280]{1,0:T(8,128)(2,1)} %all-gather.3.cloned.1.call-done.b.refs_2_, bf16[4096,1280]{1,0:T(8,128)(2,1)} %all-gather.5.cloned.1.call-done.b.refs_3_), custom_call_target="tpu_custom_call" | custom-call | flops 1 | bytes 1 | tf_op jit(solution)/shard_map/project/pallas_call | solution.py:301
  328.8 3.7 constant_dynamic-slice_fusion.3
  332.5 1.6 collective-permute-start.7
  334.1 1.5 collective-permute-start.8
  335.6 0.5 collective-permute-start.9
  336.0 33.8 %collective-permute-done.7 = bf16[768,1024]{1,0:T(8,128)(2,1)S(1)} collective-permute-done((bf16[768,1024]{1,0:T(8,128)(2,1)S(1)}, bf16[768,1024]{1,0:T(8,128)(2,1)S(1)}, u32[]{:S(2)}, u32[]{:S(2)}) %collective-permute-start.7) | collective-permute-done | bytes 1572896 | tf_op jit(solution)/shard_map/ppermute | solution.py:400
  369.9 33.1 %collective-permute-done.8 = bf16[768,1024]{1,0:T(8,128)(2,1)S(1)} collective-permute-done((bf16[768,1024]{1,0:T(8,128)(2,1)S(1)}, bf16[768,1024]{1,0:T(8,128)(2,1)S(1)}, u32[]{:S(2)}, u32[]{:S(2)}) %collective-permute-start.8) | collective-permute-done | bytes 1572896 | tf_op jit(solution)/shard_map/ppermute | solution.py:400
  403.0 0.0 collective-permute-done.9
  403.0 4.5 %add_convert_fusion = bf16[768,1024]{1,0:T(8,128)(2,1)} fusion(bf16[768,1024]{1,0:T(8,128)(2,1)S(1)} %collective-permute-done.9, bf16[768,1024]{1,0:T(8,128)(2,1)S(1)} %collective-permute-done.8, bf16[768,1024]{1,0:T(8,128)(2,1)S(1)} %collective-permute-done.7, bf16[768,1024]{1,0:T(8,128)(2,1)S(1)} %get-tuple-element.78, bf16[768,4096]{1,0:T(8,128)(2,1)} %x_ref.1, ...), kind=kLoop, calls=%fused_computation | loop fusion | flops 7864320 | bytes 9437188 | tf_op jit(solution)/shard_map/convert_element_type | solution.py:466
  407.5 7.6 %reduce-scatter.2.cloned.1.call-done.piece = bf16[512,1280]{1,0:T(8,128)(2,1)} async-done(((bf16[4096,1280]{1,0:T(8,128)(2,1)}), bf16[512,1280]{1,0:T(8,128)(2,1)}) %reduce-scatter.2.cloned.1.call-update) | async-done | bytes 1310736 | tf_op jit(solution)/shard_map/reduce_scatter | solution.py:456
  415.0 3.7 unpack.3
  (2 shorter events, 0.0 us)
Async XLA Ops:
  7.2 105.9 %all-gather.3.cloned.1.call-start = ((), (), s32[]{:S(2)}) async-start(), calls=%async_computation.1 | async-start | bytes 11796480 | tf_op jit(solution)/shard_map/all_gather | solution.py:416
  10.8 3.7 copy-start.2
  10.8 229.4 %all-gather.5.cloned.1.call-start = ((), (), s32[]{:S(2)}) async-start(), calls=%async_computation.2 | async-start | bytes 11796480 | tf_op jit(solution)/shard_map/all_gather | solution.py:416
  14.5 400.6 %reduce-scatter.2.cloned.1.call-start = ((), (), s32[]{:S(2)}) async-start(), calls=%async_computation.3 | async-start | bytes 11796480 | tf_op jit(solution)/shard_map/reduce_scatter | solution.py:456
  122.0 12.5 %copy-start.1 = (bf16[768,768]{1,0:T(8,128)(2,1)}, bf16[768,768]{1,0:T(8,128)(2,1)S(1)}, u32[]{:S(2)}) copy-start(bf16[768,768]{1,0:T(8,128)(2,1)S(1)} %product.4.qkv_ref) | copy-start | bytes 3538948
  149.9 9.1 %collective-permute-start = (bf16[2048,1280]{1,0:T(8,128)(2,1)}, bf16[2048,1280]{1,0:T(8,128)(2,1)}, u32[]{:S(2)}, u32[]{:S(2)}) collective-permute-start(bf16[2048,1280]{1,0:T(8,128)(2,1)} %side_terms.2), channel_id=1, source_target_pairs={{0,4},{4,0},{8,12},{12,8},{16,20},{20,16},{24,28},{28,24},{1,5},{5... | collective-permute-start | bytes 15728648 | tf_op jit(solution)/shard_map/ppermute | solution.py:339
  162.1 58.4 %collective-permute-start.1 = (bf16[512,1280]{1,0:T(8,128)(2,1)S(1)}, bf16[512,1280]{1,0:T(8,128)(2,1)}, u32[]{:S(2)}, u32[]{:S(2)}) collective-permute-start(bf16[512,1280]{1,0:T(8,128)(2,1)S(1)} %get-tuple-element.58), channel_id=1, source_target_pairs={{0,8},{4,12},{1,9},{5,13},{2,10},{6,14},{3,11},{7,15}} | collective-permute-start | bytes 3932168 | tf_op jit(solution)/shard_map/ppermute | solution.py:374
  164.5 56.0 %collective-permute-start.2 = (bf16[512,1280]{1,0:T(8,128)(2,1)S(1)}, bf16[512,1280]{1,0:T(8,128)(2,1)}, u32[]{:S(2)}, u32[]{:S(2)}) collective-permute-start(bf16[512,1280]{1,0:T(8,128)(2,1)S(1)} %get-tuple-element.60), channel_id=1, source_target_pairs={{24,16},{28,20},{25,17},{29,21},{26,18},{30,22},{27,19},{31,23}} | collective-permute-start | bytes 3932168 | tf_op jit(solution)/shard_map/ppermute | solution.py:375
  225.8 37.8 %collective-permute-start.3 = (bf16[512,1280]{1,0:T(8,128)(2,1)}, bf16[512,1280]{1,0:T(8,128)(2,1)}, u32[]{:S(2)}, u32[]{:S(2)}) collective-permute-start(bf16[512,1280]{1,0:T(8,128)(2,1)} %get-tuple-element.61), channel_id=1, source_target_pairs={{0,8},{4,12},{8,16},{12,20},{1,9},{5,13},{9,17},{13,21},{2,10},{6,... | collective-permute-start | bytes 3932168 | tf_op jit(solution)/shard_map/ppermute | solution.py:374
  231.4 32.2 %collective-permute-start.4 = (bf16[512,1280]{1,0:T(8,128)(2,1)S(1)}, bf16[512,1280]{1,0:T(8,128)(2,1)}, u32[]{:S(2)}, u32[]{:S(2)}) collective-permute-start(bf16[512,1280]{1,0:T(8,128)(2,1)S(1)} %get-tuple-element.67), channel_id=1, source_target_pairs={{16,8},{20,12},{24,16},{28,20},{17,9},{21,13},{25,17},{29,21},{18,... | collective-permute-start | bytes 3932168 | tf_op jit(solution)/shard_map/ppermute | solution.py:375
  249.3 12.4 %copy-start = (bf16[768,768]{1,0:T(8,128)(2,1)}, bf16[768,768]{1,0:T(8,128)(2,1)S(1)}, u32[]{:S(2)}) copy-start(bf16[768,768]{1,0:T(8,128)(2,1)S(1)} %product.6.qkv_ref) | copy-start | bytes 3538948
  249.3 14.3 %slice-start = ((s8[5242880]{0:T(1024)(128)(4,1)}), s8[4194304]{0:T(1024)(128)(4,1)S(1)}, s32[]{:S(2)}) async-start(s8[5242880]{0:T(1024)(128)(4,1)} %bitcast.33), calls=%async_computation.4 | async-start | bytes 8388608
  254.5 9.1 %slice-start.1 = ((s8[5242880]{0:T(1024)(128)(4,1)}), s8[1048576]{0:T(1024)(128)(4,1)S(1)}, s32[]{:S(2)}) async-start(s8[5242880]{0:T(1024)(128)(4,1)} %bitcast.33), calls=%async_computation.5 | async-start | bytes 2097152
  268.6 32.9 %collective-permute-start.5 = (bf16[512,1280]{1,0:T(8,128)(2,1)}, bf16[512,1280]{1,0:T(8,128)(2,1)S(1)}, u32[]{:S(2)}, u32[]{:S(2)}) collective-permute-start(bf16[512,1280]{1,0:T(8,128)(2,1)} %get-tuple-element.68), channel_id=1, source_target_pairs={{0,8},{4,12},{8,16},{12,20},{16,24},{20,28},{1,9},{5,13},{9,17},{1... | collective-permute-start | bytes 3932168 | tf_op jit(solution)/shard_map/ppermute | solution.py:374
  273.1 33.1 %collective-permute-start.6 = (bf16[512,1280]{1,0:T(8,128)(2,1)}, bf16[512,1280]{1,0:T(8,128)(2,1)}, u32[]{:S(2)}, u32[]{:S(2)}) collective-permute-start(bf16[512,1280]{1,0:T(8,128)(2,1)} %get-tuple-element.72), channel_id=1, source_target_pairs={{8,0},{12,4},{16,8},{20,12},{24,16},{28,20},{9,1},{13,5},{17,9},{2... | collective-permute-start | bytes 3932168 | tf_op jit(solution)/shard_map/ppermute | solution.py:375
  332.5 37.4 %collective-permute-start.7 = (bf16[768,1024]{1,0:T(8,128)(2,1)S(1)}, bf16[768,1024]{1,0:T(8,128)(2,1)S(1)}, u32[]{:S(2)}, u32[]{:S(2)}) collective-permute-start(bf16[768,1024]{1,0:T(8,128)(2,1)S(1)} %get-tuple-element.96), channel_id=1, source_target_pairs={{0,1},{1,0},{2,3},{3,2},{4,5},{5,4},{6,7},{7,6},{8,9},{9,8},{10,11... | collective-permute-start | bytes 4718600 | tf_op jit(solution)/shard_map/ppermute | solution.py:400
  334.1 68.9 %collective-permute-start.8 = (bf16[768,1024]{1,0:T(8,128)(2,1)S(1)}, bf16[768,1024]{1,0:T(8,128)(2,1)S(1)}, u32[]{:S(2)}, u32[]{:S(2)}) collective-permute-start(bf16[768,1024]{1,0:T(8,128)(2,1)S(1)} %get-tuple-element.95), channel_id=1, source_target_pairs={{0,2},{1,3},{2,0},{3,1},{4,6},{5,7},{6,4},{7,5},{8,10},{9,11},{10,... | collective-permute-start | bytes 4718600 | tf_op jit(solution)/shard_map/ppermute | solution.py:400
  335.6 67.4 %collective-permute-start.9 = (bf16[768,1024]{1,0:T(8,128)(2,1)S(1)}, bf16[768,1024]{1,0:T(8,128)(2,1)S(1)}, u32[]{:S(2)}, u32[]{:S(2)}) collective-permute-start(bf16[768,1024]{1,0:T(8,128)(2,1)S(1)} %get-tuple-element.94), channel_id=1, source_target_pairs={{0,3},{1,2},{2,1},{3,0},{4,7},{5,6},{6,5},{7,4},{8,11},{9,10},{10,... | collective-permute-start | bytes 4718600 | tf_op jit(solution)/shard_map/ppermute | solution.py:400
Sparse Core Ops, SparseCore 0:
  10.9 102.0 all-gather.2
  115.3 124.8 all-gather.4
  306.3 108.6 reduce-scatter.1

commit v6 on v5

--- a/solution.py
+++ b/solution.py
@@ -339,6 +339,24 @@
     return lax.ppermute(array, "wide", [(w, w ^ 1) for w in range(2 * chips)])
 
 
+def add_kernel(a, b, out):
+    out[...] = (a[...].astype(F32) + b[...].astype(F32)).astype(BF16)
+
+
+def add_blocks(a, b):
+    spec = pl.BlockSpec((1,) + a.shape[1:], lambda i: (i, 0, 0))
+    return pl.pallas_call(
+        add_kernel,
+        grid=a.shape[:1],
+        out_shape=jax.ShapeDtypeStruct(a.shape, BF16),
+        in_specs=[spec, spec],
+        out_specs=spec,
+        compiler_params=pltpu.CompilerParams(vmem_limit_bytes=VMEM_LIMIT),
+        cost_estimate=SHORT,
+        name="add_blocks",
+    )(a, b)
+
+
 class LineSum:
     def __init__(self, order, chips):
         self.order, self.chips = order, chips
@@ -353,36 +371,43 @@
         self.received = self.blocks(swap_cores(send, self.chips))
 
     def hold(self, keep):
-        self.keep = self.blocks(keep)
+        self.held = (self.blocks(keep), self.received)
 
     def advance(self):
         self.hops += 1
         t, chips, chip = self.hops, self.chips, self.chip
         far = chips - t
 
-        def messages(keep, received, *arrived):
+        def messages(held, *arrived):
             sums = []
             for i, at in enumerate((jnp.minimum(chip + far, chips - 1), jnp.maximum(chip - far, 0))):
-                total = take(keep, at).astype(F32) + take(received, at).astype(F32)
+                total = sum(take(part, at).astype(F32) for part in held)
                 if arrived:
                     total = total + arrived[i].astype(F32)
                 sums.append(total.astype(BF16))
             return tuple(sums)
 
-        up, down = self.order(messages, self.keep, self.received, *self.arrived)
+        count = len(self.held)
+        up, down = self.order(
+            lambda *a: messages(a[:count], *a[count:]), *self.held, *self.arrived
+        )
         self.arrived = (
             lax.ppermute(up, "wide", [(w, w + 2) for w in range(2 * t)]),
             lax.ppermute(down, "wide", [(w, w - 2) for w in range(2 * far, 2 * chips)]),
         )
+        if t == 1:
+            self.held = (
+                self.order(add_blocks, *self.held),
+            )
 
     def total(self):
-        def add(keep, received, *arrived):
-            result = take(keep, self.chip).astype(F32) + take(received, self.chip).astype(F32)
+        def add(held, *arrived):
+            result = take(held, self.chip).astype(F32)
             for part in arrived:
                 result = result + part.astype(F32)
             return result
 
-        return self.order(add, self.keep, self.received, *self.arrived)
+        return self.order(add, *self.held, *self.arrived)
 
 
 def narrow_sum(parts, size):

time: 433 us -> 431 us (level)
  Pallas kernels: 129 us -> 136 us
  waiting for transfers between devices: 235 us -> 229 us
    pallas_call x0 -> x1, Pallas kernels: none -> 6.95 us  [add_blocks(): pl.pallas_call(add_kernel, grid=a.shape[:1], out_shape=jax.ShapeDtypeStru...]
    ppermute x3, waiting for transfers between devices: 62.6 us -> 57.8 us  [advance(): lax.ppermute(up, 'wide', [(w, w + 2) for w in range(2 * t)])]
  transfers between devices with their start and end apart: 13 -> 13, of which waited for: 10 -> 10; matrix products, arithmetic and copies ran while one was open for 5% -> 5% of each run, Pallas kernels for 29% -> 30%
where the time goes in v6:
time: 431 us; the launch traced here: 425 us
  waiting for transfers between devices  229 us (53%)
  Pallas kernels  136 us (32%)
  other arithmetic  20.3 us (5%)
  starting transfers between devices  20.2 us (5%)
  between operations  14.4 us (3%)
  local copies, waits for them, and re-layouts  4.69 us (1%)
    all_gather x2, waiting for transfers between devices, shards(): lax.all_gather(piece, 'wide', axis=0, tiled=True)  89.8 us
    ppermute x3, waiting for transfers between devices, narrow_sum(): lax.ppermute(columns_of(mine), 'narrow', list(enumerate(to)))  66.5 us
    ppermute x3, waiting for transfers between devices, advance(): lax.ppermute(up, 'wide', [(w, w + 2) for w in range(2 * t)])  57.8 us
    pallas_call x4, Pallas kernels, product(): pl.pallas_call(product_kernel, grid=(cols // step,), out_shape=jax.ShapeD...  32.6 us
    pallas_call x2, Pallas kernels, side_terms(): pl.pallas_call(functools.partial(side_terms_kernel, count), grid_spec=plt...  16.1 us
    pallas_call x2, Pallas kernels, attend_backward(): pl.pallas_call(functools.partial(backward_kernel, members, block), out_sh...  14.7 us
    pallas_call x1, Pallas kernels, project(): pl.pallas_call(functools.partial(project_kernel, count), grid=(features /...  14.3 us
    pallas_call x1, Pallas kernels, normalize(): pl.pallas_call(norm_kernel, grid=(length // step,), out_shape=(jax.ShapeD...  13.6 us
  transfers between devices with their start and end apart: 13, of which 10 were waited for; matrix products, arithmetic and copies ran while one was open for 5% of the time, Pallas kernels for 30%

profile of v6, /device:TPU:0, one launch (start us, length us, event | category | flops | bytes accessed | tf_op | source)
XLA Modules:
  0.0 424.5 jit_solution(5932671083576204455)
XLA Ops:
  7.2 0.0 all-gather.3.cloned.1.call-start
  7.2 3.6 pack.2
  10.8 0.0 all-gather.3.cloned.1.call-update
  10.8 0.0 copy-start.3
  10.8 0.0 all-gather.5.cloned.1.call-start
  10.9 3.6 pack.3
  14.4 0.0 all-gather.5.cloned.1.call-update
  14.5 0.0 reduce-scatter.2.cloned.1.call-start
  14.5 0.0 copy-done.3
  14.5 13.6 %normalize.1 = (bf16[768,4096]{1,0:T(8,128)(2,1)}, bf16[4096,768]{1,0:T(8,128)(2,1)}, bf16[4096,768]{1,0:T(8,128)(2,1)}) custom-call(bf16[768,4096]{1,0:T(8,128)(2,1)} %x_ref.1, f32[1,4096]{1,0:T(1,128)S(1)} %bitcast.24, bf16[768,4096]{1,0:T(8,128)(2,1)} %a.1), custom_call_target="tpu_custom_call" | custom-call | flops 1 | bytes 1 | tf_op jit(solution)/shard_map/normalize/pallas_call | solution.py:201
  28.1 84.9 %all-gather.3.cloned.1.call-done.b.refs_2_ = bf16[4096,1280]{1,0:T(8,128)(2,1)} async-done(((bf16[512,1280]{1,0:T(8,128)(2,1)}), bf16[4096,1280]{1,0:T(8,128)(2,1)}) %all-gather.3.cloned.1.call-update) | async-done | bytes 10485776 | tf_op jit(solution)/shard_map/all_gather | solution.py:441
  113.1 8.9 %product.4.qkv_ref = bf16[768,768]{1,0:T(8,128)(2,1)S(1)} custom-call(bf16[768,4096]{1,0:T(8,128)(2,1)} %get-tuple-element.64.a, bf16[4096,1280]{1,0:T(8,128)(2,1)} %all-gather.3.cloned.1.call-done.b.refs_2_), custom_call_target="tpu_custom_call" | custom-call | flops 1 | bytes 1 | tf_op jit(solution)/shard_map/product/pallas_call | solution.py:220
  122.0 0.0 copy-start.1
  122.0 5.2 %attend_forward.2 = (bf16[768,512]{1,0:T(8,128)(2,1)S(1)}, f32[4,768]{1,0:T(4,128)S(1)}) custom-call(bf16[768,768]{1,0:T(8,128)(2,1)S(1)} %product.4.qkv_ref), custom_call_target="tpu_custom_call" | custom-call | flops 1 | bytes 1 | tf_op jit(solution)/shard_map/attend_forward/pallas_call | solution.py:61
  127.1 7.3 %product.5.grad_ref = bf16[768,512]{1,0:T(8,128)(2,1)S(1)} custom-call(bf16[768,4096]{1,0:T(8,128)(2,1)} %a.1, bf16[4096,1280]{1,0:T(8,128)(2,1)} %all-gather.3.cloned.1.call-done.b.refs_2_), custom_call_target="tpu_custom_call" | custom-call | flops 1 | bytes 1 | tf_op jit(solution)/shard_map/product/pallas_call | solution.py:220
  134.5 0.0 copy-done.1
  134.5 7.4 %attend_backward.2.refs_2_ = bf16[768,768]{1,0:T(8,128)(2,1)S(1)} custom-call(bf16[768,768]{1,0:T(8,128)(2,1)} %copy-done.1, bf16[768,512]{1,0:T(8,128)(2,1)S(1)} %product.5.grad_ref, f32[4,768]{1,0:T(4,128)S(1)} %get-tuple-element.55.lse_ref), custom_call_target="tpu_custom_call" | custom-call | flops 1 | bytes 1 | tf_op jit(solution)/shard_map/attend_backward/pallas_call | solution.py:106
  141.9 8.1 %side_terms.2 = bf16[2048,1280]{1,0:T(8,128)(2,1)} custom-call(s32[1]{0:T(128)} %bitcast.2.side, bf16[4096,768]{1,0:T(8,128)(2,1)} %get-tuple-element.47.refs_0_, bf16[4096,768]{1,0:T(8,128)(2,1)} %get-tuple-element.48.refs_1_, bf16[768,768]{1,0:T(8,128)(2,1)S(1)} %attend_backward.2.refs_2_, bf16[768,512]{1,0:T(8,128)(2,1)S(1)} %get-tuple-element.79.refs_3_.refs_0_), custom_call_target="tpu_custom_call" | custom-call | flops 1 | bytes 1 | tf_op jit(solution)/shard_map/side_terms/pallas_call | solution.py:271
  149.9 0.2 collective-permute-start
  150.2 8.1 %side_terms.3 = bf16[2048,1280]{1,0:T(8,128)(2,1)} custom-call(s32[1]{0:T(128)} %bitcast.side, bf16[4096,768]{1,0:T(8,128)(2,1)} %get-tuple-element.47.refs_0_, bf16[4096,768]{1,0:T(8,128)(2,1)} %get-tuple-element.48.refs_1_, bf16[768,768]{1,0:T(8,128)(2,1)S(1)} %attend_backward.2.refs_2_, bf16[768,512]{1,0:T(8,128)(2,1)S(1)} %get-tuple-element.79.refs_3_.refs_0_), custom_call_target="tpu_custom_call" | custom-call | flops 1 | bytes 1 | tf_op jit(solution)/shard_map/side_terms/pallas_call | solution.py:271
  158.3 0.8 collective-permute-done
  159.0 4.2 fusion.6
  163.2 1.4 collective-permute-start.1
  164.6 1.8 collective-permute-start.2
  166.3 7.0 %add_blocks.1 = bf16[4,512,1280]{2,1,0:T(8,128)(2,1)} custom-call(bf16[4,512,1280]{2,1,0:T(8,128)(2,1)} %bitcast.26, bf16[4,512,1280]{2,1,0:T(8,128)(2,1)} %bitcast.4.b), custom_call_target="tpu_custom_call" | custom-call | flops 1 | bytes 1 | tf_op jit(solution)/shard_map/add_blocks/pallas_call | solution.py:348
  173.3 48.6 %collective-permute-done.1 = bf16[512,1280]{1,0:T(8,128)(2,1)S(1)} collective-permute-done((bf16[512,1280]{1,0:T(8,128)(2,1)}, bf16[512,1280]{1,0:T(8,128)(2,1)S(1)}, u32[]{:S(2)}, u32[]{:S(2)}) %collective-permute-start.1) | collective-permute-done | bytes 1310752 | tf_op jit(solution)/shard_map/ppermute | solution.py:395
  221.9 1.1 copy-done.2
  223.0 0.0 collective-permute-done.2
  223.0 4.2 fusion.2
  227.1 5.4 %collective-permute-start.3 = (bf16[512,1280]{1,0:T(8,128)(2,1)}, bf16[512,1280]{1,0:T(8,128)(2,1)}, u32[]{:S(2)}, u32[]{:S(2)}) collective-permute-start(bf16[512,1280]{1,0:T(8,128)(2,1)} %get-tuple-element.63), channel_id=1, source_target_pairs={{0,8},{4,12},{8,16},{12,20},{1,9},{5,13},{9,17},{13,21},{2,10},{6,... | collective-permute-start | bytes 3932168 | tf_op jit(solution)/shard_map/ppermute | solution.py:395
  232.5 1.7 collective-permute-start.4
  234.3 4.9 %all-gather.5.cloned.1.call-done.b.refs_3_ = bf16[4096,1280]{1,0:T(8,128)(2,1)} async-done(((bf16[512,1280]{1,0:T(8,128)(2,1)}), bf16[4096,1280]{1,0:T(8,128)(2,1)}) %all-gather.5.cloned.1.call-update) | async-done | bytes 10485776 | tf_op jit(solution)/shard_map/all_gather | solution.py:441
  239.1 9.1 %product.6.qkv_ref = bf16[768,768]{1,0:T(8,128)(2,1)S(1)} custom-call(bf16[768,4096]{1,0:T(8,128)(2,1)} %get-tuple-element.64.a, bf16[4096,1280]{1,0:T(8,128)(2,1)} %all-gather.5.cloned.1.call-done.b.refs_3_), custom_call_target="tpu_custom_call" | custom-call | flops 1 | bytes 1 | tf_op jit(solution)/shard_map/product/pallas_call | solution.py:220
  248.2 0.0 copy-start
  248.2 5.2 %attend_forward.3 = (bf16[768,512]{1,0:T(8,128)(2,1)S(1)}, f32[4,768]{1,0:T(4,128)S(1)}) custom-call(bf16[768,768]{1,0:T(8,128)(2,1)S(1)} %product.6.qkv_ref), custom_call_target="tpu_custom_call" | custom-call | flops 1 | bytes 1 | tf_op jit(solution)/shard_map/attend_forward/pallas_call | solution.py:61
  253.4 0.0 slice-start
  253.4 0.0 slice-start.1
  253.4 7.2 %product.7.grad_ref = bf16[768,512]{1,0:T(8,128)(2,1)S(1)} custom-call(bf16[768,4096]{1,0:T(8,128)(2,1)} %a.1, bf16[4096,1280]{1,0:T(8,128)(2,1)} %all-gather.5.cloned.1.call-done.b.refs_3_), custom_call_target="tpu_custom_call" | custom-call | flops 1 | bytes 1 | tf_op jit(solution)/shard_map/product/pallas_call | solution.py:220
  260.7 0.0 copy-done
  260.7 2.9 collective-permute-done.3
  263.6 0.0 collective-permute-done.4
  263.6 0.0 slice-done
  263.6 0.0 slice-done.1
  263.6 3.9 fusion
  267.5 4.5 %collective-permute-start.5 = (bf16[512,1280]{1,0:T(8,128)(2,1)}, bf16[512,1280]{1,0:T(8,128)(2,1)S(1)}, u32[]{:S(2)}, u32[]{:S(2)}) collective-permute-start(bf16[512,1280]{1,0:T(8,128)(2,1)} %get-tuple-element.70), channel_id=1, source_target_pairs={{0,8},{4,12},{8,16},{12,20},{16,24},{20,28},{1,9},{5,13},{9,17},{1... | collective-permute-start | bytes 3932168 | tf_op jit(solution)/shard_map/ppermute | solution.py:395
  272.0 1.5 collective-permute-start.6
  273.5 7.3 %attend_backward.3.refs_2_ = bf16[768,768]{1,0:T(8,128)(2,1)S(1)} custom-call(bf16[768,768]{1,0:T(8,128)(2,1)} %copy-done, bf16[768,512]{1,0:T(8,128)(2,1)S(1)} %product.7.grad_ref, f32[4,768]{1,0:T(4,128)S(1)} %get-tuple-element.72.lse_ref), custom_call_target="tpu_custom_call" | custom-call | flops 1 | bytes 1 | tf_op jit(solution)/shard_map/attend_backward/pallas_call | solution.py:106
  280.9 13.0 %terms.1 = bf16[4096,1280]{1,0:T(8,128)(2,1)} custom-call(bf16[4096,768]{1,0:T(8,128)(2,1)} %get-tuple-element.47.refs_0_, bf16[4096,768]{1,0:T(8,128)(2,1)} %get-tuple-element.48.refs_1_, bf16[768,768]{1,0:T(8,128)(2,1)S(1)} %attend_backward.3.refs_2_, bf16[768,512]{1,0:T(8,128)(2,1)S(1)} %get-tuple-element.73.refs_3_.refs_1_), custom_call_target="tpu_custom_call" | custom-call | flops 1 | bytes 1 | tf_op jit(solution)/shard_map/terms/pallas_call | solution.py:249
  293.9 6.3 %collective-permute-done.5 = bf16[512,1280]{1,0:T(8,128)(2,1)S(1)} collective-permute-done((bf16[512,1280]{1,0:T(8,128)(2,1)}, bf16[512,1280]{1,0:T(8,128)(2,1)S(1)}, u32[]{:S(2)}, u32[]{:S(2)}) %collective-permute-start.5) | collective-permute-done | bytes 1310752 | tf_op jit(solution)/shard_map/ppermute | solution.py:395
  300.1 4.9 %collective-permute-done.6 = bf16[512,1280]{1,0:T(8,128)(2,1)} collective-permute-done((bf16[512,1280]{1,0:T(8,128)(2,1)}, bf16[512,1280]{1,0:T(8,128)(2,1)}, u32[]{:S(2)}, u32[]{:S(2)}) %collective-permute-start.6) | collective-permute-done | bytes 1310752 | tf_op jit(solution)/shard_map/ppermute | solution.py:396
  305.0 0.0 reduce-scatter.2.cloned.1.call-update
  305.1 3.6 fusion.4.piece
  308.7 4.1 unpack.2
  312.8 14.3 %project.1 = bf16[768,4096]{1,0:T(8,128)(2,1)} custom-call(bf16[768,512]{1,0:T(8,128)(2,1)S(1)} %get-tuple-element.79.refs_3_.refs_0_, bf16[768,512]{1,0:T(8,128)(2,1)S(1)} %get-tuple-element.73.refs_3_.refs_1_, bf16[4096,1280]{1,0:T(8,128)(2,1)} %all-gather.3.cloned.1.call-done.b.refs_2_, bf16[4096,1280]{1,0:T(8,128)(2,1)} %all-gather.5.cloned.1.call-done.b.refs_3_), custom_call_target="tpu_custom_call" | custom-call | flops 1 | bytes 1 | tf_op jit(solution)/shard_map/project/pallas_call | solution.py:301
  327.1 3.6 constant_dynamic-slice_fusion.2
  330.7 1.6 collective-permute-start.7
  332.3 1.4 collective-permute-start.8
  333.8 0.5 collective-permute-start.9
  334.3 33.8 %collective-permute-done.7 = bf16[768,1024]{1,0:T(8,128)(2,1)S(1)} collective-permute-done((bf16[768,1024]{1,0:T(8,128)(2,1)S(1)}, bf16[768,1024]{1,0:T(8,128)(2,1)S(1)}, u32[]{:S(2)}, u32[]{:S(2)}) %collective-permute-start.7) | collective-permute-done | bytes 1572896 | tf_op jit(solution)/shard_map/ppermute | solution.py:425
  368.1 32.6 %collective-permute-done.8 = bf16[768,1024]{1,0:T(8,128)(2,1)S(1)} collective-permute-done((bf16[768,1024]{1,0:T(8,128)(2,1)S(1)}, bf16[768,1024]{1,0:T(8,128)(2,1)S(1)}, u32[]{:S(2)}, u32[]{:S(2)}) %collective-permute-start.8) | collective-permute-done | bytes 1572896 | tf_op jit(solution)/shard_map/ppermute | solution.py:425
  400.7 0.0 collective-permute-done.9
  400.7 4.4 %add_convert_fusion = bf16[768,1024]{1,0:T(8,128)(2,1)} fusion(bf16[768,1024]{1,0:T(8,128)(2,1)S(1)} %collective-permute-done.9, bf16[768,1024]{1,0:T(8,128)(2,1)S(1)} %collective-permute-done.8, bf16[768,1024]{1,0:T(8,128)(2,1)S(1)} %collective-permute-done.7, bf16[768,1024]{1,0:T(8,128)(2,1)S(1)} %get-tuple-element.80, bf16[768,4096]{1,0:T(8,128)(2,1)} %x_ref.1, ...), kind=kLoop, calls=%fused_computation | loop fusion | flops 7864320 | bytes 9437188 | tf_op jit(solution)/shard_map/convert_element_type | solution.py:491
  405.2 8.7 %reduce-scatter.2.cloned.1.call-done.piece = bf16[512,1280]{1,0:T(8,128)(2,1)} async-done(((bf16[4096,1280]{1,0:T(8,128)(2,1)}), bf16[512,1280]{1,0:T(8,128)(2,1)}) %reduce-scatter.2.cloned.1.call-update) | async-done | bytes 1310736 | tf_op jit(solution)/shard_map/reduce_scatter | solution.py:481
  413.9 3.7 unpack.3
  (3 shorter events, 0.0 us)
Async XLA Ops:
  7.2 105.9 %all-gather.3.cloned.1.call-start = ((), (), s32[]{:S(2)}) async-start(), calls=%async_computation.1 | async-start | bytes 11796480 | tf_op jit(solution)/shard_map/all_gather | solution.py:441
  10.8 3.7 copy-start.3
  10.8 228.3 %all-gather.5.cloned.1.call-start = ((), (), s32[]{:S(2)}) async-start(), calls=%async_computation.2 | async-start | bytes 11796480 | tf_op jit(solution)/shard_map/all_gather | solution.py:441
  14.5 399.4 %reduce-scatter.2.cloned.1.call-start = ((), (), s32[]{:S(2)}) async-start(), calls=%async_computation.3 | async-start | bytes 11796480 | tf_op jit(solution)/shard_map/reduce_scatter | solution.py:481
  122.0 12.5 %copy-start.1 = (bf16[768,768]{1,0:T(8,128)(2,1)}, bf16[768,768]{1,0:T(8,128)(2,1)S(1)}, u32[]{:S(2)}) copy-start(bf16[768,768]{1,0:T(8,128)(2,1)S(1)} %product.4.qkv_ref) | copy-start | bytes 3538948
  149.9 9.1 %collective-permute-start = (bf16[2048,1280]{1,0:T(8,128)(2,1)}, bf16[2048,1280]{1,0:T(8,128)(2,1)}, u32[]{:S(2)}, u32[]{:S(2)}) collective-permute-start(bf16[2048,1280]{1,0:T(8,128)(2,1)} %side_terms.2), channel_id=1, source_target_pairs={{0,4},{4,0},{8,12},{12,8},{16,20},{20,16},{24,28},{28,24},{1,5},{5... | collective-permute-start | bytes 15728648 | tf_op jit(solution)/shard_map/ppermute | solution.py:339
  163.2 58.7 %collective-permute-start.1 = (bf16[512,1280]{1,0:T(8,128)(2,1)}, bf16[512,1280]{1,0:T(8,128)(2,1)S(1)}, u32[]{:S(2)}, u32[]{:S(2)}) collective-permute-start(bf16[512,1280]{1,0:T(8,128)(2,1)} %get-tuple-element.59), channel_id=1, source_target_pairs={{0,8},{4,12},{1,9},{5,13},{2,10},{6,14},{3,11},{7,15}} | collective-permute-start | bytes 3932168 | tf_op jit(solution)/shard_map/ppermute | solution.py:395
  164.6 58.4 %collective-permute-start.2 = (bf16[512,1280]{1,0:T(8,128)(2,1)S(1)}, bf16[512,1280]{1,0:T(8,128)(2,1)}, u32[]{:S(2)}, u32[]{:S(2)}) collective-permute-start(bf16[512,1280]{1,0:T(8,128)(2,1)S(1)} %get-tuple-element.62), channel_id=1, source_target_pairs={{24,16},{28,20},{25,17},{29,21},{26,18},{30,22},{27,19},{31,23}} | collective-permute-start | bytes 3932168 | tf_op jit(solution)/shard_map/ppermute | solution.py:396
  221.9 1.1 copy-start.2
  227.1 36.5 %collective-permute-start.3 = (bf16[512,1280]{1,0:T(8,128)(2,1)}, bf16[512,1280]{1,0:T(8,128)(2,1)}, u32[]{:S(2)}, u32[]{:S(2)}) collective-permute-start(bf16[512,1280]{1,0:T(8,128)(2,1)} %get-tuple-element.63), channel_id=1, source_target_pairs={{0,8},{4,12},{8,16},{12,20},{1,9},{5,13},{9,17},{13,21},{2,10},{6,... | collective-permute-start | bytes 3932168 | tf_op jit(solution)/shard_map/ppermute | solution.py:395
  232.5 31.1 %collective-permute-start.4 = (bf16[512,1280]{1,0:T(8,128)(2,1)S(1)}, bf16[512,1280]{1,0:T(8,128)(2,1)}, u32[]{:S(2)}, u32[]{:S(2)}) collective-permute-start(bf16[512,1280]{1,0:T(8,128)(2,1)S(1)} %get-tuple-element.69), channel_id=1, source_target_pairs={{16,8},{20,12},{24,16},{28,20},{17,9},{21,13},{25,17},{29,21},{18,... | collective-permute-start | bytes 3932168 | tf_op jit(solution)/shard_map/ppermute | solution.py:396
  248.2 12.5 %copy-start = (bf16[768,768]{1,0:T(8,128)(2,1)}, bf16[768,768]{1,0:T(8,128)(2,1)S(1)}, u32[]{:S(2)}) copy-start(bf16[768,768]{1,0:T(8,128)(2,1)S(1)} %product.6.qkv_ref) | copy-start | bytes 3538948
  253.4 10.2 %slice-start = ((s8[5242880]{0:T(1024)(128)(4,1)}), s8[4194304]{0:T(1024)(128)(4,1)S(1)}, s32[]{:S(2)}) async-start(s8[5242880]{0:T(1024)(128)(4,1)} %bitcast.27), calls=%async_computation.4 | async-start | bytes 8388608
  253.4 10.2 %slice-start.1 = ((s8[5242880]{0:T(1024)(128)(4,1)}), s8[1048576]{0:T(1024)(128)(4,1)S(1)}, s32[]{:S(2)}) async-start(s8[5242880]{0:T(1024)(128)(4,1)} %bitcast.27), calls=%async_computation.5 | async-start | bytes 2097152
  267.5 32.6 %collective-permute-start.5 = (bf16[512,1280]{1,0:T(8,128)(2,1)}, bf16[512,1280]{1,0:T(8,128)(2,1)S(1)}, u32[]{:S(2)}, u32[]{:S(2)}) collective-permute-start(bf16[512,1280]{1,0:T(8,128)(2,1)} %get-tuple-element.70), channel_id=1, source_target_pairs={{0,8},{4,12},{8,16},{12,20},{16,24},{20,28},{1,9},{5,13},{9,17},{1... | collective-permute-start | bytes 3932168 | tf_op jit(solution)/shard_map/ppermute | solution.py:395
  272.0 33.1 %collective-permute-start.6 = (bf16[512,1280]{1,0:T(8,128)(2,1)}, bf16[512,1280]{1,0:T(8,128)(2,1)}, u32[]{:S(2)}, u32[]{:S(2)}) collective-permute-start(bf16[512,1280]{1,0:T(8,128)(2,1)} %get-tuple-element.74), channel_id=1, source_target_pairs={{8,0},{12,4},{16,8},{20,12},{24,16},{28,20},{9,1},{13,5},{17,9},{2... | collective-permute-start | bytes 3932168 | tf_op jit(solution)/shard_map/ppermute | solution.py:396
  330.7 37.4 %collective-permute-start.7 = (bf16[768,1024]{1,0:T(8,128)(2,1)S(1)}, bf16[768,1024]{1,0:T(8,128)(2,1)S(1)}, u32[]{:S(2)}, u32[]{:S(2)}) collective-permute-start(bf16[768,1024]{1,0:T(8,128)(2,1)S(1)} %get-tuple-element.94), channel_id=1, source_target_pairs={{0,1},{1,0},{2,3},{3,2},{4,5},{5,4},{6,7},{7,6},{8,9},{9,8},{10,11... | collective-permute-start | bytes 4718600 | tf_op jit(solution)/shard_map/ppermute | solution.py:425
  332.3 68.4 %collective-permute-start.8 = (bf16[768,1024]{1,0:T(8,128)(2,1)S(1)}, bf16[768,1024]{1,0:T(8,128)(2,1)S(1)}, u32[]{:S(2)}, u32[]{:S(2)}) collective-permute-start(bf16[768,1024]{1,0:T(8,128)(2,1)S(1)} %get-tuple-element.93), channel_id=1, source_target_pairs={{0,2},{1,3},{2,0},{3,1},{4,6},{5,7},{6,4},{7,5},{8,10},{9,11},{10,... | collective-permute-start | bytes 4718600 | tf_op jit(solution)/shard_map/ppermute | solution.py:425
  333.8 67.0 %collective-permute-start.9 = (bf16[768,1024]{1,0:T(8,128)(2,1)S(1)}, bf16[768,1024]{1,0:T(8,128)(2,1)S(1)}, u32[]{:S(2)}, u32[]{:S(2)}) collective-permute-start(bf16[768,1024]{1,0:T(8,128)(2,1)S(1)} %get-tuple-element.92), channel_id=1, source_target_pairs={{0,3},{1,2},{2,1},{3,0},{4,7},{5,6},{6,5},{7,4},{8,11},{9,10},{10,... | collective-permute-start | bytes 4718600 | tf_op jit(solution)/shard_map/ppermute | solution.py:425
Sparse Core Ops, SparseCore 0:
  10.9 102.0 all-gather.2
  115.3 123.8 all-gather.4
  305.2 108.6 reduce-scatter.1
